TPU v7x, 32 devices: a whole 2x2x4 slice. The times are simulated.
32 devices in a mesh: row: 4 (over y, core), col: 8 (over z, x).
Axes of the slice: x: 2, y: 2, z: 4, core: 2. Of those that a mesh axis runs over, the one named last changes fastest.
Arguments:
- tokens: bfloat16 [256, 8192], P('col', 'row'), may hold values from -6 to 6
- out_grad: bfloat16 [256, 8192], P('col', 'row'), may hold values from -0.119628906 to 0.119628906
- w_gate: bfloat16 [8192, 14336], P('row', 'col'), may hold values from -0.09375 to 0.09375
- w_up: bfloat16 [8192, 14336], P('row', 'col'), may hold values from -0.09375 to 0.09375
- w_down: bfloat16 [8192, 14336], P('row', 'col'), may hold values from -0.0625 to 0.0625
- mask_gate: int32 [64, 112], P('row', 'col'), may hold values 0 or 1
- mask_up: int32 [64, 112], P('row', 'col'), may hold values 0 or 1
- mask_down: int32 [64, 112], P('row', 'col'), may hold values 0 or 1
Outputs:
- mixed: bfloat16 [256, 8192], P('col', 'row')
- grad_gate_w: float32 [8192, 14336], P('row', 'col')
- grad_up_w: float32 [8192, 14336], P('row', 'col')
- grad_down_w: float32 [8192, 14336], P('row', 'col')
All inputs are finite; a program needn't handle non-finite values. No bound on the sum of `mask_gate` or of `mask_up` or of `mask_down` on one device may be relied on, other than what follows from the above.
Results may differ from a plain program's by a relative error of at most 0.02.
Values may be sent and summed in bfloat16 or wider, within the bound.
No kernel may reach another device: no remote copies, remote signals or barrier semaphores. Data moves between devices by JAX's collectives and lax.ppermute only.
A program may use at most 192 MiB of HBM per device.

v0:
```python
import jax
import jax.numpy as jnp
from jax import lax
from jax.sharding import PartitionSpec as P


def expand(block_mask, weight):
    mask_rows, mask_cols = block_mask.shape
    block_rows = weight.shape[0] // mask_rows
    block_cols = weight.shape[1] // mask_cols
    factor = block_mask.astype(weight.dtype)[:, None, :, None]
    shaped = weight.reshape(mask_rows, block_rows, mask_cols, block_cols) * factor
    return shaped.reshape(weight.shape)


def per_device(tokens, out_grad, w_gate, w_up, w_down, mask_gate, mask_up, mask_down):
    gate_m = expand(mask_gate, w_gate)
    up_m = expand(mask_up, w_up)
    down_m = expand(mask_down, w_down)
    x_panel, dz_panel = (
        lax.all_gather(tokens, "col", axis=0, tiled=True),
        lax.all_gather(out_grad, "col", axis=0, tiled=True),
    )
    part_gate = jnp.dot(x_panel, gate_m, preferred_element_type=jnp.float32)
    part_up = jnp.dot(x_panel, up_m, preferred_element_type=jnp.float32)
    part_grad = jnp.dot(dz_panel, down_m, preferred_element_type=jnp.float32)
    share_rows = x_panel.shape[0] // lax.axis_size("row")
    offset = lax.axis_index("row") * share_rows
    gate_full, up_full = (
        lax.psum(part_gate.astype(jnp.bfloat16), "row").astype(jnp.float32),
        lax.psum(part_up.astype(jnp.bfloat16), "row").astype(jnp.float32),
    )
    hidden_all = (jax.nn.silu(gate_full) * up_full).astype(jnp.bfloat16)
    gate_share = lax.dynamic_slice_in_dim(gate_full, offset, share_rows, 0)
    up_share = lax.dynamic_slice_in_dim(up_full, offset, share_rows, 0)
    grad_hidden = lax.psum_scatter(
        part_grad.astype(jnp.bfloat16), "row", scatter_dimension=0, tiled=True
    ).astype(jnp.float32)
    part_mixed = jnp.dot(hidden_all, down_m.T, preferred_element_type=jnp.float32)
    mixed = lax.psum_scatter(
        part_mixed.astype(jnp.bfloat16), "col", scatter_dimension=0, tiled=True
    )
    sigmoid_gate = jax.nn.sigmoid(gate_share)
    grad_up = (grad_hidden * gate_share * sigmoid_gate).astype(jnp.bfloat16)
    grad_gate = (
        grad_hidden * up_share * sigmoid_gate * (1.0 + gate_share * (1.0 - sigmoid_gate))
    ).astype(jnp.bfloat16)
    gate_cot, up_cot = (
        lax.all_gather(grad_gate, "row", axis=0, tiled=True),
        lax.all_gather(grad_up, "row", axis=0, tiled=True),
    )
    grad_gate_w = expand(
        mask_gate, jnp.dot(x_panel.T, gate_cot, preferred_element_type=jnp.float32)
    )
    grad_up_w = expand(mask_up, jnp.dot(x_panel.T, up_cot, preferred_element_type=jnp.float32))
    grad_down_w = expand(
        mask_down, jnp.dot(dz_panel.T, hidden_all, preferred_element_type=jnp.float32)
    )
    return (mixed, grad_gate_w, grad_up_w, grad_down_w)


def solution(mesh):
    placed = (
        P("col", "row"),
        P("col", "row"),
        P("row", "col"),
        P("row", "col"),
        P("row", "col"),
        P("row", "col"),
        P("row", "col"),
        P("row", "col"),
    )
    return jax.shard_map(
        per_device,
        mesh=mesh,
        in_specs=placed,
        out_specs=(P("col", "row"), P("row", "col"), P("row", "col"), P("row", "col")),
        check_vma=False,
    )
```

profile of v0, /device:TPU:0, one launch (start us, length us, event | category | flops | bytes accessed | tf_op | source)
XLA Modules:
  0.0 261.3 jit_solution(1601314006395276468)
XLA Ops:
  7.2 0.7 all-gather.3.cloned.1.call-update
  7.9 0.0 all-gather.5.cloned.1.call-start
  7.9 0.7 all-gather.5.cloned.1.call-update
  8.6 0.0 all-reduce.3.cloned.1.call-start
  8.7 0.8 fusion.16
  9.5 0.1 copy.53
  9.6 0.1 copy.44
  9.6 0.8 fusion.15
  10.4 0.1 copy.54
  10.5 0.1 copy.47
  10.6 0.8 fusion.14
  11.4 0.1 copy.55
  11.5 0.1 copy.50
  11.6 10.5 %copy.51 = bf16[2048,1792]{0,1:T(8,128)(2,1)} copy(bf16[2048,1792]{1,0:T(8,128)(2,1)} %param.12) | data formatting | bytes 14680064 | tf_op args[4]
  22.0 10.4 %copy.45 = bf16[2048,1792]{0,1:T(8,128)(2,1)} copy(bf16[2048,1792]{1,0:T(8,128)(2,1)} %param.10) | data formatting | bytes 14680064 | tf_op args[2]
  32.4 10.4 %copy.48 = bf16[2048,1792]{0,1:T(8,128)(2,1)} copy(bf16[2048,1792]{1,0:T(8,128)(2,1)} %param.11) | data formatting | bytes 14680064 | tf_op args[3]
  42.9 10.1 %all-gather.3.cloned.1.call-done = bf16[256,2048]{1,0:T(8,128)(2,1)} async-done(((bf16[32,2048]{1,0:T(8,128)(2,1)}), bf16[256,2048]{1,0:T(8,128)(2,1)}) %all-gather.3.cloned.1.call-update) | async-done | bytes 1048592 | tf_op jit(solution)/shard_map/all_gather | solution.py:21
  53.0 1.0 mul.94
  54.0 0.2 copy-done.3
  54.2 7.5 %fusion.8 = bf16[256,1792]{1,0:T(8,128)(2,1)} fusion(bf16[256,2048]{1,0:T(8,128)(2,1)S(1)} %copy-done.3, bf16[2048,1792]{0,1:T(8,128)(2,1)} %copy.45, bf16[224,8,16,128]{3,2,1,0:T(8,128)(2,1)S(1)} %bitcast.76), kind=kOutput, calls=%fused_computation.16 | convolution fusion | flops 1883176960 | bytes 16646144 | tf_op jit(solution)/shard_map/dot_general | solution.py:24
  61.7 1.0 mul.98
  62.8 4.0 %fusion.7 = bf16[256,1792]{1,0:T(8,128)(2,1)} fusion(bf16[256,2048]{1,0:T(8,128)(2,1)S(1)} %copy-done.3, bf16[2048,1792]{0,1:T(8,128)(2,1)S(1)} %bitcast.73, bf16[224,8,16,128]{3,2,1,0:T(8,128)(2,1)S(1)} %bitcast.77), kind=kOutput, calls=%fused_computation.15 | convolution fusion | flops 1883176960 | bytes 16646144 | tf_op jit(solution)/shard_map/dot_general | solution.py:25
  66.8 0.2 reduce-scatter.7.cloned.1.call-start
  67.0 27.0 %all-gather.5.cloned.1.call-done = bf16[256,2048]{1,0:T(8,128)(2,1)} async-done(((bf16[32,2048]{1,0:T(8,128)(2,1)}), bf16[256,2048]{1,0:T(8,128)(2,1)}) %all-gather.5.cloned.1.call-update) | async-done | bytes 1048592 | tf_op jit(solution)/shard_map/all_gather | solution.py:22
  94.1 1.0 mul.102
  95.1 2.9 %copy-done = bf16[16,128,14,128]{1,0,3,2:T(8,128)(2,1)} copy-done((bf16[16,128,14,128]{1,0,3,2:T(8,128)(2,1)}, bf16[16,128,14,128]{1,0,3,2:T(8,128)(2,1)S(1)}, u32[]{:S(2)}) %copy-start) | copy-done | bytes 7340056
  98.0 5.6 %fusion.6 = bf16[256,1792]{0,1:T(8,128)(2,1)S(1)} fusion(bf16[256,2048]{1,0:T(8,128)(2,1)S(1)} %copy-done.4, bf16[2048,1792]{0,1:T(8,128)(2,1)} %copy.51, bf16[224,8,16,128]{3,2,1,0:T(8,128)(2,1)S(1)} %bitcast.74), kind=kOutput, calls=%fused_computation.14 | convolution fusion | flops 1883176960 | bytes 16646144 | tf_op jit(solution)/shard_map/dot_general | solution.py:26
  103.6 1.4 copy.61
  105.0 0.0 reduce-scatter.5.cloned.1.call-start
  105.1 38.1 %all-reduce.3.cloned.1.call-done = (bf16[256,1792]{1,0:T(8,128)(2,1)}, bf16[256,1792]{1,0:T(8,128)(2,1)}) async-done(((bf16[256,1792]{1,0:T(8,128)(2,1)}, bf16[256,1792]{1,0:T(8,128)(2,1)}), (bf16[256,1792]{1,0:T(8,128)(2,1)}, bf16[256,1792]{1,0:T(8,128)(2,1)})) %all-reduce.3.cloned.1.call-update) | async-done | bytes 1835024 | tf_op jit(solution)/shard_map/psum | solution.py:31
  143.2 2.6 %convert_element_type.64 = f32[256,1792]{1,0:T(8,128)} convert(bf16[256,1792]{1,0:T(8,128)(2,1)} %get-tuple-element.20) | non-fusion elementwise | flops 458752 | bytes 2752512 | tf_op jit(solution)/shard_map/convert_element_type | solution.py:31
  145.8 2.5 convert_element_type.60
  148.3 1.0 mul.118
  149.3 0.2 copy-done.1
  149.5 0.3 copy-done.2
  149.8 0.3 copy-done.5
  150.1 9.3 %bitcast_multiply_fusion = f32[2048,1792]{0,1:T(8,128)} fusion(f32[224,8,16,128]{3,2,1,0:T(8,128)S(1)} %bitcast.71, bf16[256,2048]{1,0:T(8,128)(2,1)S(1)} %copy-done.5, bf16[256,1792]{1,0:T(8,128)(2,1)S(1)} %copy-done.1, bf16[256,1792]{1,0:T(8,128)(2,1)S(1)} %copy-done.2), kind=kOutput, calls=%fused_computation | convolution fusion | flops 1886388224 | bytes 32243712 | tf_op jit(solution)/shard_map/dot_general | solution.py:57
  159.4 14.3 %copy.58 = f32[2048,1792]{1,0:T(8,128)} copy(f32[2048,1792]{0,1:T(8,128)} %bitcast_multiply_fusion) | data formatting | bytes 29360128
  173.7 8.7 %convolution_convert_fusion.1 = bf16[256,2048]{1,0:T(8,128)(2,1)} fusion(bf16[2048,1792]{0,1:T(8,128)(2,1)} %copy.51, bf16[224,8,16,128]{3,2,1,0:T(8,128)(2,1)} %bitcast.75, bf16[256,1792]{1,0:T(8,128)(2,1)S(1)} %copy-done.1, bf16[256,1792]{1,0:T(8,128)(2,1)S(1)} %copy-done.2), kind=kOutput, calls=%fused_computation.13 | convolution fusion | flops 1886912512 | bytes 17563648 | tf_op jit(solution)/shard_map/dot_general | solution.py:39
  182.5 1.5 fusion.13
  184.0 9.1 %all_gather.15 = bf16[256,1792]{1,0:T(8,128)(2,1)S(1)} all-gather(bf16[64,1792]{1,0:T(8,128)(2,1)S(1)} %get-tuple-element.22), channel_id=1, replica_groups=mesh['row'=4,'col'=8] {'row'}, dimensions={0}, use_global_device_ids=true | all-gather | bytes 1146880 | tf_op jit(solution)/shard_map/all_gather | solution.py:50
  193.1 1.0 mul.115
  194.1 10.9 %bitcast_multiply_fusion.1 = f32[2048,1792]{0,1:T(8,128)} fusion(f32[224,8,16,128]{3,2,1,0:T(8,128)S(1)} %bitcast.70, bf16[256,1792]{1,0:T(8,128)(2,1)S(1)} %all_gather.15, bf16[256,2048]{1,0:T(8,128)(2,1)S(1)} %copy-done.3), kind=kOutput, calls=%fused_computation.1 | convolution fusion | flops 1882718208 | bytes 31326208 | tf_op jit(solution)/shard_map/dot_general | solution.py:55
  204.9 14.3 %copy.57 = f32[2048,1792]{1,0:T(8,128)} copy(f32[2048,1792]{0,1:T(8,128)} %bitcast_multiply_fusion.1) | data formatting | bytes 29360128
  219.3 9.7 %all_gather.14 = bf16[256,1792]{1,0:T(8,128)(2,1)S(1)} all-gather(bf16[64,1792]{1,0:T(8,128)(2,1)S(1)} %get-tuple-element.23), channel_id=1, replica_groups=mesh['row'=4,'col'=8] {'row'}, dimensions={0}, use_global_device_ids=true | all-gather | bytes 1146880 | tf_op jit(solution)/shard_map/all_gather | solution.py:49
  228.9 1.0 mul.110
  229.9 10.6 %bitcast_multiply_fusion.2 = f32[2048,1792]{0,1:T(8,128)} fusion(f32[224,8,16,128]{3,2,1,0:T(8,128)S(1)} %bitcast.69, bf16[256,1792]{1,0:T(8,128)(2,1)S(1)} %all_gather.14, bf16[256,2048]{1,0:T(8,128)(2,1)S(1)} %copy-done.3), kind=kOutput, calls=%fused_computation.2 | convolution fusion | flops 1882718208 | bytes 31326208 | tf_op jit(solution)/shard_map/dot_general | solution.py:53
  240.5 14.3 %copy.56 = f32[2048,1792]{1,0:T(8,128)} copy(f32[2048,1792]{0,1:T(8,128)} %bitcast_multiply_fusion.2) | data formatting | bytes 29360128
  (18 shorter events, 0.1 us)
Async XLA Ops:
  7.2 45.8 %all-gather.3.cloned.1.call-start = ((), (), s32[]{:S(2)}) async-start(), calls=%async_computation.2 | async-start | bytes 1179648 | tf_op jit(solution)/shard_map/all_gather | solution.py:21
  7.9 86.2 %all-gather.5.cloned.1.call-start = ((), (), s32[]{:S(2)}) async-start(), calls=%async_computation.4 | async-start | bytes 1179648 | tf_op jit(solution)/shard_map/all_gather | solution.py:22
  8.6 134.5 %all-reduce.3.cloned.1.call-start = ((), (), s32[]{:S(2)}) async-start(), calls=%async_computation.6 | async-start | bytes 3670016 | tf_op jit(solution)/shard_map/psum | solution.py:31
  53.0 1.2 copy-start.3
  53.0 9.7 %slice-start = ((s8[7340032]{0:T(1024)(128)(4,1)}), s8[4194304]{0:T(1024)(128)(4,1)S(1)}, s32[]{:S(2)}) async-start(s8[7340032]{0:T(1024)(128)(4,1)} %bitcast.72), calls=%async_computation.7 | async-start | bytes 8388608
  54.2 8.5 %slice-start.1 = ((s8[7340032]{0:T(1024)(128)(4,1)}), s8[3145728]{0:T(1024)(128)(4,1)S(1)}, s32[]{:S(2)}) async-start(s8[7340032]{0:T(1024)(128)(4,1)} %bitcast.72), calls=%async_computation.8 | async-start | bytes 6291456
  66.8 115.7 %reduce-scatter.7.cloned.1.call-start = ((), (), s32[]{:S(2)}) async-start(), calls=%async_computation.5 | async-start | bytes 1146880 | tf_op jit(solution)/shard_map/reduce_scatter | solution.py:36
  94.1 4.0 %copy-start.4 = (bf16[256,2048]{1,0:T(8,128)(2,1)S(1)}, bf16[256,2048]{1,0:T(8,128)(2,1)}, u32[]{:S(2)}) copy-start(bf16[256,2048]{1,0:T(8,128)(2,1)} %all-gather.5.cloned.1.call-done) | copy-start | bytes 3145732
  95.1 2.9 %copy-start = (bf16[16,128,14,128]{1,0,3,2:T(8,128)(2,1)}, bf16[16,128,14,128]{1,0,3,2:T(8,128)(2,1)S(1)}, u32[]{:S(2)}) copy-start(bf16[16,128,14,128]{1,0,3,2:T(8,128)(2,1)S(1)} %mul.102) | copy-start | bytes 22020100
  105.0 149.7 %reduce-scatter.5.cloned.1.call-start = ((), (), s32[]{:S(2)}) async-start(), calls=%async_computation.3 | async-start | bytes 1179648 | tf_op jit(solution)/shard_map/reduce_scatter | solution.py:40
  148.3 1.2 copy-start.1
  148.3 1.5 copy-start.2
  148.3 1.8 copy-start.5
Sparse Core Ops, SparseCore 0:
  10.1 42.8 all-gather.2
  55.1 38.8 all-gather.4
  97.0 46.0 all-reduce.2
  145.6 24.1 reduce-scatter.6
  182.6 63.5 reduce-scatter.4
where the time goes:
time: 263 us; the launch traced here: 261 us
  local copies, waits for them, and re-layouts  86.1 us (33%)
  waiting for transfers between devices  76.6 us (29%)
  matrix products  56.6 us (22%)
  blocking collectives  18.7 us (7%)
  between operations  13.9 us (5%)
  other arithmetic  9.01 us (3%)
    unnamed x23, local copies, waits for them, and re-layouts  79.5 us
    psum x1, waiting for transfers between devices, per_device(): lax.psum(part_up.astype(jnp.bfloat16), 'row').astype(jnp.float32)  38.1 us
    all_gather x1, waiting for transfers between devices, per_device(): lax.all_gather(out_grad, 'col', axis=0, tiled=True)  27 us
    dot_general x1, matrix products, per_device(): jnp.dot(x_panel.T, up_cot, preferred_element_type=jnp.float32)  10.9 us
    dot_general x1, matrix products, per_device(): jnp.dot(x_panel.T, gate_cot, preferred_element_type=jnp.float32)  10.6 us
    all_gather x1, waiting for transfers between devices, per_device(): lax.all_gather(tokens, 'col', axis=0, tiled=True)  10.1 us
    all_gather x1, blocking collectives, per_device(): lax.all_gather(grad_gate, 'row', axis=0, tiled=True)  9.68 us
    dot_general x1, matrix products, per_device(): jnp.dot(dz_panel.T, hidden_all, preferred_element_type=jnp.float32)  9.34 us
  transfers between devices with their start and end apart: 5, of which 3 were waited for; matrix products, arithmetic and copies ran while one was open for 57% of the time, Pallas kernels for 0%

commit v1 on v0

v1 whole, which is shorter than its diff:
```python
import functools

import jax
import jax.numpy as jnp
from jax import lax
from jax.experimental import pallas as pl
from jax.experimental.pallas import tpu as pltpu
from jax.sharding import PartitionSpec as P

BF16 = jnp.bfloat16
F32 = jnp.float32


def tile_of(size, block, most):
    tile = block
    while tile * 2 <= most and size % (tile * 2) == 0:
        tile *= 2
    return tile


def masked_rows(weight, mask_ref, block):
    parts = []
    for index in range(mask_ref.shape[0]):
        row = mask_ref[index].astype(weight.dtype)
        parts.append(weight[index * block:(index + 1) * block, :] * row)
    return parts[0] if len(parts) == 1 else jnp.concatenate(parts, axis=0)


def panel_matmul(core, evens, odds, weights, masks, chunks):
    n_w = len(weights)
    depth, width = weights[0].shape
    half = sum(a.shape[0] for a in evens) // chunks
    blocks = masks[0].shape[0]
    block = depth // blocks
    tile = tile_of(width, 128, 256)
    n_e, n_o = len(evens), len(odds)
    n_k = lax.axis_size("col") // 2
    rows = half // n_k

    def kernel(core_ref, *refs):
        e_refs, o_refs = refs[:n_e], refs[n_e:n_e + n_o]
        w_refs = refs[n_e + n_o:n_e + n_o + n_w]
        m_refs = refs[n_e + n_o + n_w:n_e + n_o + 2 * n_w]
        panel_ref, mine_ref, theirs_ref = refs[n_e + n_o + 2 * n_w:]

        @pl.when(pl.program_id(0) == 0)
        def _():
            for group, place in ((e_refs, core_ref[0]), (o_refs, 1 - core_ref[0])):
                k = 0
                for ref in group:
                    for local in range(ref.shape[0] // (chunks * rows)):
                        for c in range(chunks):
                            start = pl.multiple_of(place * half + (c * 2 * half + k * rows), rows)
                            low = (local * chunks + c) * rows
                            panel_ref[pl.ds(start, rows), :] = ref[low:low + rows, :]
                        k += 1

        for index in range(n_w):
            w = masked_rows(w_refs[index][...], m_refs[index], block)
            out = jnp.dot(panel_ref[...], w, preferred_element_type=F32).astype(BF16)
            for c in range(chunks):
                low = c * 2 * half
                mine_ref[index * chunks + c] = out[low:low + half]
                theirs_ref[index * chunks + c] = out[low + half:low + 2 * half]

    whole = lambda a: pl.BlockSpec(a.shape, lambda n, s: (0,) * a.ndim)
    part = jax.ShapeDtypeStruct((n_w * chunks, half, width), BF16)
    part_spec = pl.BlockSpec((n_w * chunks, half, tile), lambda n, s: (0, 0, n))
    panel = jax.ShapeDtypeStruct((chunks * 2 * half, depth), BF16)
    return pl.pallas_call(
        kernel,
        grid_spec=pltpu.PrefetchScalarGridSpec(
            num_scalar_prefetch=1,
            grid=(width // tile,),
            in_specs=[whole(a) for a in (*evens, *odds)]
            + [pl.BlockSpec((depth, tile), lambda n, s: (0, n))] * n_w
            + [pl.BlockSpec((blocks, 1, tile), lambda n, s: (0, 0, n))] * n_w,
            out_specs=[whole(panel), part_spec, part_spec],
        ),
        out_shape=[panel, part, part],
        compiler_params=pltpu.CompilerParams(vmem_limit_bytes=32 * 2**20),
        cost_estimate=pl.CostEstimate(
            flops=2 * panel.shape[0] * depth * width * n_w,
            bytes_accessed=2 * depth * width * n_w,
            transcendentals=0,
        ),
    )(core, *evens, *odds, *weights, *masks)


def output_matmul(core, hid_mine, hid_theirs, weight, mask):
    depth, width = weight.shape
    half = hid_mine.shape[0]
    block = depth // mask.shape[0]
    tile = tile_of(depth, block, 256)

    def kernel(core_ref, mine_ref, theirs_ref, w_ref, m_ref, even_ref, odd_ref, hid):
        @pl.when(pl.program_id(0) == 0)
        def _():
            hid[pl.ds(pl.multiple_of(core_ref[0] * half, half), half), :] = mine_ref[...]
            hid[pl.ds(pl.multiple_of((1 - core_ref[0]) * half, half), half), :] = theirs_ref[...]

        w = masked_rows(w_ref[...], m_ref, block)
        out = lax.dot_general(
            hid[...], w, (((1,), (1,)), ((), ())), preferred_element_type=F32
        ).astype(BF16)
        even_ref[...] = out[:half]
        odd_ref[...] = out[half:]

    out = jax.ShapeDtypeStruct((half, depth), BF16)
    out_spec = pl.BlockSpec((half, tile), lambda n, s: (0, n))
    return pl.pallas_call(
        kernel,
        grid_spec=pltpu.PrefetchScalarGridSpec(
            num_scalar_prefetch=1,
            grid=(depth // tile,),
            in_specs=[
                pl.BlockSpec((half, width), lambda n, s: (0, 0)),
                pl.BlockSpec((half, width), lambda n, s: (0, 0)),
                pl.BlockSpec((tile, width), lambda n, s: (n, 0)),
                pl.BlockSpec((tile // block, 1, width), lambda n, s: (n, 0, 0)),
            ],
            out_specs=[out_spec, out_spec],
            scratch_shapes=[pltpu.VMEM((2 * half, width), BF16)],
        ),
        out_shape=[out, out],
        compiler_params=pltpu.CompilerParams(vmem_limit_bytes=32 * 2**20),
        cost_estimate=pl.CostEstimate(
            flops=4 * half * depth * width, bytes_accessed=2 * depth * width, transcendentals=0
        ),
    )(core, hid_mine, hid_theirs, weight, mask)


def weight_grads(panels, cots, masks):
    depth = panels[0].shape[1]
    width = cots[0][0].shape[1]
    tokens = sum(p.shape[0] for p in panels)
    block = depth // masks[0].shape[0]
    tile = tile_of(depth, block, 256)
    n_p, n_c, n_o = len(panels), len(cots[0]), len(cots)

    def kernel(*refs):
        p_refs = refs[:n_p]
        c_refs = refs[n_p:n_p + n_c * n_o]
        m_refs = refs[n_p + n_c * n_o:n_p + n_c * n_o + n_o]
        out_refs = refs[n_p + n_c * n_o + n_o:n_p + n_c * n_o + 2 * n_o]
        cot = refs[-1]

        @pl.when(pl.program_id(0) == 0)
        def _():
            for o in range(n_o):
                low = 0
                for ref in c_refs[o * n_c:(o + 1) * n_c]:
                    cot[o, low:low + ref.shape[0], :] = ref[...]
                    low += ref.shape[0]

        lhs = [ref[...] for ref in p_refs]
        lhs = lhs[0] if n_p == 1 else jnp.concatenate(lhs, axis=0)
        for o in range(n_o):
            out = lax.dot_general(
                lhs, cot[o], (((0,), (0,)), ((), ())), preferred_element_type=F32
            )
            for index in range(tile // block):
                out_refs[o][index * block:(index + 1) * block, :] = (
                    out[index * block:(index + 1) * block, :] * m_refs[o][index]
                )

    flat = [a for cot in cots for a in cot]
    out = jax.ShapeDtypeStruct((depth, width), F32)
    return pl.pallas_call(
        kernel,
        grid=(depth // tile,),
        in_specs=[pl.BlockSpec((p.shape[0], tile), lambda n: (0, n)) for p in panels]
        + [pl.BlockSpec(a.shape, lambda n: (0, 0)) for a in flat]
        + [pl.BlockSpec((tile // block, 1, width), lambda n: (n, 0, 0))] * n_o,
        out_specs=[pl.BlockSpec((tile, width), lambda n: (n, 0))] * n_o,
        out_shape=[out] * n_o,
        scratch_shapes=[pltpu.VMEM((n_o, tokens, width), BF16)],
        compiler_params=pltpu.CompilerParams(vmem_limit_bytes=40 * 2**20),
        cost_estimate=pl.CostEstimate(
            flops=2 * tokens * depth * width * n_o,
            bytes_accessed=4 * depth * width * n_o,
            transcendentals=0,
        ),
    )(*panels, *flat, *masks)


def swap(value, axis, bits):
    size = lax.axis_size(axis)
    return lax.ppermute(value, axis, [(i, i ^ bits) for i in range(size)])


def gather_panel(own):
    evens = [own] + [swap(own, "col", 2 * k) for k in range(1, lax.axis_size("col") // 2)]
    odds = [swap(block, "col", 1) for block in evens]
    return evens, odds


def row_sum(mine, theirs):
    pair = (mine.astype(F32) + swap(theirs, "row", 1).astype(F32)).astype(BF16)
    total = pair.astype(F32)
    for k in range(1, lax.axis_size("row") // 2):
        total = total + swap(pair, "row", 2 * k).astype(F32)
    return total


def output_sum(even, odd, rows):
    pair = (even.astype(F32) + swap(odd, "col", 1).astype(F32)).astype(BF16)
    total = pair[:rows].astype(F32)
    for k in range(1, lax.axis_size("col") // 2):
        total = total + swap(pair[k * rows:(k + 1) * rows], "col", 2 * k).astype(F32)
    return total.astype(BF16)


def spread(mask, block):
    return jnp.repeat(mask.astype(F32), block, axis=1)[:, None, :]


def after(value, *earlier):
    return lax.optimization_barrier((value, earlier))[0]


CHUNKS = 2


def per_device(tokens, out_grad, w_gate, w_up, w_down, mask_gate, mask_up, mask_down):
    block = w_gate.shape[1] // mask_gate.shape[1]
    m_gate, m_up, m_down = (spread(m, block) for m in (mask_gate, mask_up, mask_down))
    core = (lax.axis_index("row") % 2).astype(jnp.int32).reshape(1)
    rows = tokens.shape[0] // CHUNKS

    blocks = []
    previous = ()
    for c in range(CHUNKS):
        own = tokens[c * rows:(c + 1) * rows]
        if previous:
            own = after(own, *previous)
        evens, odds = gather_panel(own)
        previous = evens
        blocks.append((evens, odds))
    dz_evens, dz_odds = gather_panel(after(out_grad, *previous))

    panels, gates, ups, hids, sums = [], [], [], [], []
    for evens, odds in blocks:
        panel, mine, theirs = panel_matmul(core, evens, odds, [w_gate, w_up], [m_gate, m_up], 1)
        total = row_sum(mine, theirs)
        panels.append(panel)
        gates.append(total[0])
        ups.append(total[1])
    dz_panel, mine, theirs = panel_matmul(core, dz_evens, dz_odds, [w_down], [m_down], CHUNKS)
    grad_hidden = row_sum(mine, theirs)
    for gate, up in zip(gates, ups):
        hid = (jax.nn.silu(gate) * up).astype(BF16)
        other = swap(hid, "row", 1)
        even, odd = output_matmul(core, hid, other, w_down, m_down)
        sums.append(output_sum(even, odd, rows))
        hids += [hid, other]
    mixed = jnp.concatenate(sums, axis=0)
    (grad_down_w,) = weight_grads([dz_panel], [hids], [m_down])

    gate, up = jnp.stack(gates), jnp.stack(ups)
    s = jax.nn.sigmoid(gate)
    cot = jnp.stack(
        [
            (grad_hidden * up * s * (1.0 + gate * (1.0 - s))).astype(BF16),
            (grad_hidden * gate * s).astype(BF16),
        ]
    )
    other = swap(cot, "row", 1)
    cots = [[a[o, c] for c in range(CHUNKS) for a in (cot, other)] for o in range(2)]
    grad_gate_w, grad_up_w = weight_grads(panels, cots, [m_gate, m_up])
    return (mixed, grad_gate_w, grad_up_w, grad_down_w)


def solution(mesh):
    return jax.shard_map(
        per_device,
        mesh=mesh,
        in_specs=(P("col", "row"),) * 2 + (P("row", "col"),) * 6,
        out_specs=(P("col", "row"),) + (P("row", "col"),) * 3,
        check_vma=False,
    )
```

time: 263 us -> 150 us (0.57)
  local copies, waits for them, and re-layouts: 86.1 us -> 22.5 us
  matrix products: 56.6 us -> 0 us
  Pallas kernels: 0 us -> 41.6 us
  starting transfers between devices: 0.38 us -> 39.1 us
  waiting for transfers between devices: 76.6 us -> 40.8 us
  blocking collectives: 18.7 us -> 0 us
  between operations: 13.9 us -> 1.06 us
  other arithmetic: 9.01 us -> 4.68 us
    unnamed x23 -> x40, local copies, waits for them, and re-layouts: 79.5 us -> 19.1 us
    dot_general x7 -> x0, matrix products: 56.6 us -> none  [the longest x1 10.9 us: per_device(): jnp.dot(x_panel.T, up_cot, preferred_element_type=jnp.float32)]
    pallas_call x0 -> x7, Pallas kernels: none -> 41.6 us  [the longest x2 17.9 us: weight_grads(): pl.pallas_call(kernel, grid=(depth // tile,), in_specs=[pl.BlockSpec((p.s...]
    ppermute x0 -> x38, waiting for transfers between devices: none -> 40.8 us  [swap(): return lax.ppermute(value, axis, [(i, i ^ bits) for i in range(size)])]
    ppermute x0 -> x38, starting transfers between devices: none -> 39.1 us  [swap(): return lax.ppermute(value, axis, [(i, i ^ bits) for i in range(size)])]
    psum x1 -> x0, waiting for transfers between devices: 38.1 us -> none  [per_device(): lax.psum(part_up.astype(jnp.bfloat16), 'row').astype(jnp.float32)]
    all_gather x2 -> x0, waiting for transfers between devices: 37.1 us -> none  [the longest x1 27 us: per_device(): lax.all_gather(out_grad, 'col', axis=0, tiled=True)]
    all_gather x2 -> x0, blocking collectives: 18.7 us -> none  [the longest x1 9.68 us: per_device(): lax.all_gather(grad_gate, 'row', axis=0, tiled=True)]
  transfers between devices with their start and end apart: 5 -> 38, of which waited for: 3 -> 11; matrix products, arithmetic and copies ran while one was open for 57% -> 5% of each run, Pallas kernels for 0% -> 21%
where the time goes in v1:
time: 150 us
  Pallas kernels  41.6 us (28%)
  waiting for transfers between devices  40.8 us (27%)
  starting transfers between devices  39.1 us (26%)
  local copies, waits for them, and re-layouts  22.5 us (15%)
  other arithmetic  4.68 us (3%)
    ppermute x38, waiting for transfers between devices, swap(): return lax.ppermute(value, axis, [(i, i ^ bits) for i in range(size)])  40.8 us
    ppermute x38, starting transfers between devices, swap(): return lax.ppermute(value, axis, [(i, i ^ bits) for i in range(size)])  39.1 us
    unnamed x40, local copies, waits for them, and re-layouts  19.1 us
    pallas_call x2, Pallas kernels, weight_grads(): pl.pallas_call(kernel, grid=(depth // tile,), in_specs=[pl.BlockSpec((p.s...  17.9 us
    pallas_call x3, Pallas kernels, panel_matmul(): pl.pallas_call(kernel, grid_spec=pltpu.PrefetchScalarGridSpec(num_scalar_...  15.8 us
    pallas_call x2, Pallas kernels, output_matmul(): pl.pallas_call(kernel, grid_spec=pltpu.PrefetchScalarGridSpec(num_scalar_...  7.86 us
  transfers between devices with their start and end apart: 38, of which 11 were waited for; matrix products, arithmetic and copies ran while one was open for 5% of the time, Pallas kernels for 21%

profile of v1, /device:TPU:0, one launch (start us, length us, event | category | flops | bytes accessed | tf_op | source)
XLA Modules:
  0.0 149.7 jit_solution(1442651574674070884)
XLA Ops:
  0.6 0.9 fusion.17
  1.5 3.1 %collective-permute-start = (bf16[16,2048]{1,0:T(8,128)(2,1)S(1)}, bf16[16,2048]{1,0:T(8,128)(2,1)S(1)}, u32[]{:S(2)}, u32[]{:S(2)}) collective-permute-start(bf16[16,2048]{1,0:T(8,128)(2,1)S(1)} %get-tuple-element.58.refs_0_), channel_id=1, source_target_pairs={{0,2},{1,3},{2,0},{3,1},{4,6},{5,7},{6,4},{7,5},{8,10},{9,11},{10,... | collective-permute-start | bytes 196616 | tf_op jit(solution)/shard_map/ppermute | solution.py:189
  4.6 2.6 %collective-permute-start.1 = (bf16[16,2048]{1,0:T(8,128)(2,1)S(1)}, bf16[16,2048]{1,0:T(8,128)(2,1)S(1)}, u32[]{:S(2)}, u32[]{:S(2)}) collective-permute-start(bf16[16,2048]{1,0:T(8,128)(2,1)S(1)} %get-tuple-element.58.refs_0_), channel_id=1, source_target_pairs={{0,4},{1,5},{2,6},{3,7},{4,0},{5,1},{6,2},{7,3},{8,12},{9,13},{10,... | collective-permute-start | bytes 196616 | tf_op jit(solution)/shard_map/ppermute | solution.py:189
  7.2 4.7 %collective-permute-done.1.refs_2_ = bf16[16,2048]{1,0:T(8,128)(2,1)S(1)} collective-permute-done((bf16[16,2048]{1,0:T(8,128)(2,1)S(1)}, bf16[16,2048]{1,0:T(8,128)(2,1)S(1)}, u32[]{:S(2)}, u32[]{:S(2)}) %collective-permute-start.1) | collective-permute-done | bytes 65568 | tf_op jit(solution)/shard_map/ppermute | solution.py:189
  11.9 1.4 collective-permute-done.2.refs_3_
  13.3 2.3 %collective-permute-start.15 = (bf16[16,2048]{1,0:T(8,128)(2,1)S(1)}, bf16[16,2048]{1,0:T(8,128)(2,1)}, u32[]{:S(2)}, u32[]{:S(2)}) collective-permute-start(bf16[16,2048]{1,0:T(8,128)(2,1)S(1)} %get-tuple-element.25.refs_0_), channel_id=1, source_target_pairs={{0,4},{1,5},{2,6},{3,7},{4,0},{5,1},{6,2},{7,3},{8,12},{9,13},{10,... | collective-permute-start | bytes 196616 | tf_op jit(solution)/shard_map/ppermute | solution.py:189
  15.6 2.0 %collective-permute-start.16 = (bf16[16,2048]{1,0:T(8,128)(2,1)S(1)}, bf16[16,2048]{1,0:T(8,128)(2,1)}, u32[]{:S(2)}, u32[]{:S(2)}) collective-permute-start(bf16[16,2048]{1,0:T(8,128)(2,1)S(1)} %get-tuple-element.25.refs_0_), channel_id=1, source_target_pairs={{0,6},{1,7},{2,4},{3,5},{4,2},{5,3},{6,0},{7,1},{8,14},{9,15},{10,... | collective-permute-start | bytes 196616 | tf_op jit(solution)/shard_map/ppermute | solution.py:189
  17.7 1.5 collective-permute-start.3
  19.7 1.5 collective-permute-start.4
  21.8 1.5 collective-permute-start.6
  24.2 0.7 convert_element_type.115
  25.9 2.6 %collective-permute-start.29 = (bf16[32,2048]{1,0:T(8,128)(2,1)}, bf16[32,2048]{1,0:T(8,128)(2,1)}, u32[]{:S(2)}, u32[]{:S(2)}) collective-permute-start(bf16[32,2048]{1,0:T(8,128)(2,1)} %refs_0_), channel_id=1, source_target_pairs={{0,4},{1,5},{2,6},{3,7},{4,0},{5,1},{6,2},{7,3},{8,12},{9,13},{10,... | collective-permute-start | bytes 393224 | tf_op jit(solution)/shard_map/ppermute | solution.py:189
  28.5 1.8 %collective-permute-start.30 = (bf16[32,2048]{1,0:T(8,128)(2,1)}, bf16[32,2048]{1,0:T(8,128)(2,1)}, u32[]{:S(2)}, u32[]{:S(2)}) collective-permute-start(bf16[32,2048]{1,0:T(8,128)(2,1)} %refs_0_), channel_id=1, source_target_pairs={{0,6},{1,7},{2,4},{3,5},{4,2},{5,3},{6,0},{7,1},{8,14},{9,15},{10,... | collective-permute-start | bytes 393224 | tf_op jit(solution)/shard_map/ppermute | solution.py:189
  30.8 1.5 collective-permute-start.19
  32.3 3.1 %copy-done = bf16[2048,1792]{1,0:T(8,128)(2,1)S(1)} copy-done((bf16[2048,1792]{1,0:T(8,128)(2,1)S(1)}, bf16[2048,1792]{1,0:T(8,128)(2,1)}, u32[]{:S(2)}) %copy-start) | copy-done | bytes 7340056
  35.4 3.1 %copy-done.2 = bf16[2048,1792]{1,0:T(8,128)(2,1)S(1)} copy-done((bf16[2048,1792]{1,0:T(8,128)(2,1)S(1)}, bf16[2048,1792]{1,0:T(8,128)(2,1)}, u32[]{:S(2)}) %copy-start.2) | copy-done | bytes 7340056
  38.4 5.3 %shard_map.111 = (bf16[128,2048]{1,0:T(8,128)(2,1)S(1)}, bf16[2,64,1792]{2,1,0:T(8,128)(2,1)S(1)}, bf16[2,64,1792]{2,1,0:T(8,128)(2,1)}) custom-call(s32[1]{0:T(128)} %bitcast.core_ref, bf16[16,2048]{1,0:T(8,128)(2,1)S(1)} %get-tuple-element.58.refs_0_, bf16[16,2048]{1,0:T(8,128)(2,1)S(1)} %collective-permute-done.refs_1_, ...), custom_call_target="tpu_custom_call" | custom-call | flops 1879048192 | bytes 14680064 | tf_op jit(solution)/shard_map/pallas_call | solution.py:70
  43.7 0.8 copy-done.4
  44.5 0.8 copy-done.15
  47.1 0.8 broadcast_in_dim.11
  47.9 1.0 broadcast_in_dim_reshape.14.m_ref.refs_9_.refs_5_
  48.9 2.5 %collective-permute-done.20.refs_7_ = bf16[16,2048]{1,0:T(8,128)(2,1)} collective-permute-done((bf16[16,2048]{1,0:T(8,128)(2,1)}, bf16[16,2048]{1,0:T(8,128)(2,1)}, u32[]{:S(2)}, u32[]{:S(2)}) %collective-permute-start.20) | collective-permute-done | bytes 65568 | tf_op jit(solution)/shard_map/ppermute | solution.py:189
  51.9 1.5 collective-permute-start.32
  54.0 1.5 collective-permute-start.34
  55.4 3.1 %copy-done.1 = bf16[2048,1792]{1,0:T(8,128)(2,1)S(1)} copy-done((bf16[2048,1792]{1,0:T(8,128)(2,1)S(1)}, bf16[2048,1792]{1,0:T(8,128)(2,1)}, u32[]{:S(2)}) %copy-start.1) | copy-done | bytes 7340056
  58.5 3.1 %copy-done.3 = bf16[2048,1792]{1,0:T(8,128)(2,1)S(1)} copy-done((bf16[2048,1792]{1,0:T(8,128)(2,1)S(1)}, bf16[2048,1792]{1,0:T(8,128)(2,1)}, u32[]{:S(2)}) %copy-start.3) | copy-done | bytes 7340056
  61.6 0.8 copy-done.8
  62.4 0.8 copy-done.10
  63.3 0.8 copy-done.12
  64.1 0.8 copy-done.14
  65.0 5.4 %shard_map.113 = (bf16[128,2048]{1,0:T(8,128)(2,1)S(1)}, bf16[2,64,1792]{2,1,0:T(8,128)(2,1)S(1)}, bf16[2,64,1792]{2,1,0:T(8,128)(2,1)S(1)}) custom-call(s32[1]{0:T(128)} %bitcast.core_ref, bf16[16,2048]{1,0:T(8,128)(2,1)S(1)} %get-tuple-element.25.refs_0_, bf16[16,2048]{1,0:T(8,128)(2,1)S(1)} %copy-done.8, ...), custom_call_target="tpu_custom_call" | custom-call | flops 1879048192 | bytes 14680064 | tf_op jit(solution)/shard_map/pallas_call | solution.py:70
  70.6 5.0 %shard_map.115 = (bf16[256,2048]{1,0:T(8,128)(2,1)S(1)}, bf16[2,64,1792]{2,1,0:T(8,128)(2,1)S(1)}, bf16[2,64,1792]{2,1,0:T(8,128)(2,1)S(1)}) custom-call(s32[1]{0:T(128)} %bitcast.core_ref, bf16[32,2048]{1,0:T(8,128)(2,1)S(1)} %copy-done.6, bf16[32,2048]{1,0:T(8,128)(2,1)} %collective-permute-done.28.refs_1_, ...), custom_call_target="tpu_custom_call" | custom-call | flops 1879048192 | bytes 7340032 | tf_op jit(solution)/shard_map/pallas_call | solution.py:70
  76.1 1.1 add_convert_fusion.2
  77.3 1.6 %collective-permute-start.8 = (bf16[2,64,1792]{2,1,0:T(8,128)(2,1)S(1)}, bf16[2,64,1792]{2,1,0:T(8,128)(2,1)S(1)}, u32[]{:S(2)}, u32[]{:S(2)}) collective-permute-start(bf16[2,64,1792]{2,1,0:T(8,128)(2,1)S(1)} %add_convert_fusion.2), channel_id=1, source_target_pairs={{0,16},{8,24},{16,0},{24,8},{1,17},{9,25},{17,1},{25,9},{2,18},{10... | collective-permute-start | bytes 1376264 | tf_op jit(solution)/shard_map/ppermute | solution.py:189
  79.7 1.6 %collective-permute-start.36 = (bf16[2,64,1792]{2,1,0:T(8,128)(2,1)S(1)}, bf16[2,64,1792]{2,1,0:T(8,128)(2,1)S(1)}, u32[]{:S(2)}, u32[]{:S(2)}) collective-permute-start(bf16[2,64,1792]{2,1,0:T(8,128)(2,1)S(1)} %add_convert_fusion), channel_id=1, source_target_pairs={{0,16},{8,24},{16,0},{24,8},{1,17},{9,25},{17,1},{25,9},{2,18},{10... | collective-permute-start | bytes 1376264 | tf_op jit(solution)/shard_map/ppermute | solution.py:189
  81.3 9.5 %collective-permute-done.8 = bf16[2,64,1792]{2,1,0:T(8,128)(2,1)S(1)} collective-permute-done((bf16[2,64,1792]{2,1,0:T(8,128)(2,1)S(1)}, bf16[2,64,1792]{2,1,0:T(8,128)(2,1)S(1)}, u32[]{:S(2)}, u32[]{:S(2)}) %collective-permute-start.8) | collective-permute-done | bytes 458784 | tf_op jit(solution)/shard_map/ppermute | solution.py:189
  91.1 9.4 %collective-permute-done.22 = bf16[2,64,1792]{2,1,0:T(8,128)(2,1)S(1)} collective-permute-done((bf16[2,64,1792]{2,1,0:T(8,128)(2,1)S(1)}, bf16[2,64,1792]{2,1,0:T(8,128)(2,1)S(1)}, u32[]{:S(2)}, u32[]{:S(2)}) %collective-permute-start.22) | collective-permute-done | bytes 458784 | tf_op jit(solution)/shard_map/ppermute | solution.py:189
  101.0 3.9 %shard_map.112 = (bf16[64,2048]{1,0:T(8,128)(2,1)S(1)}, bf16[64,2048]{1,0:T(8,128)(2,1)S(1)}) custom-call(s32[1]{0:T(128)} %bitcast.core_ref, bf16[64,1792]{1,0:T(8,128)(2,1)S(1)} %fusion.7.mine_ref.refs_1_, bf16[64,1792]{1,0:T(8,128)(2,1)S(1)} %collective-permute-done.9.theirs_ref.refs_2_, bf16[2048,1792]{1,0:T(8,128)(2,1)S(1)} %bitcast.56, ...), custom_call_target="tpu_custom_call" | custom-call | flops 939524096 | bytes 7340032 | tf_op jit(solution)/shard_map/pallas_call | solution.py:111
  105.5 3.9 %collective-permute-done.36 = bf16[2,64,1792]{2,1,0:T(8,128)(2,1)S(1)} collective-permute-done((bf16[2,64,1792]{2,1,0:T(8,128)(2,1)S(1)}, bf16[2,64,1792]{2,1,0:T(8,128)(2,1)S(1)}, u32[]{:S(2)}, u32[]{:S(2)}) %collective-permute-start.36) | collective-permute-done | bytes 458784 | tf_op jit(solution)/shard_map/ppermute | solution.py:189
  110.3 3.9 %shard_map.114 = (bf16[64,2048]{1,0:T(8,128)(2,1)S(1)}, bf16[64,2048]{1,0:T(8,128)(2,1)S(1)}) custom-call(s32[1]{0:T(128)} %bitcast.core_ref, bf16[64,1792]{1,0:T(8,128)(2,1)S(1)} %fusion.3.mine_ref.refs_3_, bf16[64,1792]{1,0:T(8,128)(2,1)S(1)} %collective-permute-done.23.theirs_ref.refs_4_, bf16[2048,1792]{1,0:T(8,128)(2,1)S(1)} %bitcast.56, ...), custom_call_target="tpu_custom_call" | custom-call | flops 939524096 | bytes 7340032 | tf_op jit(solution)/shard_map/pallas_call | solution.py:111
  114.8 7.5 %shard_map.117 = f32[2048,1792]{1,0:T(8,128)} custom-call(bf16[256,2048]{1,0:T(8,128)(2,1)S(1)} %get-tuple-element.37.refs_0_, bf16[64,1792]{1,0:T(8,128)(2,1)S(1)} %fusion.7.mine_ref.refs_1_, bf16[64,1792]{1,0:T(8,128)(2,1)S(1)} %collective-permute-done.9.theirs_ref.refs_2_, bf16[64,1792]{1,0:T(8,128)(2,1)S(1)} %fusion.3.mine_ref.refs_3_, ...), custom_call_target="tpu_custom_call" | custom-call | flops 1879048192 | bytes 14680064 | tf_op jit(solution)/shard_map/pallas_call | solution.py:169
  122.4 2.1 %collective-permute-start.13 = (bf16[16,2048]{1,0:T(8,128)(2,1)S(1)}, bf16[16,2048]{1,0:T(8,128)(2,1)S(1)}, u32[]{:S(2)}, u32[]{:S(2)}) collective-permute-start(bf16[16,2048]{1,0:T(8,128)(2,1)S(1)} %get-tuple-element.53), channel_id=1, source_target_pairs={{0,6},{1,7},{2,4},{3,5},{4,2},{5,3},{6,0},{7,1},{8,14},{9,15},{10,... | collective-permute-start | bytes 196616 | tf_op jit(solution)/shard_map/ppermute | solution.py:189
  124.5 2.3 %collective-permute-start.11 = (bf16[16,2048]{1,0:T(8,128)(2,1)S(1)}, bf16[16,2048]{1,0:T(8,128)(2,1)S(1)}, u32[]{:S(2)}, u32[]{:S(2)}) collective-permute-start(bf16[16,2048]{1,0:T(8,128)(2,1)S(1)} %get-tuple-element.52), channel_id=1, source_target_pairs={{0,2},{1,3},{2,0},{3,1},{4,6},{5,7},{6,4},{7,5},{8,10},{9,11},{10,... | collective-permute-start | bytes 196616 | tf_op jit(solution)/shard_map/ppermute | solution.py:189
  127.0 2.1 %collective-permute-start.27 = (bf16[16,2048]{1,0:T(8,128)(2,1)S(1)}, bf16[16,2048]{1,0:T(8,128)(2,1)S(1)}, u32[]{:S(2)}, u32[]{:S(2)}) collective-permute-start(bf16[16,2048]{1,0:T(8,128)(2,1)S(1)} %get-tuple-element.56), channel_id=1, source_target_pairs={{0,6},{1,7},{2,4},{3,5},{4,2},{5,3},{6,0},{7,1},{8,14},{9,15},{10,... | collective-permute-start | bytes 196616 | tf_op jit(solution)/shard_map/ppermute | solution.py:189
  129.2 4.9 %collective-permute-done.12 = bf16[16,2048]{1,0:T(8,128)(2,1)S(1)} collective-permute-done((bf16[16,2048]{1,0:T(8,128)(2,1)S(1)}, bf16[16,2048]{1,0:T(8,128)(2,1)S(1)}, u32[]{:S(2)}, u32[]{:S(2)}) %collective-permute-start.12) | collective-permute-done | bytes 65568 | tf_op jit(solution)/shard_map/ppermute | solution.py:189
  134.2 2.7 %collective-permute-done.26 = bf16[16,2048]{1,0:T(8,128)(2,1)S(1)} collective-permute-done((bf16[16,2048]{1,0:T(8,128)(2,1)S(1)}, bf16[16,2048]{1,0:T(8,128)(2,1)S(1)}, u32[]{:S(2)}, u32[]{:S(2)}) %collective-permute-start.26) | collective-permute-done | bytes 65568 | tf_op jit(solution)/shard_map/ppermute | solution.py:189
  136.9 1.6 %collective-permute-done.25 = bf16[16,2048]{1,0:T(8,128)(2,1)S(1)} collective-permute-done((bf16[16,2048]{1,0:T(8,128)(2,1)S(1)}, bf16[16,2048]{1,0:T(8,128)(2,1)S(1)}, u32[]{:S(2)}, u32[]{:S(2)}) %collective-permute-start.25) | collective-permute-done | bytes 65568 | tf_op jit(solution)/shard_map/ppermute | solution.py:189
  139.2 10.5 %shard_map.116 = (f32[2048,1792]{1,0:T(8,128)}, f32[2048,1792]{1,0:T(8,128)}) custom-call(bf16[128,2048]{1,0:T(8,128)(2,1)S(1)} %copy-done.16, bf16[128,2048]{1,0:T(8,128)(2,1)S(1)} %get-tuple-element.31.refs_1_, bf16[64,1792]{1,0:T(8,128)(2,1)S(1)} %get-tuple-element.60.refs_2_, bf16[64,1792]{1,0:T(8,128)(2,1)S(1)} %get-tuple-element.43.refs_3_, ...), custom_call_target="tpu_custom_call" | custom-call | flops 3758096384 | bytes 29360128 | tf_op jit(solution)/shard_map/pallas_call | solution.py:169
  (106 shorter events, 11.8 us)
Async XLA Ops:
  0.6 46.5 %copy-start.17 = (s32[16,14]{1,0:T(8,128)S(1)}, s32[16,14]{1,0:T(8,128)}, u32[]{:S(2)}) copy-start(s32[16,14]{1,0:T(8,128)} %param.15) | copy-start | bytes 2692
  1.5 5.7 %collective-permute-start = (bf16[16,2048]{1,0:T(8,128)(2,1)S(1)}, bf16[16,2048]{1,0:T(8,128)(2,1)S(1)}, u32[]{:S(2)}, u32[]{:S(2)}) collective-permute-start(bf16[16,2048]{1,0:T(8,128)(2,1)S(1)} %get-tuple-element.58.refs_0_), channel_id=1, source_target_pairs={{0,2},{1,3},{2,0},{3,1},{4,6},{5,7},{6,4},{7,5},{8,10},{9,11},{10,... | collective-permute-start | bytes 196616 | tf_op jit(solution)/shard_map/ppermute | solution.py:189
  4.6 7.3 %collective-permute-start.1 = (bf16[16,2048]{1,0:T(8,128)(2,1)S(1)}, bf16[16,2048]{1,0:T(8,128)(2,1)S(1)}, u32[]{:S(2)}, u32[]{:S(2)}) collective-permute-start(bf16[16,2048]{1,0:T(8,128)(2,1)S(1)} %get-tuple-element.58.refs_0_), channel_id=1, source_target_pairs={{0,4},{1,5},{2,6},{3,7},{4,0},{5,1},{6,2},{7,3},{8,12},{9,13},{10,... | collective-permute-start | bytes 196616 | tf_op jit(solution)/shard_map/ppermute | solution.py:189
  7.2 6.1 %collective-permute-start.2 = (bf16[16,2048]{1,0:T(8,128)(2,1)S(1)}, bf16[16,2048]{1,0:T(8,128)(2,1)S(1)}, u32[]{:S(2)}, u32[]{:S(2)}) collective-permute-start(bf16[16,2048]{1,0:T(8,128)(2,1)S(1)} %get-tuple-element.58.refs_0_), channel_id=1, source_target_pairs={{0,6},{1,7},{2,4},{3,5},{4,2},{5,3},{6,0},{7,1},{8,14},{9,15},{10,... | collective-permute-start | bytes 196616 | tf_op jit(solution)/shard_map/ppermute | solution.py:189
  13.3 6.4 %collective-permute-start.14 = (bf16[16,2048]{1,0:T(8,128)(2,1)S(1)}, bf16[16,2048]{1,0:T(8,128)(2,1)S(1)}, u32[]{:S(2)}, u32[]{:S(2)}) collective-permute-start(bf16[16,2048]{1,0:T(8,128)(2,1)S(1)} %get-tuple-element.25.refs_0_), channel_id=1, source_target_pairs={{0,2},{1,3},{2,0},{3,1},{4,6},{5,7},{6,4},{7,5},{8,10},{9,11},{10,... | collective-permute-start | bytes 196616 | tf_op jit(solution)/shard_map/ppermute | solution.py:189
  13.3 7.9 %collective-permute-start.15 = (bf16[16,2048]{1,0:T(8,128)(2,1)S(1)}, bf16[16,2048]{1,0:T(8,128)(2,1)}, u32[]{:S(2)}, u32[]{:S(2)}) collective-permute-start(bf16[16,2048]{1,0:T(8,128)(2,1)S(1)} %get-tuple-element.25.refs_0_), channel_id=1, source_target_pairs={{0,4},{1,5},{2,6},{3,7},{4,0},{5,1},{6,2},{7,3},{8,12},{9,13},{10,... | collective-permute-start | bytes 196616 | tf_op jit(solution)/shard_map/ppermute | solution.py:189
  15.6 6.2 %collective-permute-start.16 = (bf16[16,2048]{1,0:T(8,128)(2,1)S(1)}, bf16[16,2048]{1,0:T(8,128)(2,1)}, u32[]{:S(2)}, u32[]{:S(2)}) collective-permute-start(bf16[16,2048]{1,0:T(8,128)(2,1)S(1)} %get-tuple-element.25.refs_0_), channel_id=1, source_target_pairs={{0,6},{1,7},{2,4},{3,5},{4,2},{5,3},{6,0},{7,1},{8,14},{9,15},{10,... | collective-permute-start | bytes 196616 | tf_op jit(solution)/shard_map/ppermute | solution.py:189
  17.7 7.5 %collective-permute-start.3 = (bf16[16,2048]{1,0:T(8,128)(2,1)S(1)}, bf16[16,2048]{1,0:T(8,128)(2,1)S(1)}, u32[]{:S(2)}, u32[]{:S(2)}) collective-permute-start(bf16[16,2048]{1,0:T(8,128)(2,1)S(1)} %get-tuple-element.58.refs_0_), channel_id=1, source_target_pairs={{0,1},{1,0},{2,3},{3,2},{4,5},{5,4},{6,7},{7,6},{8,9},{9,8},{10,11... | collective-permute-start | bytes 196616 | tf_op jit(solution)/shard_map/ppermute | solution.py:189
  19.2 6.1 %collective-permute-start.17 = (bf16[16,2048]{1,0:T(8,128)(2,1)S(1)}, bf16[16,2048]{1,0:T(8,128)(2,1)S(1)}, u32[]{:S(2)}, u32[]{:S(2)}) collective-permute-start(bf16[16,2048]{1,0:T(8,128)(2,1)S(1)} %get-tuple-element.25.refs_0_), channel_id=1, source_target_pairs={{0,1},{1,0},{2,3},{3,2},{4,5},{5,4},{6,7},{7,6},{8,9},{9,8},{10,11... | collective-permute-start | bytes 196616 | tf_op jit(solution)/shard_map/ppermute | solution.py:189
  19.7 27.4 %copy-start.7 = (bf16[16,2048]{1,0:T(8,128)(2,1)}, bf16[16,2048]{1,0:T(8,128)(2,1)S(1)}, u32[]{:S(2)}) copy-start(bf16[16,2048]{1,0:T(8,128)(2,1)S(1)} %collective-permute-done.14.refs_1_) | copy-start | bytes 196612
  19.7 8.7 %collective-permute-start.4 = (bf16[16,2048]{1,0:T(8,128)(2,1)S(1)}, bf16[16,2048]{1,0:T(8,128)(2,1)S(1)}, u32[]{:S(2)}, u32[]{:S(2)}) collective-permute-start(bf16[16,2048]{1,0:T(8,128)(2,1)S(1)} %collective-permute-done.refs_1_), channel_id=1, source_target_pairs={{0,1},{1,0},{2,3},{3,2},{4,5},{5,4},{6,7},{7,6},{8,9},{9,8},{10,11... | collective-permute-start | bytes 196616 | tf_op jit(solution)/shard_map/ppermute | solution.py:189
  21.2 9.0 %collective-permute-start.5 = (bf16[16,2048]{1,0:T(8,128)(2,1)S(1)}, bf16[16,2048]{1,0:T(8,128)(2,1)S(1)}, u32[]{:S(2)}, u32[]{:S(2)}) collective-permute-start(bf16[16,2048]{1,0:T(8,128)(2,1)S(1)} %collective-permute-done.1.refs_2_), channel_id=1, source_target_pairs={{0,1},{1,0},{2,3},{3,2},{4,5},{5,4},{6,7},{7,6},{8,9},{9,8},{10,11... | collective-permute-start | bytes 196616 | tf_op jit(solution)/shard_map/ppermute | solution.py:189
  21.8 9.0 %collective-permute-start.6 = (bf16[16,2048]{1,0:T(8,128)(2,1)S(1)}, bf16[16,2048]{1,0:T(8,128)(2,1)S(1)}, u32[]{:S(2)}, u32[]{:S(2)}) collective-permute-start(bf16[16,2048]{1,0:T(8,128)(2,1)S(1)} %collective-permute-done.2.refs_3_), channel_id=1, source_target_pairs={{0,1},{1,0},{2,3},{3,2},{4,5},{5,4},{6,7},{7,6},{8,9},{9,8},{10,11... | collective-permute-start | bytes 196616 | tf_op jit(solution)/shard_map/ppermute | solution.py:189
  25.1 26.8 %collective-permute-start.28 = (bf16[32,2048]{1,0:T(8,128)(2,1)}, bf16[32,2048]{1,0:T(8,128)(2,1)}, u32[]{:S(2)}, u32[]{:S(2)}) collective-permute-start(bf16[32,2048]{1,0:T(8,128)(2,1)} %refs_0_), channel_id=1, source_target_pairs={{0,2},{1,3},{2,0},{3,1},{4,6},{5,7},{6,4},{7,5},{8,10},{9,11},{10,... | collective-permute-start | bytes 393224 | tf_op jit(solution)/shard_map/ppermute | solution.py:189
  25.9 27.5 %collective-permute-start.29 = (bf16[32,2048]{1,0:T(8,128)(2,1)}, bf16[32,2048]{1,0:T(8,128)(2,1)}, u32[]{:S(2)}, u32[]{:S(2)}) collective-permute-start(bf16[32,2048]{1,0:T(8,128)(2,1)} %refs_0_), channel_id=1, source_target_pairs={{0,4},{1,5},{2,6},{3,7},{4,0},{5,1},{6,2},{7,3},{8,12},{9,13},{10,... | collective-permute-start | bytes 393224 | tf_op jit(solution)/shard_map/ppermute | solution.py:189
  28.5 25.5 %collective-permute-start.30 = (bf16[32,2048]{1,0:T(8,128)(2,1)}, bf16[32,2048]{1,0:T(8,128)(2,1)}, u32[]{:S(2)}, u32[]{:S(2)}) collective-permute-start(bf16[32,2048]{1,0:T(8,128)(2,1)} %refs_0_), channel_id=1, source_target_pairs={{0,6},{1,7},{2,4},{3,5},{4,2},{5,3},{6,0},{7,1},{8,14},{9,15},{10,... | collective-permute-start | bytes 393224 | tf_op jit(solution)/shard_map/ppermute | solution.py:189
  30.2 15.1 %collective-permute-start.18 = (bf16[16,2048]{1,0:T(8,128)(2,1)S(1)}, bf16[16,2048]{1,0:T(8,128)(2,1)S(1)}, u32[]{:S(2)}, u32[]{:S(2)}) collective-permute-start(bf16[16,2048]{1,0:T(8,128)(2,1)S(1)} %collective-permute-done.14.refs_1_), channel_id=1, source_target_pairs={{0,1},{1,0},{2,3},{3,2},{4,5},{5,4},{6,7},{7,6},{8,9},{9,8},{10,11... | collective-permute-start | bytes 196616 | tf_op jit(solution)/shard_map/ppermute | solution.py:189
  30.8 15.2 %collective-permute-start.19 = (bf16[16,2048]{1,0:T(8,128)(2,1)}, bf16[16,2048]{1,0:T(8,128)(2,1)S(1)}, u32[]{:S(2)}, u32[]{:S(2)}) collective-permute-start(bf16[16,2048]{1,0:T(8,128)(2,1)} %collective-permute-done.15.refs_2_), channel_id=1, source_target_pairs={{0,1},{1,0},{2,3},{3,2},{4,5},{5,4},{6,7},{7,6},{8,9},{9,8},{10,11... | collective-permute-start | bytes 196616 | tf_op jit(solution)/shard_map/ppermute | solution.py:189
  32.3 3.1 %copy-start = (bf16[2048,1792]{1,0:T(8,128)(2,1)S(1)}, bf16[2048,1792]{1,0:T(8,128)(2,1)}, u32[]{:S(2)}) copy-start(bf16[2048,1792]{1,0:T(8,128)(2,1)} %refs_8_.4) | copy-start | bytes 22020100
  45.3 25.2 %slice-start = ((s8[7340032]{0:T(1024)(128)(4,1)}), s8[3145728]{0:T(1024)(128)(4,1)S(1)}, s32[]{:S(2)}) async-start(s8[7340032]{0:T(1024)(128)(4,1)} %bitcast.55), calls=%async_computation | async-start | bytes 6291456
  45.9 30.2 %collective-permute-start.7 = (bf16[2,64,1792]{2,1,0:T(8,128)(2,1)}, bf16[2,64,1792]{2,1,0:T(8,128)(2,1)}, u32[]{:S(2)}, u32[]{:S(2)}) collective-permute-start(bf16[2,64,1792]{2,1,0:T(8,128)(2,1)} %get-tuple-element.22), channel_id=1, source_target_pairs={{0,8},{8,0},{16,24},{24,16},{1,9},{9,1},{17,25},{25,17},{2,10},{10... | collective-permute-start | bytes 1376264 | tf_op jit(solution)/shard_map/ppermute | solution.py:189
  46.5 4.8 %collective-permute-start.20 = (bf16[16,2048]{1,0:T(8,128)(2,1)}, bf16[16,2048]{1,0:T(8,128)(2,1)}, u32[]{:S(2)}, u32[]{:S(2)}) collective-permute-start(bf16[16,2048]{1,0:T(8,128)(2,1)} %collective-permute-done.16.refs_3_), channel_id=1, source_target_pairs={{0,1},{1,0},{2,3},{3,2},{4,5},{5,4},{6,7},{7,6},{8,9},{9,8},{10,11... | collective-permute-start | bytes 196616 | tf_op jit(solution)/shard_map/ppermute | solution.py:189
  48.9 21.6 %slice-start.1 = ((s8[7340032]{0:T(1024)(128)(4,1)}), s8[4194304]{0:T(1024)(128)(4,1)S(1)}, s32[]{:S(2)}) async-start(s8[7340032]{0:T(1024)(128)(4,1)} %bitcast.55), calls=%async_computation.1 | async-start | bytes 8388608
  51.4 19.0 %collective-permute-start.31 = (bf16[32,2048]{1,0:T(8,128)(2,1)}, bf16[32,2048]{1,0:T(8,128)(2,1)S(1)}, u32[]{:S(2)}, u32[]{:S(2)}) collective-permute-start(bf16[32,2048]{1,0:T(8,128)(2,1)} %refs_0_), channel_id=1, source_target_pairs={{0,1},{1,0},{2,3},{3,2},{4,5},{5,4},{6,7},{7,6},{8,9},{9,8},{10,11... | collective-permute-start | bytes 393224 | tf_op jit(solution)/shard_map/ppermute | solution.py:189
  51.9 18.6 %collective-permute-start.32 = (bf16[32,2048]{1,0:T(8,128)(2,1)}, bf16[32,2048]{1,0:T(8,128)(2,1)S(1)}, u32[]{:S(2)}, u32[]{:S(2)}) collective-permute-start(bf16[32,2048]{1,0:T(8,128)(2,1)} %collective-permute-done.28.refs_1_), channel_id=1, source_target_pairs={{0,1},{1,0},{2,3},{3,2},{4,5},{5,4},{6,7},{7,6},{8,9},{9,8},{10,11... | collective-permute-start | bytes 393224 | tf_op jit(solution)/shard_map/ppermute | solution.py:189
  53.4 17.1 %collective-permute-start.33 = (bf16[32,2048]{1,0:T(8,128)(2,1)}, bf16[32,2048]{1,0:T(8,128)(2,1)S(1)}, u32[]{:S(2)}, u32[]{:S(2)}) collective-permute-start(bf16[32,2048]{1,0:T(8,128)(2,1)} %collective-permute-done.29.refs_2_), channel_id=1, source_target_pairs={{0,1},{1,0},{2,3},{3,2},{4,5},{5,4},{6,7},{7,6},{8,9},{9,8},{10,11... | collective-permute-start | bytes 393224 | tf_op jit(solution)/shard_map/ppermute | solution.py:189
  54.0 16.5 %collective-permute-start.34 = (bf16[32,2048]{1,0:T(8,128)(2,1)}, bf16[32,2048]{1,0:T(8,128)(2,1)S(1)}, u32[]{:S(2)}, u32[]{:S(2)}) collective-permute-start(bf16[32,2048]{1,0:T(8,128)(2,1)} %collective-permute-done.30.refs_3_), channel_id=1, source_target_pairs={{0,1},{1,0},{2,3},{3,2},{4,5},{5,4},{6,7},{7,6},{8,9},{9,8},{10,11... | collective-permute-start | bytes 393224 | tf_op jit(solution)/shard_map/ppermute | solution.py:189
  55.4 3.1 %copy-start.1 = (bf16[2048,1792]{1,0:T(8,128)(2,1)S(1)}, bf16[2048,1792]{1,0:T(8,128)(2,1)}, u32[]{:S(2)}) copy-start(bf16[2048,1792]{1,0:T(8,128)(2,1)} %refs_8_.4) | copy-start | bytes 22020100
  58.5 3.1 %copy-start.3 = (bf16[2048,1792]{1,0:T(8,128)(2,1)S(1)}, bf16[2048,1792]{1,0:T(8,128)(2,1)}, u32[]{:S(2)}) copy-start(bf16[2048,1792]{1,0:T(8,128)(2,1)} %refs_9_.3) | copy-start | bytes 22020100
  65.0 5.6 %copy-start.6 = (bf16[32,2048]{1,0:T(8,128)(2,1)S(1)}, bf16[32,2048]{1,0:T(8,128)(2,1)}, u32[]{:S(2)}) copy-start(bf16[32,2048]{1,0:T(8,128)(2,1)} %refs_0_) | copy-start | bytes 393220
  65.0 11.2 %copy-start.5 = (bf16[2,64,1792]{2,1,0:T(8,128)(2,1)S(1)}, bf16[2,64,1792]{2,1,0:T(8,128)(2,1)}, u32[]{:S(2)}) copy-start(bf16[2,64,1792]{2,1,0:T(8,128)(2,1)} %copy-done.4) | copy-start | bytes 1376260
  70.4 8.5 %collective-permute-start.21 = (bf16[2,64,1792]{2,1,0:T(8,128)(2,1)S(1)}, bf16[2,64,1792]{2,1,0:T(8,128)(2,1)S(1)}, u32[]{:S(2)}, u32[]{:S(2)}) collective-permute-start(bf16[2,64,1792]{2,1,0:T(8,128)(2,1)S(1)} %get-tuple-element.27), channel_id=1, source_target_pairs={{0,8},{8,0},{16,24},{24,16},{1,9},{9,1},{17,25},{25,17},{2,10},{10... | collective-permute-start | bytes 1376264 | tf_op jit(solution)/shard_map/ppermute | solution.py:189
  75.6 4.0 %collective-permute-start.35 = (bf16[2,64,1792]{2,1,0:T(8,128)(2,1)S(1)}, bf16[2,64,1792]{2,1,0:T(8,128)(2,1)S(1)}, u32[]{:S(2)}, u32[]{:S(2)}) collective-permute-start(bf16[2,64,1792]{2,1,0:T(8,128)(2,1)S(1)} %get-tuple-element.34), channel_id=1, source_target_pairs={{0,8},{8,0},{16,24},{24,16},{1,9},{9,1},{17,25},{25,17},{2,10},{10... | collective-permute-start | bytes 1376264 | tf_op jit(solution)/shard_map/ppermute | solution.py:189
  77.3 13.4 %collective-permute-start.8 = (bf16[2,64,1792]{2,1,0:T(8,128)(2,1)S(1)}, bf16[2,64,1792]{2,1,0:T(8,128)(2,1)S(1)}, u32[]{:S(2)}, u32[]{:S(2)}) collective-permute-start(bf16[2,64,1792]{2,1,0:T(8,128)(2,1)S(1)} %add_convert_fusion.2), channel_id=1, source_target_pairs={{0,16},{8,24},{16,0},{24,8},{1,17},{9,25},{17,1},{25,9},{2,18},{10... | collective-permute-start | bytes 1376264 | tf_op jit(solution)/shard_map/ppermute | solution.py:189
  79.0 21.6 %collective-permute-start.22 = (bf16[2,64,1792]{2,1,0:T(8,128)(2,1)S(1)}, bf16[2,64,1792]{2,1,0:T(8,128)(2,1)S(1)}, u32[]{:S(2)}, u32[]{:S(2)}) collective-permute-start(bf16[2,64,1792]{2,1,0:T(8,128)(2,1)S(1)} %add_convert_fusion.1), channel_id=1, source_target_pairs={{0,16},{8,24},{16,0},{24,8},{1,17},{9,25},{17,1},{25,9},{2,18},{10... | collective-permute-start | bytes 1376264 | tf_op jit(solution)/shard_map/ppermute | solution.py:189
  79.7 29.8 %collective-permute-start.36 = (bf16[2,64,1792]{2,1,0:T(8,128)(2,1)S(1)}, bf16[2,64,1792]{2,1,0:T(8,128)(2,1)S(1)}, u32[]{:S(2)}, u32[]{:S(2)}) collective-permute-start(bf16[2,64,1792]{2,1,0:T(8,128)(2,1)S(1)} %add_convert_fusion), channel_id=1, source_target_pairs={{0,16},{8,24},{16,0},{24,8},{1,17},{9,25},{17,1},{25,9},{2,18},{10... | collective-permute-start | bytes 1376264 | tf_op jit(solution)/shard_map/ppermute | solution.py:189
  91.0 10.0 %collective-permute-start.9 = (bf16[64,1792]{1,0:T(8,128)(2,1)S(1)}, bf16[64,1792]{1,0:T(8,128)(2,1)S(1)}, u32[]{:S(2)}, u32[]{:S(2)}) collective-permute-start(bf16[64,1792]{1,0:T(8,128)(2,1)S(1)} %fusion.7.mine_ref.refs_1_), channel_id=1, source_target_pairs={{0,8},{8,0},{16,24},{24,16},{1,9},{9,1},{17,25},{25,17},{2,10},{10... | collective-permute-start | bytes 688136 | tf_op jit(solution)/shard_map/ppermute | solution.py:189
  100.9 9.4 %collective-permute-start.23 = (bf16[64,1792]{1,0:T(8,128)(2,1)S(1)}, bf16[64,1792]{1,0:T(8,128)(2,1)S(1)}, u32[]{:S(2)}, u32[]{:S(2)}) collective-permute-start(bf16[64,1792]{1,0:T(8,128)(2,1)S(1)} %fusion.3.mine_ref.refs_3_), channel_id=1, source_target_pairs={{0,8},{8,0},{16,24},{24,16},{1,9},{9,1},{17,25},{25,17},{2,10},{10... | collective-permute-start | bytes 688136 | tf_op jit(solution)/shard_map/ppermute | solution.py:189
  104.9 17.4 %collective-permute-start.10 = (bf16[64,2048]{1,0:T(8,128)(2,1)S(1)}, bf16[64,2048]{1,0:T(8,128)(2,1)S(1)}, u32[]{:S(2)}, u32[]{:S(2)}) collective-permute-start(bf16[64,2048]{1,0:T(8,128)(2,1)S(1)} %get-tuple-element.24), channel_id=1, source_target_pairs={{0,1},{1,0},{2,3},{3,2},{4,5},{5,4},{6,7},{7,6},{8,9},{9,8},{10,11... | collective-permute-start | bytes 786440 | tf_op jit(solution)/shard_map/ppermute | solution.py:189
  110.2 29.0 %copy-start.16 = (bf16[128,2048]{1,0:T(8,128)(2,1)S(1)}, bf16[128,2048]{1,0:T(8,128)(2,1)}, u32[]{:S(2)}) copy-start(bf16[128,2048]{1,0:T(8,128)(2,1)} %copy-done.15) | copy-start | bytes 1572868
  110.2 28.9 %collective-permute-start.37 = (bf16[2,2,64,1792]{3,2,1,0:T(8,128)(2,1)S(1)}, bf16[2,2,64,1792]{3,2,1,0:T(8,128)(2,1)S(1)}, u32[]{:S(2)}, u32[]{:S(2)}) collective-permute-start(bf16[2,2,64,1792]{3,2,1,0:T(8,128)(2,1)S(1)} %pad_maximum_fusion.1), channel_id=1, source_target_pairs={{0,8},{8,0},{16,24},{24,16},{1,9},{9,1},{17,25},{25,17},{2,10},{10... | collective-permute-start | bytes 2752520 | tf_op jit(solution)/shard_map/ppermute | solution.py:189
  114.2 12.7 %collective-permute-start.24 = (bf16[64,2048]{1,0:T(8,128)(2,1)S(1)}, bf16[64,2048]{1,0:T(8,128)(2,1)S(1)}, u32[]{:S(2)}, u32[]{:S(2)}) collective-permute-start(bf16[64,2048]{1,0:T(8,128)(2,1)S(1)} %get-tuple-element.29), channel_id=1, source_target_pairs={{0,1},{1,0},{2,3},{3,2},{4,5},{5,4},{6,7},{7,6},{8,9},{9,8},{10,11... | collective-permute-start | bytes 786440 | tf_op jit(solution)/shard_map/ppermute | solution.py:189
  122.4 6.8 %collective-permute-start.13 = (bf16[16,2048]{1,0:T(8,128)(2,1)S(1)}, bf16[16,2048]{1,0:T(8,128)(2,1)S(1)}, u32[]{:S(2)}, u32[]{:S(2)}) collective-permute-start(bf16[16,2048]{1,0:T(8,128)(2,1)S(1)} %get-tuple-element.53), channel_id=1, source_target_pairs={{0,6},{1,7},{2,4},{3,5},{4,2},{5,3},{6,0},{7,1},{8,14},{9,15},{10,... | collective-permute-start | bytes 196616 | tf_op jit(solution)/shard_map/ppermute | solution.py:189
  124.5 9.6 %collective-permute-start.12 = (bf16[16,2048]{1,0:T(8,128)(2,1)S(1)}, bf16[16,2048]{1,0:T(8,128)(2,1)S(1)}, u32[]{:S(2)}, u32[]{:S(2)}) collective-permute-start(bf16[16,2048]{1,0:T(8,128)(2,1)S(1)} %get-tuple-element.54), channel_id=1, source_target_pairs={{0,4},{1,5},{2,6},{3,7},{4,0},{5,1},{6,2},{7,3},{8,12},{9,13},{10,... | collective-permute-start | bytes 196616 | tf_op jit(solution)/shard_map/ppermute | solution.py:189
  124.5 9.6 %collective-permute-start.11 = (bf16[16,2048]{1,0:T(8,128)(2,1)S(1)}, bf16[16,2048]{1,0:T(8,128)(2,1)S(1)}, u32[]{:S(2)}, u32[]{:S(2)}) collective-permute-start(bf16[16,2048]{1,0:T(8,128)(2,1)S(1)} %get-tuple-element.52), channel_id=1, source_target_pairs={{0,2},{1,3},{2,0},{3,1},{4,6},{5,7},{6,4},{7,5},{8,10},{9,11},{10,... | collective-permute-start | bytes 196616 | tf_op jit(solution)/shard_map/ppermute | solution.py:189
  127.0 7.2 %collective-permute-start.27 = (bf16[16,2048]{1,0:T(8,128)(2,1)S(1)}, bf16[16,2048]{1,0:T(8,128)(2,1)S(1)}, u32[]{:S(2)}, u32[]{:S(2)}) collective-permute-start(bf16[16,2048]{1,0:T(8,128)(2,1)S(1)} %get-tuple-element.56), channel_id=1, source_target_pairs={{0,6},{1,7},{2,4},{3,5},{4,2},{5,3},{6,0},{7,1},{8,14},{9,15},{10,... | collective-permute-start | bytes 196616 | tf_op jit(solution)/shard_map/ppermute | solution.py:189
  129.2 7.6 %collective-permute-start.26 = (bf16[16,2048]{1,0:T(8,128)(2,1)S(1)}, bf16[16,2048]{1,0:T(8,128)(2,1)S(1)}, u32[]{:S(2)}, u32[]{:S(2)}) collective-permute-start(bf16[16,2048]{1,0:T(8,128)(2,1)S(1)} %get-tuple-element.57), channel_id=1, source_target_pairs={{0,4},{1,5},{2,6},{3,7},{4,0},{5,1},{6,2},{7,3},{8,12},{9,13},{10,... | collective-permute-start | bytes 196616 | tf_op jit(solution)/shard_map/ppermute | solution.py:189
  134.1 4.3 %collective-permute-start.25 = (bf16[16,2048]{1,0:T(8,128)(2,1)S(1)}, bf16[16,2048]{1,0:T(8,128)(2,1)S(1)}, u32[]{:S(2)}, u32[]{:S(2)}) collective-permute-start(bf16[16,2048]{1,0:T(8,128)(2,1)S(1)} %get-tuple-element.55), channel_id=1, source_target_pairs={{0,2},{1,3},{2,0},{3,1},{4,6},{5,7},{6,4},{7,5},{8,10},{9,11},{10,... | collective-permute-start | bytes 196616 | tf_op jit(solution)/shard_map/ppermute | solution.py:189
  (10 other events, 9.9 us)

commit v2 on v0

v2 whole, which is shorter than its diff:
```python
import functools

import jax
import jax.numpy as jnp
from jax import lax
from jax.experimental import pallas as pl
from jax.experimental.pallas import tpu as pltpu
from jax.sharding import PartitionSpec as P

BF16 = jnp.bfloat16
F32 = jnp.float32


SMALL = 20 * 2**20
LARGE = 32 * 2**20
LITTLE = pl.CostEstimate(flops=1, bytes_accessed=1, transcendentals=0)


def tile_of(size, most=896):
    return max(t for t in range(128, most + 1, 128) if size % t == 0)


def whole_vmem():
    return pl.BlockSpec(memory_space=pltpu.VMEM)


def token_spec():
    return pl.BlockSpec(memory_space=pl.ANY)


TOKEN = jax.ShapeDtypeStruct((8,), jnp.int32)


def hbm(array):
    return pltpu.with_memory_space_constraint(array, pltpu.HBM)


def masked(weight, mask_ref, first, block):
    rows = []
    for i in range(weight.shape[0] // block):
        columns = []
        for j in range(weight.shape[1] // block):
            part = weight[i * block:(i + 1) * block, j * block:(j + 1) * block]
            kept = mask_ref[first + i, j].astype(F32)
            if weight.dtype == BF16:
                factor = jnp.full((16, block), kept).astype(BF16)
                part = part.reshape(block // 16, 16, block) * factor[None]
                columns.append(part.reshape(block, block))
            else:
                columns.append(part * kept)
        rows.append(jnp.concatenate(columns, axis=1) if len(columns) > 1 else columns[0])
    return rows[0] if len(rows) == 1 else jnp.concatenate(rows, axis=0)


def panel_matmul(pieces, arrays, weights, masks, chunks, rows, *earlier):
    n_w = len(weights)
    depth, width = weights[0].shape
    half = len(pieces) // 2 * rows
    step = tile_of(depth, 256)
    block = depth // masks[0].shape[0]
    n_a = len(arrays)
    n_c = len(chunks)

    def kernel(*refs):
        core = lax.axis_index("row") % 2
        a_refs, w_refs = refs[:n_a], refs[n_a:n_a + n_w]
        m_refs = refs[n_a + n_w:n_a + 2 * n_w]
        out_panel, mine_ref, theirs_ref, token_ref, panel_ref, own, held, total, kept, sem, own_sem = refs[-11:]
        mask_copies = [
            pltpu.make_async_copy(m_refs[index], kept.at[index], own_sem.at[2 + index])
            for index in range(n_w)
        ]
        for copy in mask_copies:
            copy.start()
        copies = {}
        for part, low in enumerate(range(0, depth, step)):
            for index in range(n_w):
                at = pl.ds(low, step)
                copies[index, low] = pltpu.make_async_copy(
                    w_refs[index].at[at], held.at[index, at], sem.at[index, part]
                )
        fetch = pltpu.make_async_copy(a_refs[0], own, own_sem.at[0])
        fetch.start()
        for copy in copies.values():
            copy.start()
        fetch.wait()
        a_refs = (own, *a_refs[1:])
        for array, low, odd, k in pieces:
            place = 1 - core if odd else core
            for index, c in enumerate(chunks):
                start = pl.multiple_of(place * half + (index * 2 * half + k * rows), rows)
                panel_ref[pl.ds(start, rows), :] = a_refs[array][pl.ds(low + c * rows, rows), :]
        store = pltpu.make_async_copy(panel_ref, out_panel, own_sem.at[1])
        store.start()
        for copy in mask_copies:
            copy.wait()
        for low in range(0, depth, step):
            for index in range(n_w):
                copies[index, low].wait()
                w = masked(held[index, low:low + step, :], kept.at[index], low // block, block)
                part = jnp.dot(panel_ref[:, low:low + step], w, preferred_element_type=F32)
                if low > 0:
                    part = part + total[index]
                if low + step < depth:
                    total[index] = part
                else:
                    out = part.astype(BF16)
                    for c in range(n_c):
                        top = c * 2 * half
                        mine_ref[index * n_c + c] = out[top:top + half]
                        theirs_ref[index * n_c + c] = out[top + half:top + 2 * half]
        store.wait()

    part = jax.ShapeDtypeStruct((n_w * n_c, half, width), BF16)
    panel = jax.ShapeDtypeStruct((n_c * 2 * half, depth), BF16)
    return pl.pallas_call(
        kernel,
        in_specs=[pl.BlockSpec(memory_space=pl.ANY)]
        + [whole_vmem()] * (n_a - 1)
        + [pl.BlockSpec(memory_space=pl.ANY)] * (2 * n_w)
        + [token_spec()] * len(earlier),
        out_specs=[pl.BlockSpec(memory_space=pl.ANY)] + [whole_vmem()] * 2 + [token_spec()],
        out_shape=[pltpu.HBM(panel.shape, BF16), part, part, TOKEN],
        scratch_shapes=[
            pltpu.VMEM(panel.shape, BF16),
            pltpu.VMEM(arrays[0].shape, BF16),
            pltpu.VMEM((n_w, depth, width), BF16),
            pltpu.VMEM((n_w, *panel.shape[:1], width), F32),
            pltpu.SMEM((n_w, *masks[0].shape), jnp.int32),
            pltpu.SemaphoreType.DMA((n_w, depth // step)),
            pltpu.SemaphoreType.DMA((2 + n_w,)),
        ],
        compiler_params=pltpu.CompilerParams(vmem_limit_bytes=LARGE),
        cost_estimate=LITTLE,
    )(*arrays, *[hbm(w) for w in (*weights, *masks)], *earlier)


def output_matmul(hid_mine, hid_theirs, weight, mask):
    depth, width = weight.shape
    half = hid_mine.shape[0]
    step = tile_of(depth, 512)
    block = depth // mask.shape[0]

    def kernel(mine_ref, theirs_ref, w_ref, m_ref, even_ref, odd_ref, token_ref, hid, held, kept, sem):
        core = lax.axis_index("row") % 2
        mask_copy = pltpu.make_async_copy(m_ref, kept, sem.at[depth // step])
        mask_copy.start()
        copies = {}
        for part, low in enumerate(range(0, depth, step)):
            at = pl.ds(low, step)
            copies[low] = pltpu.make_async_copy(w_ref.at[at], held.at[at], sem.at[part])
        for copy in copies.values():
            copy.start()
        hid[pl.ds(pl.multiple_of(core * half, half), half), :] = mine_ref[...]
        hid[pl.ds(pl.multiple_of((1 - core) * half, half), half), :] = theirs_ref[...]
        mask_copy.wait()
        for low in range(0, depth, step):
            copies[low].wait()
            held[low:low + step, :] = masked(held[low:low + step, :], kept, low // block, block)
            out = lax.dot_general(
                hid[...],
                held[low:low + step, :],
                (((1,), (1,)), ((), ())),
                preferred_element_type=F32,
            ).astype(BF16)
            even_ref[:, low:low + step] = out[:half]
            odd_ref[:, low:low + step] = out[half:]

    out = jax.ShapeDtypeStruct((half, depth), BF16)
    return pl.pallas_call(
        kernel,
        in_specs=[whole_vmem()] * 2 + [pl.BlockSpec(memory_space=pl.ANY)] * 2,
        out_specs=[whole_vmem()] * 2 + [token_spec()],
        out_shape=[out, out, TOKEN],
        scratch_shapes=[
            pltpu.VMEM((2 * half, width), BF16),
            pltpu.VMEM((depth, width), BF16),
            pltpu.SMEM(mask.shape, jnp.int32),
            pltpu.SemaphoreType.DMA((depth // step + 1,)),
        ],
        compiler_params=pltpu.CompilerParams(vmem_limit_bytes=LARGE),
        cost_estimate=LITTLE,
    )(hid_mine, hid_theirs, hbm(weight), hbm(mask))


def join(values, *earlier):
    rows, depth = values[0].shape
    n = len(values)

    def kernel(*refs):
        for index in range(n):
            refs[-2][index * rows:(index + 1) * rows, :] = refs[index][...]

    return pl.pallas_call(
        kernel,
        in_specs=[whole_vmem()] * n + [token_spec()] * len(earlier),
        out_specs=[whole_vmem(), token_spec()],
        out_shape=[jax.ShapeDtypeStruct((n * rows, depth), values[0].dtype), TOKEN],
        compiler_params=pltpu.CompilerParams(vmem_limit_bytes=SMALL),
        cost_estimate=LITTLE,
    )(*values, *earlier)


def add_blocks(first, second, count, *earlier):
    rows = first.shape[0] // count

    def kernel(first_ref, second_ref, *refs):
        for index in range(count):
            at = slice(index * rows, (index + 1) * rows)
            total = first_ref[at].astype(F32) + second_ref[at].astype(F32)
            refs[len(earlier) + index][...] = total.astype(BF16)

    out = jax.ShapeDtypeStruct((rows, *first.shape[1:]), BF16)
    return pl.pallas_call(
        kernel,
        in_specs=[whole_vmem()] * 2 + [token_spec()] * len(earlier),
        out_specs=[whole_vmem()] * count + [token_spec()],
        out_shape=[out] * count + [TOKEN],
        compiler_params=pltpu.CompilerParams(vmem_limit_bytes=SMALL),
        cost_estimate=LITTLE,
    )(first, second, *earlier)


def add_shares(firsts, seconds, count):
    rows = firsts[0].shape[0] // count
    n_c = len(firsts)

    def kernel(*refs):
        for c in range(n_c):
            for index in range(count):
                at = slice(index * rows, (index + 1) * rows)
                total = refs[c][at].astype(F32) + refs[n_c + c][at].astype(F32)
                refs[2 * n_c + index][c * rows:(c + 1) * rows] = total.astype(BF16)

    out = jax.ShapeDtypeStruct((n_c * rows, *firsts[0].shape[1:]), BF16)
    return pl.pallas_call(
        kernel,
        in_specs=[whole_vmem()] * (2 * n_c),
        out_specs=[whole_vmem()] * count + [token_spec()],
        out_shape=[out] * count + [TOKEN],
        compiler_params=pltpu.CompilerParams(vmem_limit_bytes=SMALL),
        cost_estimate=LITTLE,
    )(*firsts, *seconds)


def total_of(refs, at):
    total = refs[0][at].astype(F32)
    for ref in refs[1:]:
        total = total + ref[at].astype(F32)
    return total


def hidden_of(parts, *earlier):
    _, rows, width = parts[0].shape
    n = len(parts)

    def kernel(*refs):
        gate, up = total_of(refs[:n], 0), total_of(refs[:n], 1)
        refs[-2][...] = (jax.nn.silu(gate) * up).astype(BF16)

    return pl.pallas_call(
        kernel,
        in_specs=[whole_vmem()] * n + [token_spec()] * len(earlier),
        out_specs=[whole_vmem(), token_spec()],
        out_shape=[jax.ShapeDtypeStruct((rows, width), BF16), TOKEN],
        compiler_params=pltpu.CompilerParams(vmem_limit_bytes=SMALL),
        cost_estimate=LITTLE,
    )(*parts, *earlier)


def cotangents(chunks, grads, *earlier):
    n_c, rows, width = grads[0].shape
    n, n_g = len(chunks[0]), len(grads)

    def kernel(*refs):
        out_ref = refs[-1]
        for c in range(n_c):
            parts = refs[c * n:(c + 1) * n]
            grad = total_of(refs[n_c * n:n_c * n + n_g], c)
            gate, up = total_of(parts, 0), total_of(parts, 1)
            s = jax.nn.sigmoid(gate)
            out_ref[0, c] = (grad * up * s * (1.0 + gate * (1.0 - s))).astype(BF16)
            out_ref[1, c] = (grad * gate * s).astype(BF16)

    return pl.pallas_call(
        kernel,
        in_specs=[whole_vmem()] * (n_c * n + n_g) + [token_spec()] * len(earlier),
        out_specs=whole_vmem(),
        out_shape=jax.ShapeDtypeStruct((2, n_c, rows, width), BF16),
        compiler_params=pltpu.CompilerParams(vmem_limit_bytes=SMALL),
        cost_estimate=LITTLE,
    )(*[p for c in chunks for p in c], *grads, *earlier)


def weight_grads(panels, cots, masks):
    depth = panels[0].shape[1]
    width = cots[0][0].shape[1]
    tokens = sum(p.shape[0] for p in panels)
    block = depth // masks[0].shape[0]
    tile = tile_of(depth, 256)
    n_p, n_c, n_o = len(panels), len(cots[0]), len(cots)
    slots = 4

    def kernel(*refs):
        p_refs = refs[:n_p]
        c_refs = refs[n_p:n_p + n_c * n_o]
        m_refs = refs[n_p + n_c * n_o:n_p + n_c * n_o + n_o]
        out_refs = refs[-7 - n_o:-7]
        token_ref, cot, panel, out, kept, sem, fetch_sem = refs[-7:]
        low = 0
        fetches = [
            pltpu.make_async_copy(m_refs[o], kept.at[o], fetch_sem.at[n_p + o]) for o in range(n_o)
        ]
        for fetch in fetches:
            fetch.start()
        for index, ref in enumerate(p_refs):
            fetches.append(
                pltpu.make_async_copy(ref, panel.at[pl.ds(low, ref.shape[0])], fetch_sem.at[index])
            )
            fetches[-1].start()
            low += ref.shape[0]
        for o in range(n_o):
            low = 0
            for ref in c_refs[o * n_c:(o + 1) * n_c]:
                cot[o, low:low + ref.shape[0], :] = ref[...]
                low += ref.shape[0]
        for fetch in fetches:
            fetch.wait()
        copies = []
        for low in range(0, depth, tile):
            for o in range(n_o):
                slot = len(copies) % slots
                if len(copies) >= slots:
                    copies[-slots].wait()
                part = lax.dot_general(
                    panel[:, low:low + tile],
                    cot[o],
                    (((0,), (0,)), ((), ())),
                    preferred_element_type=F32,
                )
                out[slot] = masked(part, kept.at[o], low // block, block)
                copies.append(
                    pltpu.make_async_copy(
                        out.at[slot], out_refs[o].at[pl.ds(low, tile)], sem.at[slot]
                    )
                )
                copies[-1].start()
        for copy in copies[-slots:]:
            copy.wait()

    flat = [a for cot in cots for a in cot]
    out = jax.ShapeDtypeStruct((depth, width), F32)
    return pl.pallas_call(
        kernel,
        in_specs=[pl.BlockSpec(memory_space=pl.ANY)] * n_p
        + [whole_vmem()] * len(flat)
        + [pl.BlockSpec(memory_space=pl.ANY)] * n_o,
        out_specs=[pl.BlockSpec(memory_space=pl.ANY)] * n_o + [token_spec()],
        out_shape=[out] * n_o + [TOKEN],
        scratch_shapes=[
            pltpu.VMEM((n_o, tokens, width), BF16),
            pltpu.VMEM((tokens, depth), BF16),
            pltpu.VMEM((slots, tile, width), F32),
            pltpu.SMEM((n_o, *masks[0].shape), jnp.int32),
            pltpu.SemaphoreType.DMA((slots,)),
            pltpu.SemaphoreType.DMA((n_p + n_o,)),
        ],
        compiler_params=pltpu.CompilerParams(vmem_limit_bytes=LARGE),
        cost_estimate=pl.CostEstimate(
            flops=2 * tokens * depth * width * n_o,
            bytes_accessed=4 * depth * width * n_o,
            transcendentals=0,
        ),
    )(*[hbm(p) for p in panels], *flat, *[hbm(m) for m in masks])


def swap(value, axis, bits):
    size = lax.axis_size(axis)
    return lax.ppermute(value, axis, [(i, i ^ bits) for i in range(size)])


def exchange(pair):
    return [pair] + [swap(pair, "row", 2 * k) for k in range(1, lax.axis_size("row") // 2)]


def output_sum(parts, *earlier):
    n = len(parts)

    def kernel(*refs):
        refs[-1][...] = total_of(refs[:n], slice(None)).astype(BF16)

    return pl.pallas_call(
        kernel,
        in_specs=[whole_vmem()] * n + [token_spec()] * len(earlier),
        out_specs=whole_vmem(),
        out_shape=jax.ShapeDtypeStruct(parts[0].shape, BF16),
        compiler_params=pltpu.CompilerParams(vmem_limit_bytes=SMALL),
        cost_estimate=LITTLE,
    )(*parts, *earlier)


CHUNKS = 2


def per_device(tokens, out_grad, w_gate, w_up, w_down, mask_gate, mask_up, mask_down):
    local = tokens.shape[0]
    rows = local // CHUNKS
    n_k = lax.axis_size("col") // 2
    every = range(CHUNKS)

    evens = [tokens] + [swap(tokens, "col", 2 * k) for k in range(1, n_k)]
    x_arrays = [hbm(tokens), *evens[1:]] + [swap(e, "col", 1) for e in evens]
    x_pieces = [(k + odd * n_k, 0, odd, k) for odd in (0, 1) for k in range(n_k)]
    dz_evens = [out_grad] + [swap(out_grad, "col", 2 * k) for k in range(1, n_k)]
    dz_pieces = [(odd, k * local, odd, k) for odd in (0, 1) for k in range(n_k)]

    panels, steps = [], []
    earlier = []
    for c in every:
        panel, mine, theirs, token = panel_matmul(
            x_pieces, x_arrays, [w_gate, w_up], [mask_gate, mask_up], [c], rows, *earlier
        )
        panels.append(panel)
        steps.append((mine, swap(theirs, "row", 1)))
        if c == 0:
            pair, first = add_blocks(*steps[0], 1)
            earlier = [first]
    dz_even, joined = join(dz_evens, token)
    dz_arrays = [dz_even, swap(dz_even, "col", 1)]

    chunks, hids, sums = [], [], []
    parts = exchange(pair)
    for c in every:
        chunks.append(parts)
        hid, formed = hidden_of(parts)
        if c + 1 < CHUNKS:
            pair, added = add_blocks(*steps[c + 1], 1, formed)
            parts = exchange(pair)
        else:
            dz_pair, added = add_blocks(*dz_step, 1, formed)
            grads = exchange(dz_pair)
        other = swap(hid, "row", 1)
        even, odd, token = output_matmul(hid, other, w_down, mask_down)
        sums.append((even, swap(odd, "col", 1)))
        hids += [hid, other]
        if c == 0:
            dz_panel, mine, theirs, token = panel_matmul(
                dz_pieces, dz_arrays, [w_down], [mask_down], every, rows, token
            )
            dz_step = (mine, swap(theirs, "row", 1))
    *shares, summed = add_shares(*zip(*sums), n_k)
    shares = shares[:1] + [swap(shares[k], "col", 2 * k) for k in range(1, n_k)]
    grad_down_w, _ = weight_grads([dz_panel], [hids], [mask_down])

    cot = cotangents(chunks, grads, summed)
    other = swap(cot, "row", 1)
    cots = [[a[o, c] for c in every for a in (cot, other)] for o in range(2)]
    grad_gate_w, grad_up_w, token = weight_grads(panels, cots, [mask_gate, mask_up])
    mixed = output_sum(shares, token)
    return (mixed, grad_gate_w, grad_up_w, grad_down_w)


def solution(mesh):
    return jax.shard_map(
        per_device,
        mesh=mesh,
        in_specs=(P("col", "row"),) * 2 + (P("row", "col"),) * 6,
        out_specs=(P("col", "row"),) + (P("row", "col"),) * 3,
        check_vma=False,
    )
```

time: 263 us -> 108 us (0.41)
  local copies, waits for them, and re-layouts: 86.1 us -> 0.13 us
  matrix products: 56.6 us -> 0 us
  Pallas kernels: 0 us -> 51.3 us
  waiting for transfers between devices: 76.6 us -> 27 us
  starting transfers between devices: 0.38 us -> 28.4 us
  blocking collectives: 18.7 us -> 0 us
  between operations: 13.9 us -> 0.84 us
  other arithmetic: 9.01 us -> 0 us
    unnamed x23 -> x2, local copies, waits for them, and re-layouts: 79.5 us -> 0.01 us
    dot_general x7 -> x0, matrix products: 56.6 us -> none  [the longest x1 10.9 us: per_device(): jnp.dot(x_panel.T, up_cot, preferred_element_type=jnp.float32)]
    pallas_call x0 -> x16, Pallas kernels: none -> 51.3 us  [the longest x3 21.6 us: panel_matmul(): pl.pallas_call(kernel, in_specs=[pl.BlockSpec(memory_space=pl.ANY)] + [wh...]
    psum x1 -> x0, waiting for transfers between devices: 38.1 us -> none  [per_device(): lax.psum(part_up.astype(jnp.bfloat16), 'row').astype(jnp.float32)]
    all_gather x2 -> x0, waiting for transfers between devices: 37.1 us -> none  [the longest x1 27 us: per_device(): lax.all_gather(out_grad, 'col', axis=0, tiled=True)]
    ppermute x0 -> x25, starting transfers between devices: none -> 28.4 us  [swap(): return lax.ppermute(value, axis, [(i, i ^ bits) for i in range(size)])]
    ppermute x0 -> x25, waiting for transfers between devices: none -> 27 us  [swap(): return lax.ppermute(value, axis, [(i, i ^ bits) for i in range(size)])]
    all_gather x2 -> x0, blocking collectives: 18.7 us -> none  [the longest x1 9.68 us: per_device(): lax.all_gather(grad_gate, 'row', axis=0, tiled=True)]
  transfers between devices with their start and end apart: 5 -> 25, of which waited for: 3 -> 11; matrix products, arithmetic and copies ran while one was open for 57% -> 0% of each run, Pallas kernels for 0% -> 39%
where the time goes in v2:
time: 108 us
  Pallas kernels  51.3 us (48%)
  starting transfers between devices  28.4 us (26%)
  waiting for transfers between devices  27 us (25%)
    ppermute x25, starting transfers between devices, swap(): return lax.ppermute(value, axis, [(i, i ^ bits) for i in range(size)])  28.4 us
    ppermute x25, waiting for transfers between devices, swap(): return lax.ppermute(value, axis, [(i, i ^ bits) for i in range(size)])  27 us
    pallas_call x3, Pallas kernels, panel_matmul(): pl.pallas_call(kernel, in_specs=[pl.BlockSpec(memory_space=pl.ANY)] + [wh...  21.6 us
    pallas_call x2, Pallas kernels, weight_grads(): pl.pallas_call(kernel, in_specs=[pl.BlockSpec(memory_space=pl.ANY)] * n_p...  18.4 us
    pallas_call x2, Pallas kernels, output_matmul(): pl.pallas_call(kernel, in_specs=[whole_vmem()] * 2 + [pl.BlockSpec(memory...  9.12 us
  transfers between devices with their start and end apart: 25, of which 11 were waited for; matrix products, arithmetic and copies ran while one was open for 0% of the time, Pallas kernels for 39%

profile of v2, /device:TPU:0, one launch (start us, length us, event | category | flops | bytes accessed | tf_op | source)
XLA Modules:
  0.0 107.7 jit_solution(13247557720453184232)
XLA Ops:
  0.6 3.1 %collective-permute-start = (bf16[32,2048]{1,0:T(8,128)(2,1)}, bf16[32,2048]{1,0:T(8,128)(2,1)S(1)}, u32[]{:S(2)}, u32[]{:S(2)}) collective-permute-start(bf16[32,2048]{1,0:T(8,128)(2,1)} %refs_0_.4), channel_id=1, source_target_pairs={{0,2},{1,3},{2,0},{3,1},{4,6},{5,7},{6,4},{7,5},{8,10},{9,11},{10,... | collective-permute-start | bytes 393224 | tf_op jit(solution)/shard_map/ppermute | solution.py:379
  3.7 2.6 %collective-permute-start.1 = (bf16[32,2048]{1,0:T(8,128)(2,1)}, bf16[32,2048]{1,0:T(8,128)(2,1)S(1)}, u32[]{:S(2)}, u32[]{:S(2)}) collective-permute-start(bf16[32,2048]{1,0:T(8,128)(2,1)} %refs_0_.4), channel_id=1, source_target_pairs={{0,4},{1,5},{2,6},{3,7},{4,0},{5,1},{6,2},{7,3},{8,12},{9,13},{10,... | collective-permute-start | bytes 393224 | tf_op jit(solution)/shard_map/ppermute | solution.py:379
  6.3 1.7 %collective-permute-start.3 = (bf16[32,2048]{1,0:T(8,128)(2,1)}, bf16[32,2048]{1,0:T(8,128)(2,1)S(1)}, u32[]{:S(2)}, u32[]{:S(2)}) collective-permute-start(bf16[32,2048]{1,0:T(8,128)(2,1)} %refs_0_.4), channel_id=1, source_target_pairs={{0,1},{1,0},{2,3},{3,2},{4,5},{5,4},{6,7},{7,6},{8,9},{9,8},{10,11... | collective-permute-start | bytes 393224 | tf_op jit(solution)/shard_map/ppermute | solution.py:379
  8.0 0.9 collective-permute-done.refs_1_
  9.0 1.7 %collective-permute-start.4 = (bf16[32,2048]{1,0:T(8,128)(2,1)S(1)}, bf16[32,2048]{1,0:T(8,128)(2,1)S(1)}, u32[]{:S(2)}, u32[]{:S(2)}) collective-permute-start(bf16[32,2048]{1,0:T(8,128)(2,1)S(1)} %collective-permute-done.refs_1_), channel_id=1, source_target_pairs={{0,1},{1,0},{2,3},{3,2},{4,5},{5,4},{6,7},{7,6},{8,9},{9,8},{10,11... | collective-permute-start | bytes 393224 | tf_op jit(solution)/shard_map/ppermute | solution.py:379
  10.7 6.2 %collective-permute-done.1.refs_2_ = bf16[32,2048]{1,0:T(8,128)(2,1)S(1)} collective-permute-done((bf16[32,2048]{1,0:T(8,128)(2,1)}, bf16[32,2048]{1,0:T(8,128)(2,1)S(1)}, u32[]{:S(2)}, u32[]{:S(2)}) %collective-permute-start.1) | collective-permute-done | bytes 131104 | tf_op jit(solution)/shard_map/ppermute | solution.py:379
  16.9 1.5 %collective-permute-start.5 = (bf16[32,2048]{1,0:T(8,128)(2,1)S(1)}, bf16[32,2048]{1,0:T(8,128)(2,1)S(1)}, u32[]{:S(2)}, u32[]{:S(2)}) collective-permute-start(bf16[32,2048]{1,0:T(8,128)(2,1)S(1)} %collective-permute-done.1.refs_2_), channel_id=1, source_target_pairs={{0,1},{1,0},{2,3},{3,2},{4,5},{5,4},{6,7},{7,6},{8,9},{9,8},{10,11... | collective-permute-start | bytes 393224 | tf_op jit(solution)/shard_map/ppermute | solution.py:379
  18.4 0.5 collective-permute-start.6
  18.9 2.9 %collective-permute-done.5.refs_6_ = bf16[32,2048]{1,0:T(8,128)(2,1)S(1)} collective-permute-done((bf16[32,2048]{1,0:T(8,128)(2,1)S(1)}, bf16[32,2048]{1,0:T(8,128)(2,1)S(1)}, u32[]{:S(2)}, u32[]{:S(2)}) %collective-permute-start.5) | collective-permute-done | bytes 131104 | tf_op jit(solution)/shard_map/ppermute | solution.py:379
  21.8 1.5 %collective-permute-done.6.refs_7_ = bf16[32,2048]{1,0:T(8,128)(2,1)S(1)} collective-permute-done((bf16[32,2048]{1,0:T(8,128)(2,1)S(1)}, bf16[32,2048]{1,0:T(8,128)(2,1)S(1)}, u32[]{:S(2)}, u32[]{:S(2)}) %collective-permute-start.6) | collective-permute-done | bytes 131104 | tf_op jit(solution)/shard_map/ppermute | solution.py:379
  23.3 8.4 %shard_map.111 = (bf16[128,2048]{1,0:T(8,128)(2,1)}, bf16[2,64,1792]{2,1,0:T(8,128)(2,1)S(1)}, bf16[2,64,1792]{2,1,0:T(8,128)(2,1)S(1)}, s32[8]{0:T(128)}) custom-call(bf16[32,2048]{1,0:T(8,128)(2,1)} %refs_0_.4, bf16[32,2048]{1,0:T(8,128)(2,1)S(1)} %collective-permute-done.refs_1_, bf16[32,2048]{1,0:T(8,128)(2,1)S(1)} %collective-permute-done.1.refs_2_, ...), custom_call_target="tpu_custom_call" | custom-call | flops 1 | bytes 1 | tf_op jit(solution)/shard_map/pallas_call | solution.py:116
  31.7 0.1 collective-permute-start.7
  31.8 1.8 %collective-permute-done.7.second_ref = bf16[2,64,1792]{2,1,0:T(8,128)(2,1)S(1)} collective-permute-done((bf16[2,64,1792]{2,1,0:T(8,128)(2,1)S(1)}, bf16[2,64,1792]{2,1,0:T(8,128)(2,1)S(1)}, u32[]{:S(2)}, u32[]{:S(2)}) %collective-permute-start.7) | collective-permute-done | bytes 458784 | tf_op jit(solution)/shard_map/ppermute | solution.py:379
  33.6 0.1 shard_map.112
  33.7 1.6 %collective-permute-start.8 = (bf16[2,64,1792]{2,1,0:T(8,128)(2,1)S(1)}, bf16[2,64,1792]{2,1,0:T(8,128)(2,1)S(1)}, u32[]{:S(2)}, u32[]{:S(2)}) collective-permute-start(bf16[2,64,1792]{2,1,0:T(8,128)(2,1)S(1)} %get-tuple-element.39.refs_0_), channel_id=1, source_target_pairs={{0,16},{8,24},{16,0},{24,8},{1,17},{9,25},{17,1},{25,9},{2,18},{10... | collective-permute-start | bytes 1376264 | tf_op jit(solution)/shard_map/ppermute | solution.py:379
  35.3 0.7 collective-permute-start.18
  36.0 2.1 %collective-permute-start.19 = (bf16[32,2048]{1,0:T(8,128)(2,1)S(1)}, bf16[32,2048]{1,0:T(8,128)(2,1)S(1)}, u32[]{:S(2)}, u32[]{:S(2)}) collective-permute-start(bf16[32,2048]{1,0:T(8,128)(2,1)S(1)} %copy-done), channel_id=1, source_target_pairs={{0,4},{1,5},{2,6},{3,7},{4,0},{5,1},{6,2},{7,3},{8,12},{9,13},{10,... | collective-permute-start | bytes 393224 | tf_op jit(solution)/shard_map/ppermute | solution.py:379
  38.1 1.5 %collective-permute-start.20 = (bf16[32,2048]{1,0:T(8,128)(2,1)S(1)}, bf16[32,2048]{1,0:T(8,128)(2,1)S(1)}, u32[]{:S(2)}, u32[]{:S(2)}) collective-permute-start(bf16[32,2048]{1,0:T(8,128)(2,1)S(1)} %copy-done), channel_id=1, source_target_pairs={{0,6},{1,7},{2,4},{3,5},{4,2},{5,3},{6,0},{7,1},{8,14},{9,15},{10,... | collective-permute-start | bytes 393224 | tf_op jit(solution)/shard_map/ppermute | solution.py:379
  39.7 8.4 %shard_map.115 = (bf16[128,2048]{1,0:T(8,128)(2,1)}, bf16[2,64,1792]{2,1,0:T(8,128)(2,1)S(1)}, bf16[2,64,1792]{2,1,0:T(8,128)(2,1)S(1)}, s32[8]{0:T(128)S(1)}) custom-call(bf16[32,2048]{1,0:T(8,128)(2,1)} %refs_0_.4, bf16[32,2048]{1,0:T(8,128)(2,1)S(1)} %collective-permute-done.refs_1_, bf16[32,2048]{1,0:T(8,128)(2,1)S(1)} %collective-permute-done.1.refs_2_, ...), custom_call_target="tpu_custom_call" | custom-call | flops 1 | bytes 1 | tf_op jit(solution)/shard_map/pallas_call | solution.py:116
  48.1 0.8 collective-permute-done.19.refs_2_
  48.9 1.6 %collective-permute-start.21 = (bf16[128,2048]{1,0:T(8,128)(2,1)S(1)}, bf16[128,2048]{1,0:T(8,128)(2,1)S(1)}, u32[]{:S(2)}, u32[]{:S(2)}) collective-permute-start(bf16[128,2048]{1,0:T(8,128)(2,1)S(1)} %get-tuple-element.58.refs_0_), channel_id=1, source_target_pairs={{0,1},{1,0},{2,3},{3,2},{4,5},{5,4},{6,7},{7,6},{8,9},{9,8},{10,11... | collective-permute-start | bytes 1572872 | tf_op jit(solution)/shard_map/ppermute | solution.py:379
  50.5 0.2 shard_map.113
  50.7 0.6 collective-permute-start.9
  51.2 1.1 collective-permute-done.10.second_ref
  52.3 0.1 shard_map.116
  52.4 0.6 collective-permute-start.11
  53.0 4.6 %shard_map.114 = (bf16[64,2048]{1,0:T(8,128)(2,1)S(1)}, bf16[64,2048]{1,0:T(8,128)(2,1)S(1)}, s32[8]{0:T(128)S(1)}) custom-call(bf16[64,1792]{1,0:T(8,128)(2,1)S(1)} %get-tuple-element.40.mine_ref.refs_1_, bf16[64,1792]{1,0:T(8,128)(2,1)S(1)} %collective-permute-done.9.theirs_ref.refs_2_, bf16[2048,1792]{1,0:T(8,128)(2,1)} %refs_2_.1, s32[16,14]{1,0:T(8,128)} %refs_5_.1), custom_call_target="tpu_custom_call" | custom-call | flops 1 | bytes 1 | tf_op jit(solution)/shard_map/pallas_call | solution.py:170
  57.6 3.5 %collective-permute-done.21.refs_1_ = bf16[128,2048]{1,0:T(8,128)(2,1)S(1)} collective-permute-done((bf16[128,2048]{1,0:T(8,128)(2,1)S(1)}, bf16[128,2048]{1,0:T(8,128)(2,1)S(1)}, u32[]{:S(2)}, u32[]{:S(2)}) %collective-permute-start.21) | collective-permute-done | bytes 524320 | tf_op jit(solution)/shard_map/ppermute | solution.py:379
  61.1 4.9 %shard_map.121 = (bf16[256,2048]{1,0:T(8,128)(2,1)}, bf16[2,64,1792]{2,1,0:T(8,128)(2,1)S(1)}, bf16[2,64,1792]{2,1,0:T(8,128)(2,1)S(1)}, s32[8]{0:T(128)}) custom-call(bf16[128,2048]{1,0:T(8,128)(2,1)S(1)} %get-tuple-element.58.refs_0_, bf16[128,2048]{1,0:T(8,128)(2,1)S(1)} %collective-permute-done.21.refs_1_, bf16[2048,1792]{1,0:T(8,128)(2,1)} %refs_2_.1, ...), custom_call_target="tpu_custom_call" | custom-call | flops 1 | bytes 1 | tf_op jit(solution)/shard_map/pallas_call | solution.py:116
  65.9 0.1 collective-permute-start.22
  66.0 0.2 shard_map.117
  66.2 0.5 collective-permute-start.12
  66.7 1.1 collective-permute-done.22.second_ref
  67.8 0.1 shard_map.122
  67.9 0.6 collective-permute-start.23
  68.5 1.4 %collective-permute-start.13 = (bf16[64,2048]{1,0:T(8,128)(2,1)S(1)}, bf16[64,2048]{1,0:T(8,128)(2,1)S(1)}, u32[]{:S(2)}, u32[]{:S(2)}) collective-permute-start(bf16[64,2048]{1,0:T(8,128)(2,1)S(1)} %get-tuple-element.49), channel_id=1, source_target_pairs={{0,1},{1,0},{2,3},{3,2},{4,5},{5,4},{6,7},{7,6},{8,9},{9,8},{10,11... | collective-permute-start | bytes 786440 | tf_op jit(solution)/shard_map/ppermute | solution.py:379
  69.9 4.6 %shard_map.118 = (bf16[64,2048]{1,0:T(8,128)(2,1)S(1)}, bf16[64,2048]{1,0:T(8,128)(2,1)S(1)}, s32[8]{0:T(128)}) custom-call(bf16[64,1792]{1,0:T(8,128)(2,1)S(1)} %get-tuple-element.47.mine_ref.refs_3_, bf16[64,1792]{1,0:T(8,128)(2,1)S(1)} %collective-permute-done.12.theirs_ref.refs_4_, bf16[2048,1792]{1,0:T(8,128)(2,1)} %refs_2_.1, s32[16,14]{1,0:T(8,128)} %refs_5_.1), custom_call_target="tpu_custom_call" | custom-call | flops 1 | bytes 1 | tf_op jit(solution)/shard_map/pallas_call | solution.py:170
  74.5 0.7 collective-permute-start.14
  75.2 1.4 %collective-permute-done.13.refs_2_ = bf16[64,2048]{1,0:T(8,128)(2,1)S(1)} collective-permute-done((bf16[64,2048]{1,0:T(8,128)(2,1)S(1)}, bf16[64,2048]{1,0:T(8,128)(2,1)S(1)}, u32[]{:S(2)}, u32[]{:S(2)}) %collective-permute-start.13) | collective-permute-done | bytes 262176 | tf_op jit(solution)/shard_map/ppermute | solution.py:379
  76.6 5.7 %collective-permute-done.14.refs_3_ = bf16[64,2048]{1,0:T(8,128)(2,1)S(1)} collective-permute-done((bf16[64,2048]{1,0:T(8,128)(2,1)S(1)}, bf16[64,2048]{1,0:T(8,128)(2,1)S(1)}, u32[]{:S(2)}, u32[]{:S(2)}) %collective-permute-start.14) | collective-permute-done | bytes 262176 | tf_op jit(solution)/shard_map/ppermute | solution.py:379
  82.3 0.1 shard_map.119
  82.4 0.6 shard_map.123
  83.2 7.0 %shard_map.126 = (f32[2048,1792]{1,0:T(8,128)}, s32[8]{0:T(128)}) custom-call(bf16[256,2048]{1,0:T(8,128)(2,1)} %get-tuple-element.68.refs_0_, bf16[64,1792]{1,0:T(8,128)(2,1)S(1)} %get-tuple-element.40.mine_ref.refs_1_, bf16[64,1792]{1,0:T(8,128)(2,1)S(1)} %collective-permute-done.9.theirs_ref.refs_2_, ...), custom_call_target="tpu_custom_call" | custom-call | flops 1879048192 | bytes 14680064 | tf_op jit(solution)/shard_map/pallas_call | solution.py:353
  90.2 2.8 %collective-permute-start.15 = (bf16[32,2048]{1,0:T(8,128)(2,1)S(1)}, bf16[32,2048]{1,0:T(8,128)(2,1)S(1)}, u32[]{:S(2)}, u32[]{:S(2)}) collective-permute-start(bf16[32,2048]{1,0:T(8,128)(2,1)S(1)} %get-tuple-element.52), channel_id=1, source_target_pairs={{0,2},{1,3},{2,0},{3,1},{4,6},{5,7},{6,4},{7,5},{8,10},{9,11},{10,... | collective-permute-start | bytes 393224 | tf_op jit(solution)/shard_map/ppermute | solution.py:379
  92.9 1.0 collective-permute-start.16
  93.9 1.4 %collective-permute-start.17 = (bf16[32,2048]{1,0:T(8,128)(2,1)S(1)}, bf16[32,2048]{1,0:T(8,128)(2,1)S(1)}, u32[]{:S(2)}, u32[]{:S(2)}) collective-permute-start(bf16[32,2048]{1,0:T(8,128)(2,1)S(1)} %get-tuple-element.54), channel_id=1, source_target_pairs={{0,6},{1,7},{2,4},{3,5},{4,2},{5,3},{6,0},{7,1},{8,14},{9,15},{10,... | collective-permute-start | bytes 393224 | tf_op jit(solution)/shard_map/ppermute | solution.py:379
  95.5 11.4 %shard_map.124 = (f32[2048,1792]{1,0:T(8,128)}, f32[2048,1792]{1,0:T(8,128)}, s32[8]{0:T(128)S(1)}) custom-call(bf16[128,2048]{1,0:T(8,128)(2,1)} %get-tuple-element.55.refs_0_, bf16[128,2048]{1,0:T(8,128)(2,1)} %get-tuple-element.56.refs_1_, bf16[64,1792]{1,0:T(8,128)(2,1)S(1)} %get-tuple-element.77.refs_2_, ...), custom_call_target="tpu_custom_call" | custom-call | flops 3758096384 | bytes 29360128 | tf_op jit(solution)/shard_map/pallas_call | solution.py:353
  107.0 0.7 shard_map.125
  (22 shorter events, 0.3 us)
Async XLA Ops:
  0.6 34.7 %copy-start = (bf16[32,2048]{1,0:T(8,128)(2,1)S(1)}, bf16[32,2048]{1,0:T(8,128)(2,1)}, u32[]{:S(2)}) copy-start(bf16[32,2048]{1,0:T(8,128)(2,1)} %refs_0_.5) | copy-start | bytes 393220
  0.6 8.3 %collective-permute-start = (bf16[32,2048]{1,0:T(8,128)(2,1)}, bf16[32,2048]{1,0:T(8,128)(2,1)S(1)}, u32[]{:S(2)}, u32[]{:S(2)}) collective-permute-start(bf16[32,2048]{1,0:T(8,128)(2,1)} %refs_0_.4), channel_id=1, source_target_pairs={{0,2},{1,3},{2,0},{3,1},{4,6},{5,7},{6,4},{7,5},{8,10},{9,11},{10,... | collective-permute-start | bytes 393224 | tf_op jit(solution)/shard_map/ppermute | solution.py:379
  3.7 13.2 %collective-permute-start.1 = (bf16[32,2048]{1,0:T(8,128)(2,1)}, bf16[32,2048]{1,0:T(8,128)(2,1)S(1)}, u32[]{:S(2)}, u32[]{:S(2)}) collective-permute-start(bf16[32,2048]{1,0:T(8,128)(2,1)} %refs_0_.4), channel_id=1, source_target_pairs={{0,4},{1,5},{2,6},{3,7},{4,0},{5,1},{6,2},{7,3},{8,12},{9,13},{10,... | collective-permute-start | bytes 393224 | tf_op jit(solution)/shard_map/ppermute | solution.py:379
  6.3 12.1 %collective-permute-start.2 = (bf16[32,2048]{1,0:T(8,128)(2,1)}, bf16[32,2048]{1,0:T(8,128)(2,1)S(1)}, u32[]{:S(2)}, u32[]{:S(2)}) collective-permute-start(bf16[32,2048]{1,0:T(8,128)(2,1)} %refs_0_.4), channel_id=1, source_target_pairs={{0,6},{1,7},{2,4},{3,5},{4,2},{5,3},{6,0},{7,1},{8,14},{9,15},{10,... | collective-permute-start | bytes 393224 | tf_op jit(solution)/shard_map/ppermute | solution.py:379
  6.3 12.6 %collective-permute-start.3 = (bf16[32,2048]{1,0:T(8,128)(2,1)}, bf16[32,2048]{1,0:T(8,128)(2,1)S(1)}, u32[]{:S(2)}, u32[]{:S(2)}) collective-permute-start(bf16[32,2048]{1,0:T(8,128)(2,1)} %refs_0_.4), channel_id=1, source_target_pairs={{0,1},{1,0},{2,3},{3,2},{4,5},{5,4},{6,7},{7,6},{8,9},{9,8},{10,11... | collective-permute-start | bytes 393224 | tf_op jit(solution)/shard_map/ppermute | solution.py:379
  9.0 9.9 %collective-permute-start.4 = (bf16[32,2048]{1,0:T(8,128)(2,1)S(1)}, bf16[32,2048]{1,0:T(8,128)(2,1)S(1)}, u32[]{:S(2)}, u32[]{:S(2)}) collective-permute-start(bf16[32,2048]{1,0:T(8,128)(2,1)S(1)} %collective-permute-done.refs_1_), channel_id=1, source_target_pairs={{0,1},{1,0},{2,3},{3,2},{4,5},{5,4},{6,7},{7,6},{8,9},{9,8},{10,11... | collective-permute-start | bytes 393224 | tf_op jit(solution)/shard_map/ppermute | solution.py:379
  16.9 5.0 %collective-permute-start.5 = (bf16[32,2048]{1,0:T(8,128)(2,1)S(1)}, bf16[32,2048]{1,0:T(8,128)(2,1)S(1)}, u32[]{:S(2)}, u32[]{:S(2)}) collective-permute-start(bf16[32,2048]{1,0:T(8,128)(2,1)S(1)} %collective-permute-done.1.refs_2_), channel_id=1, source_target_pairs={{0,1},{1,0},{2,3},{3,2},{4,5},{5,4},{6,7},{7,6},{8,9},{9,8},{10,11... | collective-permute-start | bytes 393224 | tf_op jit(solution)/shard_map/ppermute | solution.py:379
  18.4 5.0 %collective-permute-start.6 = (bf16[32,2048]{1,0:T(8,128)(2,1)S(1)}, bf16[32,2048]{1,0:T(8,128)(2,1)S(1)}, u32[]{:S(2)}, u32[]{:S(2)}) collective-permute-start(bf16[32,2048]{1,0:T(8,128)(2,1)S(1)} %collective-permute-done.2.refs_3_), channel_id=1, source_target_pairs={{0,1},{1,0},{2,3},{3,2},{4,5},{5,4},{6,7},{7,6},{8,9},{9,8},{10,11... | collective-permute-start | bytes 393224 | tf_op jit(solution)/shard_map/ppermute | solution.py:379
  31.7 1.9 %collective-permute-start.7 = (bf16[2,64,1792]{2,1,0:T(8,128)(2,1)S(1)}, bf16[2,64,1792]{2,1,0:T(8,128)(2,1)S(1)}, u32[]{:S(2)}, u32[]{:S(2)}) collective-permute-start(bf16[2,64,1792]{2,1,0:T(8,128)(2,1)S(1)} %get-tuple-element.38), channel_id=1, source_target_pairs={{0,8},{8,0},{16,24},{24,16},{1,9},{9,1},{17,25},{25,17},{2,10},{10... | collective-permute-start | bytes 1376264 | tf_op jit(solution)/shard_map/ppermute | solution.py:379
  33.7 16.8 %collective-permute-start.8 = (bf16[2,64,1792]{2,1,0:T(8,128)(2,1)S(1)}, bf16[2,64,1792]{2,1,0:T(8,128)(2,1)S(1)}, u32[]{:S(2)}, u32[]{:S(2)}) collective-permute-start(bf16[2,64,1792]{2,1,0:T(8,128)(2,1)S(1)} %get-tuple-element.39.refs_0_), channel_id=1, source_target_pairs={{0,16},{8,24},{16,0},{24,8},{1,17},{9,25},{17,1},{25,9},{2,18},{10... | collective-permute-start | bytes 1376264 | tf_op jit(solution)/shard_map/ppermute | solution.py:379
  35.3 12.8 %collective-permute-start.18 = (bf16[32,2048]{1,0:T(8,128)(2,1)S(1)}, bf16[32,2048]{1,0:T(8,128)(2,1)S(1)}, u32[]{:S(2)}, u32[]{:S(2)}) collective-permute-start(bf16[32,2048]{1,0:T(8,128)(2,1)S(1)} %copy-done), channel_id=1, source_target_pairs={{0,2},{1,3},{2,0},{3,1},{4,6},{5,7},{6,4},{7,5},{8,10},{9,11},{10,... | collective-permute-start | bytes 393224 | tf_op jit(solution)/shard_map/ppermute | solution.py:379
  36.0 12.9 %collective-permute-start.19 = (bf16[32,2048]{1,0:T(8,128)(2,1)S(1)}, bf16[32,2048]{1,0:T(8,128)(2,1)S(1)}, u32[]{:S(2)}, u32[]{:S(2)}) collective-permute-start(bf16[32,2048]{1,0:T(8,128)(2,1)S(1)} %copy-done), channel_id=1, source_target_pairs={{0,4},{1,5},{2,6},{3,7},{4,0},{5,1},{6,2},{7,3},{8,12},{9,13},{10,... | collective-permute-start | bytes 393224 | tf_op jit(solution)/shard_map/ppermute | solution.py:379
  38.1 10.8 %collective-permute-start.20 = (bf16[32,2048]{1,0:T(8,128)(2,1)S(1)}, bf16[32,2048]{1,0:T(8,128)(2,1)S(1)}, u32[]{:S(2)}, u32[]{:S(2)}) collective-permute-start(bf16[32,2048]{1,0:T(8,128)(2,1)S(1)} %copy-done), channel_id=1, source_target_pairs={{0,6},{1,7},{2,4},{3,5},{4,2},{5,3},{6,0},{7,1},{8,14},{9,15},{10,... | collective-permute-start | bytes 393224 | tf_op jit(solution)/shard_map/ppermute | solution.py:379
  48.9 12.1 %collective-permute-start.21 = (bf16[128,2048]{1,0:T(8,128)(2,1)S(1)}, bf16[128,2048]{1,0:T(8,128)(2,1)S(1)}, u32[]{:S(2)}, u32[]{:S(2)}) collective-permute-start(bf16[128,2048]{1,0:T(8,128)(2,1)S(1)} %get-tuple-element.58.refs_0_), channel_id=1, source_target_pairs={{0,1},{1,0},{2,3},{3,2},{4,5},{5,4},{6,7},{7,6},{8,9},{9,8},{10,11... | collective-permute-start | bytes 1572872 | tf_op jit(solution)/shard_map/ppermute | solution.py:379
  50.5 1.8 %collective-permute-start.10 = (bf16[2,64,1792]{2,1,0:T(8,128)(2,1)S(1)}, bf16[2,64,1792]{2,1,0:T(8,128)(2,1)S(1)}, u32[]{:S(2)}, u32[]{:S(2)}) collective-permute-start(bf16[2,64,1792]{2,1,0:T(8,128)(2,1)S(1)} %get-tuple-element.44), channel_id=1, source_target_pairs={{0,8},{8,0},{16,24},{24,16},{1,9},{9,1},{17,25},{25,17},{2,10},{10... | collective-permute-start | bytes 1376264 | tf_op jit(solution)/shard_map/ppermute | solution.py:379
  50.7 2.3 %collective-permute-start.9 = (bf16[64,1792]{1,0:T(8,128)(2,1)S(1)}, bf16[64,1792]{1,0:T(8,128)(2,1)S(1)}, u32[]{:S(2)}, u32[]{:S(2)}) collective-permute-start(bf16[64,1792]{1,0:T(8,128)(2,1)S(1)} %get-tuple-element.40.mine_ref.refs_1_), channel_id=1, source_target_pairs={{0,8},{8,0},{16,24},{24,16},{1,9},{9,1},{17,25},{25,17},{2,10},{10... | collective-permute-start | bytes 688136 | tf_op jit(solution)/shard_map/ppermute | solution.py:379
  52.4 13.6 %collective-permute-start.11 = (bf16[2,64,1792]{2,1,0:T(8,128)(2,1)S(1)}, bf16[2,64,1792]{2,1,0:T(8,128)(2,1)S(1)}, u32[]{:S(2)}, u32[]{:S(2)}) collective-permute-start(bf16[2,64,1792]{2,1,0:T(8,128)(2,1)S(1)} %get-tuple-element.46.refs_0_.refs_2_), channel_id=1, source_target_pairs={{0,16},{8,24},{16,0},{24,8},{1,17},{9,25},{17,1},{25,9},{2,18},{10... | collective-permute-start | bytes 1376264 | tf_op jit(solution)/shard_map/ppermute | solution.py:379
  65.9 1.9 %collective-permute-start.22 = (bf16[2,64,1792]{2,1,0:T(8,128)(2,1)S(1)}, bf16[2,64,1792]{2,1,0:T(8,128)(2,1)S(1)}, u32[]{:S(2)}, u32[]{:S(2)}) collective-permute-start(bf16[2,64,1792]{2,1,0:T(8,128)(2,1)S(1)} %get-tuple-element.61), channel_id=1, source_target_pairs={{0,8},{8,0},{16,24},{24,16},{1,9},{9,1},{17,25},{25,17},{2,10},{10... | collective-permute-start | bytes 1376264 | tf_op jit(solution)/shard_map/ppermute | solution.py:379
  66.2 3.7 %collective-permute-start.12 = (bf16[64,1792]{1,0:T(8,128)(2,1)S(1)}, bf16[64,1792]{1,0:T(8,128)(2,1)S(1)}, u32[]{:S(2)}, u32[]{:S(2)}) collective-permute-start(bf16[64,1792]{1,0:T(8,128)(2,1)S(1)} %get-tuple-element.47.mine_ref.refs_3_), channel_id=1, source_target_pairs={{0,8},{8,0},{16,24},{24,16},{1,9},{9,1},{17,25},{25,17},{2,10},{10... | collective-permute-start | bytes 688136 | tf_op jit(solution)/shard_map/ppermute | solution.py:379
  67.9 14.5 %collective-permute-start.23 = (bf16[2,64,1792]{2,1,0:T(8,128)(2,1)S(1)}, bf16[2,64,1792]{2,1,0:T(8,128)(2,1)S(1)}, u32[]{:S(2)}, u32[]{:S(2)}) collective-permute-start(bf16[2,64,1792]{2,1,0:T(8,128)(2,1)S(1)} %get-tuple-element.63.refs_4_), channel_id=1, source_target_pairs={{0,16},{8,24},{16,0},{24,8},{1,17},{9,25},{17,1},{25,9},{2,18},{10... | collective-permute-start | bytes 1376264 | tf_op jit(solution)/shard_map/ppermute | solution.py:379
  68.5 8.1 %collective-permute-start.13 = (bf16[64,2048]{1,0:T(8,128)(2,1)S(1)}, bf16[64,2048]{1,0:T(8,128)(2,1)S(1)}, u32[]{:S(2)}, u32[]{:S(2)}) collective-permute-start(bf16[64,2048]{1,0:T(8,128)(2,1)S(1)} %get-tuple-element.49), channel_id=1, source_target_pairs={{0,1},{1,0},{2,3},{3,2},{4,5},{5,4},{6,7},{7,6},{8,9},{9,8},{10,11... | collective-permute-start | bytes 786440 | tf_op jit(solution)/shard_map/ppermute | solution.py:379
  74.5 7.8 %collective-permute-start.14 = (bf16[64,2048]{1,0:T(8,128)(2,1)S(1)}, bf16[64,2048]{1,0:T(8,128)(2,1)S(1)}, u32[]{:S(2)}, u32[]{:S(2)}) collective-permute-start(bf16[64,2048]{1,0:T(8,128)(2,1)S(1)} %get-tuple-element.50), channel_id=1, source_target_pairs={{0,1},{1,0},{2,3},{3,2},{4,5},{5,4},{6,7},{7,6},{8,9},{9,8},{10,11... | collective-permute-start | bytes 786440 | tf_op jit(solution)/shard_map/ppermute | solution.py:379
  83.1 12.3 %collective-permute-start.24 = (bf16[2,2,64,1792]{3,2,1,0:T(8,128)(2,1)S(1)}, bf16[2,2,64,1792]{3,2,1,0:T(8,128)(2,1)S(1)}, u32[]{:S(2)}, u32[]{:S(2)}) collective-permute-start(bf16[2,2,64,1792]{3,2,1,0:T(8,128)(2,1)S(1)} %shard_map.123), channel_id=1, source_target_pairs={{0,8},{8,0},{16,24},{24,16},{1,9},{9,1},{17,25},{25,17},{2,10},{10... | collective-permute-start | bytes 2752520 | tf_op jit(solution)/shard_map/ppermute | solution.py:379
  90.2 16.8 %collective-permute-start.15 = (bf16[32,2048]{1,0:T(8,128)(2,1)S(1)}, bf16[32,2048]{1,0:T(8,128)(2,1)S(1)}, u32[]{:S(2)}, u32[]{:S(2)}) collective-permute-start(bf16[32,2048]{1,0:T(8,128)(2,1)S(1)} %get-tuple-element.52), channel_id=1, source_target_pairs={{0,2},{1,3},{2,0},{3,1},{4,6},{5,7},{6,4},{7,5},{8,10},{9,11},{10,... | collective-permute-start | bytes 393224 | tf_op jit(solution)/shard_map/ppermute | solution.py:379
  92.9 14.0 %collective-permute-start.16 = (bf16[32,2048]{1,0:T(8,128)(2,1)S(1)}, bf16[32,2048]{1,0:T(8,128)(2,1)S(1)}, u32[]{:S(2)}, u32[]{:S(2)}) collective-permute-start(bf16[32,2048]{1,0:T(8,128)(2,1)S(1)} %get-tuple-element.53), channel_id=1, source_target_pairs={{0,4},{1,5},{2,6},{3,7},{4,0},{5,1},{6,2},{7,3},{8,12},{9,13},{10,... | collective-permute-start | bytes 393224 | tf_op jit(solution)/shard_map/ppermute | solution.py:379
  93.9 13.0 %collective-permute-start.17 = (bf16[32,2048]{1,0:T(8,128)(2,1)S(1)}, bf16[32,2048]{1,0:T(8,128)(2,1)S(1)}, u32[]{:S(2)}, u32[]{:S(2)}) collective-permute-start(bf16[32,2048]{1,0:T(8,128)(2,1)S(1)} %get-tuple-element.54), channel_id=1, source_target_pairs={{0,6},{1,7},{2,4},{3,5},{4,2},{5,3},{6,0},{7,1},{8,14},{9,15},{10,... | collective-permute-start | bytes 393224 | tf_op jit(solution)/shard_map/ppermute | solution.py:379

commit v3 on v2

--- a/solution.py
+++ b/solution.py
@@ -52,22 +52,22 @@
     return rows[0] if len(rows) == 1 else jnp.concatenate(rows, axis=0)
 
 
-def panel_matmul(pieces, arrays, weights, masks, chunks, rows, *earlier):
+def panel_matmul(pieces, arrays, weights, masks, rows, *earlier):
     n_w = len(weights)
     depth, width = weights[0].shape
-    half = len(pieces) // 2 * rows
+    n_c = 1 + max(piece[2] for piece in pieces)
+    half = len(pieces) // (2 * n_c) * rows
     step = tile_of(depth, 256)
     block = depth // masks[0].shape[0]
     n_a = len(arrays)
-    n_c = len(chunks)
 
     def kernel(*refs):
         core = lax.axis_index("row") % 2
         a_refs, w_refs = refs[:n_a], refs[n_a:n_a + n_w]
         m_refs = refs[n_a + n_w:n_a + 2 * n_w]
-        out_panel, mine_ref, theirs_ref, token_ref, panel_ref, own, held, total, kept, sem, own_sem = refs[-11:]
+        out_panel, mine_ref, theirs_ref, token_ref, panel_ref, held, total, kept, sem, one_sem = refs[-10:]
         mask_copies = [
-            pltpu.make_async_copy(m_refs[index], kept.at[index], own_sem.at[2 + index])
+            pltpu.make_async_copy(m_refs[index], kept.at[index], one_sem.at[index])
             for index in range(n_w)
         ]
         for copy in mask_copies:
@@ -79,18 +79,13 @@
                 copies[index, low] = pltpu.make_async_copy(
                     w_refs[index].at[at], held.at[index, at], sem.at[index, part]
                 )
-        fetch = pltpu.make_async_copy(a_refs[0], own, own_sem.at[0])
-        fetch.start()
         for copy in copies.values():
             copy.start()
-        fetch.wait()
-        a_refs = (own, *a_refs[1:])
-        for array, low, odd, k in pieces:
-            place = 1 - core if odd else core
-            for index, c in enumerate(chunks):
-                start = pl.multiple_of(place * half + (index * 2 * half + k * rows), rows)
-                panel_ref[pl.ds(start, rows), :] = a_refs[array][pl.ds(low + c * rows, rows), :]
-        store = pltpu.make_async_copy(panel_ref, out_panel, own_sem.at[1])
+        for array, low, chunk, part, k in pieces:
+            place = 1 - core if part else core
+            start = pl.multiple_of(place * half + (chunk * 2 * half + k * rows), rows)
+            panel_ref[pl.ds(start, rows), :] = a_refs[array][pl.ds(low, rows), :]
+        store = pltpu.make_async_copy(panel_ref, out_panel, one_sem.at[n_w])
         store.start()
         for copy in mask_copies:
             copy.wait()
@@ -115,33 +110,34 @@
     panel = jax.ShapeDtypeStruct((n_c * 2 * half, depth), BF16)
     return pl.pallas_call(
         kernel,
-        in_specs=[pl.BlockSpec(memory_space=pl.ANY)]
-        + [whole_vmem()] * (n_a - 1)
+        in_specs=[whole_vmem()] * n_a
         + [pl.BlockSpec(memory_space=pl.ANY)] * (2 * n_w)
         + [token_spec()] * len(earlier),
         out_specs=[pl.BlockSpec(memory_space=pl.ANY)] + [whole_vmem()] * 2 + [token_spec()],
         out_shape=[pltpu.HBM(panel.shape, BF16), part, part, TOKEN],
         scratch_shapes=[
             pltpu.VMEM(panel.shape, BF16),
-            pltpu.VMEM(arrays[0].shape, BF16),
             pltpu.VMEM((n_w, depth, width), BF16),
             pltpu.VMEM((n_w, *panel.shape[:1], width), F32),
             pltpu.SMEM((n_w, *masks[0].shape), jnp.int32),
             pltpu.SemaphoreType.DMA((n_w, depth // step)),
-            pltpu.SemaphoreType.DMA((2 + n_w,)),
+            pltpu.SemaphoreType.DMA((1 + n_w,)),
         ],
         compiler_params=pltpu.CompilerParams(vmem_limit_bytes=LARGE),
         cost_estimate=LITTLE,
     )(*arrays, *[hbm(w) for w in (*weights, *masks)], *earlier)
 
 
-def output_matmul(hid_mine, hid_theirs, weight, mask):
+def output_matmul(hid_mine, hid_theirs, weight, mask, count):
     depth, width = weight.shape
     half = hid_mine.shape[0]
+    rows = 2 * half // count
     step = tile_of(depth, 512)
     block = depth // mask.shape[0]
 
-    def kernel(mine_ref, theirs_ref, w_ref, m_ref, even_ref, odd_ref, token_ref, hid, held, kept, sem):
+    def kernel(mine_ref, theirs_ref, w_ref, m_ref, *refs):
+        out_refs = refs[:count]
+        token_ref, hid, held, kept, sem = refs[count:]
         core = lax.axis_index("row") % 2
         mask_copy = pltpu.make_async_copy(m_ref, kept, sem.at[depth // step])
         mask_copy.start()
@@ -163,15 +159,15 @@
                 (((1,), (1,)), ((), ())),
                 preferred_element_type=F32,
             ).astype(BF16)
-            even_ref[:, low:low + step] = out[:half]
-            odd_ref[:, low:low + step] = out[half:]
-
-    out = jax.ShapeDtypeStruct((half, depth), BF16)
+            for k in range(count):
+                out_refs[k][:, low:low + step] = out[k * rows:(k + 1) * rows]
+
+    out = jax.ShapeDtypeStruct((rows, depth), BF16)
     return pl.pallas_call(
         kernel,
         in_specs=[whole_vmem()] * 2 + [pl.BlockSpec(memory_space=pl.ANY)] * 2,
-        out_specs=[whole_vmem()] * 2 + [token_spec()],
-        out_shape=[out, out, TOKEN],
+        out_specs=[whole_vmem()] * count + [token_spec()],
+        out_shape=[out] * count + [TOKEN],
         scratch_shapes=[
             pltpu.VMEM((2 * half, width), BF16),
             pltpu.VMEM((depth, width), BF16),
@@ -219,28 +215,6 @@
         compiler_params=pltpu.CompilerParams(vmem_limit_bytes=SMALL),
         cost_estimate=LITTLE,
     )(first, second, *earlier)
-
-
-def add_shares(firsts, seconds, count):
-    rows = firsts[0].shape[0] // count
-    n_c = len(firsts)
-
-    def kernel(*refs):
-        for c in range(n_c):
-            for index in range(count):
-                at = slice(index * rows, (index + 1) * rows)
-                total = refs[c][at].astype(F32) + refs[n_c + c][at].astype(F32)
-                refs[2 * n_c + index][c * rows:(c + 1) * rows] = total.astype(BF16)
-
-    out = jax.ShapeDtypeStruct((n_c * rows, *firsts[0].shape[1:]), BF16)
-    return pl.pallas_call(
-        kernel,
-        in_specs=[whole_vmem()] * (2 * n_c),
-        out_specs=[whole_vmem()] * count + [token_spec()],
-        out_shape=[out] * count + [TOKEN],
-        compiler_params=pltpu.CompilerParams(vmem_limit_bytes=SMALL),
-        cost_estimate=LITTLE,
-    )(*firsts, *seconds)
 
 
 def total_of(refs, at):
@@ -287,12 +261,12 @@
         in_specs=[whole_vmem()] * (n_c * n + n_g) + [token_spec()] * len(earlier),
         out_specs=whole_vmem(),
         out_shape=jax.ShapeDtypeStruct((2, n_c, rows, width), BF16),
-        compiler_params=pltpu.CompilerParams(vmem_limit_bytes=SMALL),
+        compiler_params=pltpu.CompilerParams(vmem_limit_bytes=max(SMALL, 48 * n_c * rows * width)),
         cost_estimate=LITTLE,
     )(*[p for c in chunks for p in c], *grads, *earlier)
 
 
-def weight_grads(panels, cots, masks):
+def weight_grads(panels, cots, masks, *earlier, cost=None):
     depth = panels[0].shape[1]
     width = cots[0][0].shape[1]
     tokens = sum(p.shape[0] for p in panels)
@@ -354,7 +328,8 @@
         kernel,
         in_specs=[pl.BlockSpec(memory_space=pl.ANY)] * n_p
         + [whole_vmem()] * len(flat)
-        + [pl.BlockSpec(memory_space=pl.ANY)] * n_o,
+        + [pl.BlockSpec(memory_space=pl.ANY)] * n_o
+        + [token_spec()] * len(earlier),
         out_specs=[pl.BlockSpec(memory_space=pl.ANY)] * n_o + [token_spec()],
         out_shape=[out] * n_o + [TOKEN],
         scratch_shapes=[
@@ -366,12 +341,13 @@
             pltpu.SemaphoreType.DMA((n_p + n_o,)),
         ],
         compiler_params=pltpu.CompilerParams(vmem_limit_bytes=LARGE),
-        cost_estimate=pl.CostEstimate(
+        cost_estimate=cost
+        or pl.CostEstimate(
             flops=2 * tokens * depth * width * n_o,
             bytes_accessed=4 * depth * width * n_o,
             transcendentals=0,
         ),
-    )(*[hbm(p) for p in panels], *flat, *[hbm(m) for m in masks])
+    )(*[hbm(p) for p in panels], *flat, *[hbm(m) for m in masks], *earlier)
 
 
 def swap(value, axis, bits):
@@ -383,80 +359,85 @@
     return [pair] + [swap(pair, "row", 2 * k) for k in range(1, lax.axis_size("row") // 2)]
 
 
-def output_sum(parts, *earlier):
+def output_sum(parts, dtype, *earlier):
     n = len(parts)
 
     def kernel(*refs):
-        refs[-1][...] = total_of(refs[:n], slice(None)).astype(BF16)
+        refs[-2][...] = total_of(refs[:n], slice(None)).astype(dtype)
 
     return pl.pallas_call(
         kernel,
         in_specs=[whole_vmem()] * n + [token_spec()] * len(earlier),
-        out_specs=whole_vmem(),
-        out_shape=jax.ShapeDtypeStruct(parts[0].shape, BF16),
+        out_specs=[whole_vmem(), token_spec()],
+        out_shape=[jax.ShapeDtypeStruct(parts[0].shape, dtype), TOKEN],
         compiler_params=pltpu.CompilerParams(vmem_limit_bytes=SMALL),
         cost_estimate=LITTLE,
     )(*parts, *earlier)
 
 
-CHUNKS = 2
-
-
 def per_device(tokens, out_grad, w_gate, w_up, w_down, mask_gate, mask_up, mask_down):
-    local = tokens.shape[0]
-    rows = local // CHUNKS
+    rows = tokens.shape[0]
     n_k = lax.axis_size("col") // 2
-    every = range(CHUNKS)
+    part = n_k // 2
+
+    def places(chunk, k):
+        return chunk, k // part, k % part
 
     evens = [tokens] + [swap(tokens, "col", 2 * k) for k in range(1, n_k)]
-    x_arrays = [hbm(tokens), *evens[1:]] + [swap(e, "col", 1) for e in evens]
-    x_pieces = [(k + odd * n_k, 0, odd, k) for odd in (0, 1) for k in range(n_k)]
-    dz_evens = [out_grad] + [swap(out_grad, "col", 2 * k) for k in range(1, n_k)]
-    dz_pieces = [(odd, k * local, odd, k) for odd in (0, 1) for k in range(n_k)]
-
-    panels, steps = [], []
-    earlier = []
-    for c in every:
-        panel, mine, theirs, token = panel_matmul(
-            x_pieces, x_arrays, [w_gate, w_up], [mask_gate, mask_up], [c], rows, *earlier
-        )
-        panels.append(panel)
-        steps.append((mine, swap(theirs, "row", 1)))
-        if c == 0:
-            pair, first = add_blocks(*steps[0], 1)
-            earlier = [first]
-    dz_even, joined = join(dz_evens, token)
+    own, swapped = join([tokens, swap(tokens, "col", 1)])
+    panel, mine, theirs, token = panel_matmul(
+        [(k, 0, *places(0, k)) for k in range(n_k)],
+        [own, *evens[1:]],
+        [w_gate, w_up],
+        [mask_gate, mask_up],
+        rows,
+        swapped,
+    )
+    rest, _ = join(evens[1:], token)
+    rest_odd = swap(rest, "col", 1)
+    pair, first = add_blocks(mine, swap(theirs, "row", 1), 1)
+    parts = exchange(pair)
+    dz_even, joined = join([out_grad] + [swap(out_grad, "col", 2 * k) for k in range(1, n_k)], first)
+    panel_odd, mine, theirs, token = panel_matmul(
+        [(min(k, 1), max(k - 1, 0) * rows if k else rows, *places(0, k)) for k in range(n_k)],
+        [own, rest_odd],
+        [w_gate, w_up],
+        [mask_gate, mask_up],
+        rows,
+        first,
+        joined,
+    )
+    panels = [panel, panel_odd]
+    step = (mine, swap(theirs, "row", 1))
+
     dz_arrays = [dz_even, swap(dz_even, "col", 1)]
-
-    chunks, hids, sums = [], [], []
-    parts = exchange(pair)
-    for c in every:
+    dz_pieces = [(c, k * rows, *places(c, k)) for c in range(2) for k in range(n_k)]
+
+    chunks, hids, outs = [], [], []
+    for c in range(2):
         chunks.append(parts)
         hid, formed = hidden_of(parts)
-        if c + 1 < CHUNKS:
-            pair, added = add_blocks(*steps[c + 1], 1, formed)
-            parts = exchange(pair)
-        else:
-            dz_pair, added = add_blocks(*dz_step, 1, formed)
-            grads = exchange(dz_pair)
+        pair, added = add_blocks(*step, 1, formed)
+        parts = exchange(pair)
         other = swap(hid, "row", 1)
-        even, odd, token = output_matmul(hid, other, w_down, mask_down)
-        sums.append((even, swap(odd, "col", 1)))
+        *out, token = output_matmul(hid, other, w_down, mask_down, n_k)
+        outs.append(out)
         hids += [hid, other]
         if c == 0:
             dz_panel, mine, theirs, token = panel_matmul(
-                dz_pieces, dz_arrays, [w_down], [mask_down], every, rows, token
+                dz_pieces, dz_arrays, [w_down], [mask_down], rows, token
             )
-            dz_step = (mine, swap(theirs, "row", 1))
-    *shares, summed = add_shares(*zip(*sums), n_k)
-    shares = shares[:1] + [swap(shares[k], "col", 2 * k) for k in range(1, n_k)]
-    grad_down_w, _ = weight_grads([dz_panel], [hids], [mask_down])
-
-    cot = cotangents(chunks, grads, summed)
+            step = (mine, swap(theirs, "row", 1))
+    own_share = outs[0][:1] + [swap(outs[0][k], "col", 2 * k) for k in range(1, n_k)]
+    grad_down_w, token = weight_grads([dz_panel], [hids], [mask_down], token, cost=LITTLE)
+    own_share, token = output_sum(own_share, F32, token)
+    shares = [own_share] + [swap(outs[1][k], "col", 2 * k + 1) for k in range(n_k)]
+
+    cot = cotangents(chunks, parts, token)
     other = swap(cot, "row", 1)
-    cots = [[a[o, c] for c in every for a in (cot, other)] for o in range(2)]
+    cots = [[a[o, c] for c in range(2) for a in (cot, other)] for o in range(2)]
     grad_gate_w, grad_up_w, token = weight_grads(panels, cots, [mask_gate, mask_up])
-    mixed = output_sum(shares, token)
+    mixed, _ = output_sum(shares, BF16, token)
     return (mixed, grad_gate_w, grad_up_w, grad_down_w)
 
 

time: 108 us -> 101 us (0.935)
  Pallas kernels: 51.3 us -> 46.4 us
  waiting for transfers between devices: 27 us -> 23.1 us
    pallas_call x4 -> x3, Pallas kernels: 21.7 us -> 16.6 us  [panel_matmul(): pl.pallas_call(kernel, in_specs=[whole_vmem()] * n_a + [pl.BlockSpec(memo...]
    ppermute x25, waiting for transfers between devices: 27 us -> 23.1 us  [swap(): return lax.ppermute(value, axis, [(i, i ^ bits) for i in range(size)])]
  transfers between devices with their start and end apart: 25 -> 25, of which waited for: 11 -> 7; matrix products, arithmetic and copies ran while one was open for 0% -> 0% of each run, Pallas kernels for 39% -> 39%
where the time goes in v3:
time: 101 us; the launch traced here: 100 us
  Pallas kernels  46.4 us (46%)
  starting transfers between devices  28.7 us (28%)
  waiting for transfers between devices  23.1 us (23%)
  local copies, waits for them, and re-layouts  1.06 us (1%)
    ppermute x25, starting transfers between devices, swap(): return lax.ppermute(value, axis, [(i, i ^ bits) for i in range(size)])  28.7 us
    ppermute x25, waiting for transfers between devices, swap(): return lax.ppermute(value, axis, [(i, i ^ bits) for i in range(size)])  23.1 us
    pallas_call x2, Pallas kernels, weight_grads(): pl.pallas_call(kernel, in_specs=[pl.BlockSpec(memory_space=pl.ANY)] * n_p...  18.4 us
    pallas_call x3, Pallas kernels, panel_matmul(): pl.pallas_call(kernel, in_specs=[whole_vmem()] * n_a + [pl.BlockSpec(memo...  16.6 us
    pallas_call x2, Pallas kernels, output_matmul(): pl.pallas_call(kernel, in_specs=[whole_vmem()] * 2 + [pl.BlockSpec(memory...  9.12 us
  transfers between devices with their start and end apart: 25, of which 7 were waited for; matrix products, arithmetic and copies ran while one was open for 0% of the time, Pallas kernels for 39%

profile of v3, /device:TPU:0, one launch (start us, length us, event | category | flops | bytes accessed | tf_op | source)
XLA Modules:
  0.0 100.1 jit_solution(6664519852557688562)
XLA Ops:
  0.6 3.0 %collective-permute-start = (bf16[32,2048]{1,0:T(8,128)(2,1)}, bf16[32,2048]{1,0:T(8,128)(2,1)S(1)}, u32[]{:S(2)}, u32[]{:S(2)}) collective-permute-start(bf16[32,2048]{1,0:T(8,128)(2,1)} %refs_0_.2), channel_id=1, source_target_pairs={{0,1},{1,0},{2,3},{3,2},{4,5},{5,4},{6,7},{7,6},{8,9},{9,8},{10,11... | collective-permute-start | bytes 393224 | tf_op jit(solution)/shard_map/ppermute | solution.py:355
  3.6 1.6 %collective-permute-start.1 = (bf16[32,2048]{1,0:T(8,128)(2,1)}, bf16[32,2048]{1,0:T(8,128)(2,1)S(1)}, u32[]{:S(2)}, u32[]{:S(2)}) collective-permute-start(bf16[32,2048]{1,0:T(8,128)(2,1)} %refs_0_.2), channel_id=1, source_target_pairs={{0,2},{1,3},{2,0},{3,1},{4,6},{5,7},{6,4},{7,5},{8,10},{9,11},{10,... | collective-permute-start | bytes 393224 | tf_op jit(solution)/shard_map/ppermute | solution.py:355
  5.2 2.5 %collective-permute-start.3 = (bf16[32,2048]{1,0:T(8,128)(2,1)}, bf16[32,2048]{1,0:T(8,128)(2,1)S(1)}, u32[]{:S(2)}, u32[]{:S(2)}) collective-permute-start(bf16[32,2048]{1,0:T(8,128)(2,1)} %refs_0_.2), channel_id=1, source_target_pairs={{0,6},{1,7},{2,4},{3,5},{4,2},{5,3},{6,0},{7,1},{8,14},{9,15},{10,... | collective-permute-start | bytes 393224 | tf_op jit(solution)/shard_map/ppermute | solution.py:355
  7.7 0.1 collective-permute-start.2
  7.8 0.9 copy-done.1
  8.8 6.2 %collective-permute-done.3.refs_3_.refs_2_ = bf16[32,2048]{1,0:T(8,128)(2,1)S(1)} collective-permute-done((bf16[32,2048]{1,0:T(8,128)(2,1)}, bf16[32,2048]{1,0:T(8,128)(2,1)S(1)}, u32[]{:S(2)}, u32[]{:S(2)}) %collective-permute-start.3) | collective-permute-done | bytes 131104 | tf_op jit(solution)/shard_map/ppermute | solution.py:355
  15.1 4.4 %collective-permute-done.2.refs_2_.refs_1_ = bf16[32,2048]{1,0:T(8,128)(2,1)S(1)} collective-permute-done((bf16[32,2048]{1,0:T(8,128)(2,1)}, bf16[32,2048]{1,0:T(8,128)(2,1)S(1)}, u32[]{:S(2)}, u32[]{:S(2)}) %collective-permute-start.2) | collective-permute-done | bytes 131104 | tf_op jit(solution)/shard_map/ppermute | solution.py:355
  19.4 5.9 %shard_map.112 = (bf16[128,2048]{1,0:T(8,128)(2,1)}, bf16[2,64,1792]{2,1,0:T(8,128)(2,1)S(1)}, bf16[2,64,1792]{2,1,0:T(8,128)(2,1)S(1)}, s32[8]{0:T(128)S(1)}) custom-call(bf16[64,2048]{1,0:T(8,128)(2,1)S(1)} %get-tuple-element.45.refs_0_, bf16[32,2048]{1,0:T(8,128)(2,1)S(1)} %collective-permute-done.1.refs_1_.refs_0_, ...), custom_call_target="tpu_custom_call" | custom-call | flops 1 | bytes 1 | tf_op jit(solution)/shard_map/pallas_call | solution.py:111
  25.3 0.1 collective-permute-start.4
  25.4 0.6 collective-permute-start.14
  26.0 1.2 %collective-permute-done.4.second_ref = bf16[2,64,1792]{2,1,0:T(8,128)(2,1)S(1)} collective-permute-done((bf16[2,64,1792]{2,1,0:T(8,128)(2,1)S(1)}, bf16[2,64,1792]{2,1,0:T(8,128)(2,1)S(1)}, u32[]{:S(2)}, u32[]{:S(2)}) %collective-permute-start.4) | collective-permute-done | bytes 458784 | tf_op jit(solution)/shard_map/ppermute | solution.py:355
  27.2 0.1 shard_map.113
  27.3 1.6 %collective-permute-start.5 = (bf16[2,64,1792]{2,1,0:T(8,128)(2,1)S(1)}, bf16[2,64,1792]{2,1,0:T(8,128)(2,1)S(1)}, u32[]{:S(2)}, u32[]{:S(2)}) collective-permute-start(bf16[2,64,1792]{2,1,0:T(8,128)(2,1)S(1)} %get-tuple-element.49.refs_0_), channel_id=1, source_target_pairs={{0,16},{8,24},{16,0},{24,8},{1,17},{9,25},{17,1},{25,9},{2,18},{10... | collective-permute-start | bytes 1376264 | tf_op jit(solution)/shard_map/ppermute | solution.py:355
  28.9 0.2 collective-permute-start.11
  29.1 3.0 %collective-permute-start.10 = (bf16[32,2048]{1,0:T(8,128)(2,1)S(1)}, bf16[32,2048]{1,0:T(8,128)(2,1)S(1)}, u32[]{:S(2)}, u32[]{:S(2)}) collective-permute-start(bf16[32,2048]{1,0:T(8,128)(2,1)S(1)} %copy-done), channel_id=1, source_target_pairs={{0,2},{1,3},{2,0},{3,1},{4,6},{5,7},{6,4},{7,5},{8,10},{9,11},{10,... | collective-permute-start | bytes 393224 | tf_op jit(solution)/shard_map/ppermute | solution.py:355
  32.1 1.2 %collective-permute-start.12 = (bf16[32,2048]{1,0:T(8,128)(2,1)S(1)}, bf16[32,2048]{1,0:T(8,128)(2,1)S(1)}, u32[]{:S(2)}, u32[]{:S(2)}) collective-permute-start(bf16[32,2048]{1,0:T(8,128)(2,1)S(1)} %copy-done), channel_id=1, source_target_pairs={{0,6},{1,7},{2,4},{3,5},{4,2},{5,3},{6,0},{7,1},{8,14},{9,15},{10,... | collective-permute-start | bytes 393224 | tf_op jit(solution)/shard_map/ppermute | solution.py:355
  33.3 5.5 %collective-permute-done.11.refs_2_ = bf16[32,2048]{1,0:T(8,128)(2,1)S(1)} collective-permute-done((bf16[32,2048]{1,0:T(8,128)(2,1)S(1)}, bf16[32,2048]{1,0:T(8,128)(2,1)S(1)}, u32[]{:S(2)}, u32[]{:S(2)}) %collective-permute-start.11) | collective-permute-done | bytes 131104 | tf_op jit(solution)/shard_map/ppermute | solution.py:355
  38.8 2.1 %collective-permute-done.10.refs_1_ = bf16[32,2048]{1,0:T(8,128)(2,1)S(1)} collective-permute-done((bf16[32,2048]{1,0:T(8,128)(2,1)S(1)}, bf16[32,2048]{1,0:T(8,128)(2,1)S(1)}, u32[]{:S(2)}, u32[]{:S(2)}) %collective-permute-start.10) | collective-permute-done | bytes 131104 | tf_op jit(solution)/shard_map/ppermute | solution.py:355
  40.9 0.6 collective-permute-start.13
  41.5 5.9 %shard_map.119 = (bf16[128,2048]{1,0:T(8,128)(2,1)}, bf16[2,64,1792]{2,1,0:T(8,128)(2,1)S(1)}, bf16[2,64,1792]{2,1,0:T(8,128)(2,1)S(1)}, s32[8]{0:T(128)}) custom-call(bf16[64,2048]{1,0:T(8,128)(2,1)S(1)} %get-tuple-element.45.refs_0_, bf16[96,2048]{1,0:T(8,128)(2,1)S(1)} %collective-permute-done.14.refs_1_, bf16[2048,1792]{1,0:T(8,128)(2,1)} %refs_2_.3, ...), custom_call_target="tpu_custom_call" | custom-call | flops 1 | bytes 1 | tf_op jit(solution)/shard_map/pallas_call | solution.py:111
  47.4 0.1 collective-permute-start.15
  47.5 0.2 shard_map.114
  47.7 0.5 collective-permute-start.6
  48.2 1.1 %collective-permute-done.15.second_ref = bf16[2,64,1792]{2,1,0:T(8,128)(2,1)S(1)} collective-permute-done((bf16[2,64,1792]{2,1,0:T(8,128)(2,1)S(1)}, bf16[2,64,1792]{2,1,0:T(8,128)(2,1)S(1)}, u32[]{:S(2)}, u32[]{:S(2)}) %collective-permute-start.15) | collective-permute-done | bytes 458784 | tf_op jit(solution)/shard_map/ppermute | solution.py:355
  49.3 0.1 shard_map.120
  49.4 0.6 collective-permute-start.16
  50.0 4.6 %shard_map.115 = (bf16[32,2048]{1,0:T(8,128)(2,1)S(1)}, bf16[32,2048]{1,0:T(8,128)(2,1)S(1)}, bf16[32,2048]{1,0:T(8,128)(2,1)S(1)}, bf16[32,2048]{1,0:T(8,128)(2,1)S(1)}, s32[8]{0:T(128)S(1)}) custom-call(bf16[64,1792]{1,0:T(8,128)(2,1)S(1)} %get-tuple-element.50.mine_ref.refs_1_, bf16[64,1792]{1,0:T(8,128)(2,1)S(1)} %collective-permute-done.6.theirs_ref.refs_2_, ...), custom_call_target="tpu_custom_call" | custom-call | flops 1 | bytes 1 | tf_op jit(solution)/shard_map/pallas_call | solution.py:166
  54.6 4.9 %shard_map.117 = (bf16[256,2048]{1,0:T(8,128)(2,1)}, bf16[2,64,1792]{2,1,0:T(8,128)(2,1)S(1)}, bf16[2,64,1792]{2,1,0:T(8,128)(2,1)S(1)}, s32[8]{0:T(128)}) custom-call(bf16[128,2048]{1,0:T(8,128)(2,1)S(1)} %get-tuple-element.56.refs_0_, bf16[128,2048]{1,0:T(8,128)(2,1)S(1)} %collective-permute-done.13.refs_1_, bf16[2048,1792]{1,0:T(8,128)(2,1)} %w_ref.3, ...), custom_call_target="tpu_custom_call" | custom-call | flops 1 | bytes 1 | tf_op jit(solution)/shard_map/pallas_call | solution.py:111
  59.4 0.1 collective-permute-start.22
  59.5 2.5 %collective-permute-done.16.refs_1_.refs_3_ = bf16[2,64,1792]{2,1,0:T(8,128)(2,1)S(1)} collective-permute-done((bf16[2,64,1792]{2,1,0:T(8,128)(2,1)S(1)}, bf16[2,64,1792]{2,1,0:T(8,128)(2,1)S(1)}, u32[]{:S(2)}, u32[]{:S(2)}) %collective-permute-start.16) | collective-permute-done | bytes 458784 | tf_op jit(solution)/shard_map/ppermute | solution.py:355
  62.0 0.2 shard_map.121
  62.2 0.1 shard_map.125
  62.3 0.7 collective-permute-start.23
  63.0 3.2 %collective-permute-start.7 = (bf16[32,2048]{1,0:T(8,128)(2,1)S(1)}, bf16[32,2048]{1,0:T(8,128)(2,1)S(1)}, u32[]{:S(2)}, u32[]{:S(2)}) collective-permute-start(bf16[32,2048]{1,0:T(8,128)(2,1)S(1)} %get-tuple-element.52), channel_id=1, source_target_pairs={{0,2},{1,3},{2,0},{3,1},{4,6},{5,7},{6,4},{7,5},{8,10},{9,11},{10,... | collective-permute-start | bytes 393224 | tf_op jit(solution)/shard_map/ppermute | solution.py:355
  66.2 2.4 %collective-permute-start.9 = (bf16[32,2048]{1,0:T(8,128)(2,1)S(1)}, bf16[32,2048]{1,0:T(8,128)(2,1)S(1)}, u32[]{:S(2)}, u32[]{:S(2)}) collective-permute-start(bf16[32,2048]{1,0:T(8,128)(2,1)S(1)} %get-tuple-element.54), channel_id=1, source_target_pairs={{0,6},{1,7},{2,4},{3,5},{4,2},{5,3},{6,0},{7,1},{8,14},{9,15},{10,... | collective-permute-start | bytes 393224 | tf_op jit(solution)/shard_map/ppermute | solution.py:355
  68.5 4.6 %shard_map.122 = (bf16[32,2048]{1,0:T(8,128)(2,1)S(1)}, bf16[32,2048]{1,0:T(8,128)(2,1)S(1)}, bf16[32,2048]{1,0:T(8,128)(2,1)S(1)}, bf16[32,2048]{1,0:T(8,128)(2,1)S(1)}, s32[8]{0:T(128)S(1)}) custom-call(bf16[64,1792]{1,0:T(8,128)(2,1)S(1)} %get-tuple-element.66.mine_ref.refs_3_, bf16[64,1792]{1,0:T(8,128)(2,1)S(1)} %collective-permute-done.17.theirs_ref.refs_4_, ...), custom_call_target="tpu_custom_call" | custom-call | flops 1 | bytes 1 | tf_op jit(solution)/shard_map/pallas_call | solution.py:166
  73.1 7.0 %shard_map.123 = (f32[2048,1792]{1,0:T(8,128)}, s32[8]{0:T(128)S(1)}) custom-call(bf16[256,2048]{1,0:T(8,128)(2,1)} %get-tuple-element.58.refs_0_, bf16[64,1792]{1,0:T(8,128)(2,1)S(1)} %get-tuple-element.50.mine_ref.refs_1_, bf16[64,1792]{1,0:T(8,128)(2,1)S(1)} %collective-permute-done.6.theirs_ref.refs_2_, ...), custom_call_target="tpu_custom_call" | custom-call | flops 1 | bytes 1 | tf_op jit(solution)/shard_map/pallas_call | solution.py:327
  80.1 0.1 shard_map.124
  80.2 0.7 shard_map.126
  80.9 0.1 collective-permute-start.24
  81.0 1.6 %collective-permute-start.18 = (bf16[32,2048]{1,0:T(8,128)(2,1)S(1)}, bf16[32,2048]{1,0:T(8,128)(2,1)S(1)}, u32[]{:S(2)}, u32[]{:S(2)}) collective-permute-start(bf16[32,2048]{1,0:T(8,128)(2,1)S(1)} %get-tuple-element.70), channel_id=1, source_target_pairs={{0,1},{1,0},{2,3},{3,2},{4,5},{5,4},{6,7},{7,6},{8,9},{9,8},{10,11... | collective-permute-start | bytes 393224 | tf_op jit(solution)/shard_map/ppermute | solution.py:355
  82.5 1.6 %collective-permute-start.19 = (bf16[32,2048]{1,0:T(8,128)(2,1)S(1)}, bf16[32,2048]{1,0:T(8,128)(2,1)S(1)}, u32[]{:S(2)}, u32[]{:S(2)}) collective-permute-start(bf16[32,2048]{1,0:T(8,128)(2,1)S(1)} %get-tuple-element.71), channel_id=1, source_target_pairs={{0,3},{1,2},{2,1},{3,0},{4,7},{5,6},{6,5},{7,4},{8,11},{9,10},{10,... | collective-permute-start | bytes 393224 | tf_op jit(solution)/shard_map/ppermute | solution.py:355
  84.1 1.4 %collective-permute-start.20 = (bf16[32,2048]{1,0:T(8,128)(2,1)S(1)}, bf16[32,2048]{1,0:T(8,128)(2,1)S(1)}, u32[]{:S(2)}, u32[]{:S(2)}) collective-permute-start(bf16[32,2048]{1,0:T(8,128)(2,1)S(1)} %get-tuple-element.72), channel_id=1, source_target_pairs={{0,5},{1,4},{2,7},{3,6},{4,1},{5,0},{6,3},{7,2},{8,13},{9,12},{10,... | collective-permute-start | bytes 393224 | tf_op jit(solution)/shard_map/ppermute | solution.py:355
  85.5 2.3 %collective-permute-start.21 = (bf16[32,2048]{1,0:T(8,128)(2,1)S(1)}, bf16[32,2048]{1,0:T(8,128)(2,1)S(1)}, u32[]{:S(2)}, u32[]{:S(2)}) collective-permute-start(bf16[32,2048]{1,0:T(8,128)(2,1)S(1)} %get-tuple-element.73), channel_id=1, source_target_pairs={{0,7},{1,6},{2,5},{3,4},{4,3},{5,2},{6,1},{7,0},{8,15},{9,14},{10,... | collective-permute-start | bytes 393224 | tf_op jit(solution)/shard_map/ppermute | solution.py:355
  87.8 0.1 slice_bitcast_fusion.1
  87.9 0.1 slice_bitcast_fusion
  87.9 11.4 %shard_map.127 = (f32[2048,1792]{1,0:T(8,128)}, f32[2048,1792]{1,0:T(8,128)}, s32[8]{0:T(128)S(1)}) custom-call(bf16[128,2048]{1,0:T(8,128)(2,1)} %get-tuple-element.74.refs_0_, bf16[128,2048]{1,0:T(8,128)(2,1)} %get-tuple-element.75.refs_1_, bf16[64,1792]{1,0:T(8,128)(2,1)S(1)} %get-tuple-element.93.refs_2_, ...), custom_call_target="tpu_custom_call" | custom-call | flops 3758096384 | bytes 29360128 | tf_op jit(solution)/shard_map/pallas_call | solution.py:327
  99.4 0.7 shard_map.128
  (26 shorter events, 0.2 us)
Async XLA Ops:
  0.6 28.3 %copy-start = (bf16[32,2048]{1,0:T(8,128)(2,1)S(1)}, bf16[32,2048]{1,0:T(8,128)(2,1)}, u32[]{:S(2)}) copy-start(bf16[32,2048]{1,0:T(8,128)(2,1)} %refs_0_.3) | copy-start | bytes 393220
  0.6 7.2 %collective-permute-start = (bf16[32,2048]{1,0:T(8,128)(2,1)}, bf16[32,2048]{1,0:T(8,128)(2,1)S(1)}, u32[]{:S(2)}, u32[]{:S(2)}) collective-permute-start(bf16[32,2048]{1,0:T(8,128)(2,1)} %refs_0_.2), channel_id=1, source_target_pairs={{0,1},{1,0},{2,3},{3,2},{4,5},{5,4},{6,7},{7,6},{8,9},{9,8},{10,11... | collective-permute-start | bytes 393224 | tf_op jit(solution)/shard_map/ppermute | solution.py:355
  3.6 5.2 %collective-permute-start.1 = (bf16[32,2048]{1,0:T(8,128)(2,1)}, bf16[32,2048]{1,0:T(8,128)(2,1)S(1)}, u32[]{:S(2)}, u32[]{:S(2)}) collective-permute-start(bf16[32,2048]{1,0:T(8,128)(2,1)} %refs_0_.2), channel_id=1, source_target_pairs={{0,2},{1,3},{2,0},{3,1},{4,6},{5,7},{6,4},{7,5},{8,10},{9,11},{10,... | collective-permute-start | bytes 393224 | tf_op jit(solution)/shard_map/ppermute | solution.py:355
  5.2 9.8 %collective-permute-start.3 = (bf16[32,2048]{1,0:T(8,128)(2,1)}, bf16[32,2048]{1,0:T(8,128)(2,1)S(1)}, u32[]{:S(2)}, u32[]{:S(2)}) collective-permute-start(bf16[32,2048]{1,0:T(8,128)(2,1)} %refs_0_.2), channel_id=1, source_target_pairs={{0,6},{1,7},{2,4},{3,5},{4,2},{5,3},{6,0},{7,1},{8,14},{9,15},{10,... | collective-permute-start | bytes 393224 | tf_op jit(solution)/shard_map/ppermute | solution.py:355
  7.7 11.7 %collective-permute-start.2 = (bf16[32,2048]{1,0:T(8,128)(2,1)}, bf16[32,2048]{1,0:T(8,128)(2,1)S(1)}, u32[]{:S(2)}, u32[]{:S(2)}) collective-permute-start(bf16[32,2048]{1,0:T(8,128)(2,1)} %refs_0_.2), channel_id=1, source_target_pairs={{0,4},{1,5},{2,6},{3,7},{4,0},{5,1},{6,2},{7,3},{8,12},{9,13},{10,... | collective-permute-start | bytes 393224 | tf_op jit(solution)/shard_map/ppermute | solution.py:355
  7.8 0.9 copy-start.1
  25.3 1.9 %collective-permute-start.4 = (bf16[2,64,1792]{2,1,0:T(8,128)(2,1)S(1)}, bf16[2,64,1792]{2,1,0:T(8,128)(2,1)S(1)}, u32[]{:S(2)}, u32[]{:S(2)}) collective-permute-start(bf16[2,64,1792]{2,1,0:T(8,128)(2,1)S(1)} %get-tuple-element.48), channel_id=1, source_target_pairs={{0,8},{8,0},{16,24},{24,16},{1,9},{9,1},{17,25},{25,17},{2,10},{10... | collective-permute-start | bytes 1376264 | tf_op jit(solution)/shard_map/ppermute | solution.py:355
  25.4 16.1 %collective-permute-start.14 = (bf16[96,2048]{1,0:T(8,128)(2,1)S(1)}, bf16[96,2048]{1,0:T(8,128)(2,1)S(1)}, u32[]{:S(2)}, u32[]{:S(2)}) collective-permute-start(bf16[96,2048]{1,0:T(8,128)(2,1)S(1)} %get-tuple-element.60), channel_id=1, source_target_pairs={{0,1},{1,0},{2,3},{3,2},{4,5},{5,4},{6,7},{7,6},{8,9},{9,8},{10,11... | collective-permute-start | bytes 1179656 | tf_op jit(solution)/shard_map/ppermute | solution.py:355
  27.3 20.2 %collective-permute-start.5 = (bf16[2,64,1792]{2,1,0:T(8,128)(2,1)S(1)}, bf16[2,64,1792]{2,1,0:T(8,128)(2,1)S(1)}, u32[]{:S(2)}, u32[]{:S(2)}) collective-permute-start(bf16[2,64,1792]{2,1,0:T(8,128)(2,1)S(1)} %get-tuple-element.49.refs_0_), channel_id=1, source_target_pairs={{0,16},{8,24},{16,0},{24,8},{1,17},{9,25},{17,1},{25,9},{2,18},{10... | collective-permute-start | bytes 1376264 | tf_op jit(solution)/shard_map/ppermute | solution.py:355
  28.9 9.9 %collective-permute-start.11 = (bf16[32,2048]{1,0:T(8,128)(2,1)S(1)}, bf16[32,2048]{1,0:T(8,128)(2,1)S(1)}, u32[]{:S(2)}, u32[]{:S(2)}) collective-permute-start(bf16[32,2048]{1,0:T(8,128)(2,1)S(1)} %copy-done), channel_id=1, source_target_pairs={{0,4},{1,5},{2,6},{3,7},{4,0},{5,1},{6,2},{7,3},{8,12},{9,13},{10,... | collective-permute-start | bytes 393224 | tf_op jit(solution)/shard_map/ppermute | solution.py:355
  29.1 11.8 %collective-permute-start.10 = (bf16[32,2048]{1,0:T(8,128)(2,1)S(1)}, bf16[32,2048]{1,0:T(8,128)(2,1)S(1)}, u32[]{:S(2)}, u32[]{:S(2)}) collective-permute-start(bf16[32,2048]{1,0:T(8,128)(2,1)S(1)} %copy-done), channel_id=1, source_target_pairs={{0,2},{1,3},{2,0},{3,1},{4,6},{5,7},{6,4},{7,5},{8,10},{9,11},{10,... | collective-permute-start | bytes 393224 | tf_op jit(solution)/shard_map/ppermute | solution.py:355
  32.1 8.8 %collective-permute-start.12 = (bf16[32,2048]{1,0:T(8,128)(2,1)S(1)}, bf16[32,2048]{1,0:T(8,128)(2,1)S(1)}, u32[]{:S(2)}, u32[]{:S(2)}) collective-permute-start(bf16[32,2048]{1,0:T(8,128)(2,1)S(1)} %copy-done), channel_id=1, source_target_pairs={{0,6},{1,7},{2,4},{3,5},{4,2},{5,3},{6,0},{7,1},{8,14},{9,15},{10,... | collective-permute-start | bytes 393224 | tf_op jit(solution)/shard_map/ppermute | solution.py:355
  40.9 13.6 %collective-permute-start.13 = (bf16[128,2048]{1,0:T(8,128)(2,1)S(1)}, bf16[128,2048]{1,0:T(8,128)(2,1)S(1)}, u32[]{:S(2)}, u32[]{:S(2)}) collective-permute-start(bf16[128,2048]{1,0:T(8,128)(2,1)S(1)} %get-tuple-element.56.refs_0_), channel_id=1, source_target_pairs={{0,1},{1,0},{2,3},{3,2},{4,5},{5,4},{6,7},{7,6},{8,9},{9,8},{10,11... | collective-permute-start | bytes 1572872 | tf_op jit(solution)/shard_map/ppermute | solution.py:355
  47.4 1.9 %collective-permute-start.15 = (bf16[2,64,1792]{2,1,0:T(8,128)(2,1)S(1)}, bf16[2,64,1792]{2,1,0:T(8,128)(2,1)S(1)}, u32[]{:S(2)}, u32[]{:S(2)}) collective-permute-start(bf16[2,64,1792]{2,1,0:T(8,128)(2,1)S(1)} %get-tuple-element.63), channel_id=1, source_target_pairs={{0,8},{8,0},{16,24},{24,16},{1,9},{9,1},{17,25},{25,17},{2,10},{10... | collective-permute-start | bytes 1376264 | tf_op jit(solution)/shard_map/ppermute | solution.py:355
  47.7 2.3 %collective-permute-start.6 = (bf16[64,1792]{1,0:T(8,128)(2,1)S(1)}, bf16[64,1792]{1,0:T(8,128)(2,1)S(1)}, u32[]{:S(2)}, u32[]{:S(2)}) collective-permute-start(bf16[64,1792]{1,0:T(8,128)(2,1)S(1)} %get-tuple-element.50.mine_ref.refs_1_), channel_id=1, source_target_pairs={{0,8},{8,0},{16,24},{24,16},{1,9},{9,1},{17,25},{25,17},{2,10},{10... | collective-permute-start | bytes 688136 | tf_op jit(solution)/shard_map/ppermute | solution.py:355
  49.4 12.6 %collective-permute-start.16 = (bf16[2,64,1792]{2,1,0:T(8,128)(2,1)S(1)}, bf16[2,64,1792]{2,1,0:T(8,128)(2,1)S(1)}, u32[]{:S(2)}, u32[]{:S(2)}) collective-permute-start(bf16[2,64,1792]{2,1,0:T(8,128)(2,1)S(1)} %get-tuple-element.65.refs_0_.refs_2_), channel_id=1, source_target_pairs={{0,16},{8,24},{16,0},{24,8},{1,17},{9,25},{17,1},{25,9},{2,18},{10... | collective-permute-start | bytes 1376264 | tf_op jit(solution)/shard_map/ppermute | solution.py:355
  59.4 2.8 %collective-permute-start.22 = (bf16[2,64,1792]{2,1,0:T(8,128)(2,1)S(1)}, bf16[2,64,1792]{2,1,0:T(8,128)(2,1)S(1)}, u32[]{:S(2)}, u32[]{:S(2)}) collective-permute-start(bf16[2,64,1792]{2,1,0:T(8,128)(2,1)S(1)} %get-tuple-element.77), channel_id=1, source_target_pairs={{0,8},{8,0},{16,24},{24,16},{1,9},{9,1},{17,25},{25,17},{2,10},{10... | collective-permute-start | bytes 1376264 | tf_op jit(solution)/shard_map/ppermute | solution.py:355
  62.3 17.9 %collective-permute-start.23 = (bf16[2,64,1792]{2,1,0:T(8,128)(2,1)S(1)}, bf16[2,64,1792]{2,1,0:T(8,128)(2,1)S(1)}, u32[]{:S(2)}, u32[]{:S(2)}) collective-permute-start(bf16[2,64,1792]{2,1,0:T(8,128)(2,1)S(1)} %get-tuple-element.79.refs_4_), channel_id=1, source_target_pairs={{0,16},{8,24},{16,0},{24,8},{1,17},{9,25},{17,1},{25,9},{2,18},{10... | collective-permute-start | bytes 1376264 | tf_op jit(solution)/shard_map/ppermute | solution.py:355
  63.0 5.5 %collective-permute-start.17 = (bf16[64,1792]{1,0:T(8,128)(2,1)S(1)}, bf16[64,1792]{1,0:T(8,128)(2,1)S(1)}, u32[]{:S(2)}, u32[]{:S(2)}) collective-permute-start(bf16[64,1792]{1,0:T(8,128)(2,1)S(1)} %get-tuple-element.66.mine_ref.refs_3_), channel_id=1, source_target_pairs={{0,8},{8,0},{16,24},{24,16},{1,9},{9,1},{17,25},{25,17},{2,10},{10... | collective-permute-start | bytes 688136 | tf_op jit(solution)/shard_map/ppermute | solution.py:355
  63.0 17.1 %collective-permute-start.7 = (bf16[32,2048]{1,0:T(8,128)(2,1)S(1)}, bf16[32,2048]{1,0:T(8,128)(2,1)S(1)}, u32[]{:S(2)}, u32[]{:S(2)}) collective-permute-start(bf16[32,2048]{1,0:T(8,128)(2,1)S(1)} %get-tuple-element.52), channel_id=1, source_target_pairs={{0,2},{1,3},{2,0},{3,1},{4,6},{5,7},{6,4},{7,5},{8,10},{9,11},{10,... | collective-permute-start | bytes 393224 | tf_op jit(solution)/shard_map/ppermute | solution.py:355
  66.2 14.0 %collective-permute-start.8 = (bf16[32,2048]{1,0:T(8,128)(2,1)S(1)}, bf16[32,2048]{1,0:T(8,128)(2,1)S(1)}, u32[]{:S(2)}, u32[]{:S(2)}) collective-permute-start(bf16[32,2048]{1,0:T(8,128)(2,1)S(1)} %get-tuple-element.53), channel_id=1, source_target_pairs={{0,4},{1,5},{2,6},{3,7},{4,0},{5,1},{6,2},{7,3},{8,12},{9,13},{10,... | collective-permute-start | bytes 393224 | tf_op jit(solution)/shard_map/ppermute | solution.py:355
  66.2 14.0 %collective-permute-start.9 = (bf16[32,2048]{1,0:T(8,128)(2,1)S(1)}, bf16[32,2048]{1,0:T(8,128)(2,1)S(1)}, u32[]{:S(2)}, u32[]{:S(2)}) collective-permute-start(bf16[32,2048]{1,0:T(8,128)(2,1)S(1)} %get-tuple-element.54), channel_id=1, source_target_pairs={{0,6},{1,7},{2,4},{3,5},{4,2},{5,3},{6,0},{7,1},{8,14},{9,15},{10,... | collective-permute-start | bytes 393224 | tf_op jit(solution)/shard_map/ppermute | solution.py:355
  80.9 7.0 %collective-permute-start.24 = (bf16[2,2,64,1792]{3,2,1,0:T(8,128)(2,1)S(1)}, bf16[2,2,64,1792]{3,2,1,0:T(8,128)(2,1)S(1)}, u32[]{:S(2)}, u32[]{:S(2)}) collective-permute-start(bf16[2,2,64,1792]{3,2,1,0:T(8,128)(2,1)S(1)} %shard_map.126), channel_id=1, source_target_pairs={{0,8},{8,0},{16,24},{24,16},{1,9},{9,1},{17,25},{25,17},{2,10},{10... | collective-permute-start | bytes 2752520 | tf_op jit(solution)/shard_map/ppermute | solution.py:355
  81.0 18.4 %collective-permute-start.18 = (bf16[32,2048]{1,0:T(8,128)(2,1)S(1)}, bf16[32,2048]{1,0:T(8,128)(2,1)S(1)}, u32[]{:S(2)}, u32[]{:S(2)}) collective-permute-start(bf16[32,2048]{1,0:T(8,128)(2,1)S(1)} %get-tuple-element.70), channel_id=1, source_target_pairs={{0,1},{1,0},{2,3},{3,2},{4,5},{5,4},{6,7},{7,6},{8,9},{9,8},{10,11... | collective-permute-start | bytes 393224 | tf_op jit(solution)/shard_map/ppermute | solution.py:355
  82.5 16.8 %collective-permute-start.19 = (bf16[32,2048]{1,0:T(8,128)(2,1)S(1)}, bf16[32,2048]{1,0:T(8,128)(2,1)S(1)}, u32[]{:S(2)}, u32[]{:S(2)}) collective-permute-start(bf16[32,2048]{1,0:T(8,128)(2,1)S(1)} %get-tuple-element.71), channel_id=1, source_target_pairs={{0,3},{1,2},{2,1},{3,0},{4,7},{5,6},{6,5},{7,4},{8,11},{9,10},{10,... | collective-permute-start | bytes 393224 | tf_op jit(solution)/shard_map/ppermute | solution.py:355
  84.1 15.3 %collective-permute-start.20 = (bf16[32,2048]{1,0:T(8,128)(2,1)S(1)}, bf16[32,2048]{1,0:T(8,128)(2,1)S(1)}, u32[]{:S(2)}, u32[]{:S(2)}) collective-permute-start(bf16[32,2048]{1,0:T(8,128)(2,1)S(1)} %get-tuple-element.72), channel_id=1, source_target_pairs={{0,5},{1,4},{2,7},{3,6},{4,1},{5,0},{6,3},{7,2},{8,13},{9,12},{10,... | collective-permute-start | bytes 393224 | tf_op jit(solution)/shard_map/ppermute | solution.py:355
  85.5 13.9 %collective-permute-start.21 = (bf16[32,2048]{1,0:T(8,128)(2,1)S(1)}, bf16[32,2048]{1,0:T(8,128)(2,1)S(1)}, u32[]{:S(2)}, u32[]{:S(2)}) collective-permute-start(bf16[32,2048]{1,0:T(8,128)(2,1)S(1)} %get-tuple-element.73), channel_id=1, source_target_pairs={{0,7},{1,6},{2,5},{3,4},{4,3},{5,2},{6,1},{7,0},{8,15},{9,14},{10,... | collective-permute-start | bytes 393224 | tf_op jit(solution)/shard_map/ppermute | solution.py:355

commit v4 on v3

--- a/solution.py
+++ b/solution.py
@@ -386,8 +386,8 @@
     evens = [tokens] + [swap(tokens, "col", 2 * k) for k in range(1, n_k)]
     own, swapped = join([tokens, swap(tokens, "col", 1)])
     panel, mine, theirs, token = panel_matmul(
-        [(k, 0, *places(0, k)) for k in range(n_k)],
-        [own, *evens[1:]],
+        [(n_k - k if k else 0, 0, *places(0, k)) for k in range(n_k)],
+        [own, *evens[:0:-1]],
         [w_gate, w_up],
         [mask_gate, mask_up],
         rows,

time: 101 us -> 99.2 us (0.982)
  waiting for transfers between devices: 23.1 us -> 21.6 us
    ppermute x25, waiting for transfers between devices: 23.1 us -> 21.6 us  [swap(): return lax.ppermute(value, axis, [(i, i ^ bits) for i in range(size)])]
  transfers between devices with their start and end apart: 25 -> 25, of which waited for: 7 -> 8; matrix products, arithmetic and copies ran while one was open for 0% -> 0% of each run, Pallas kernels for 39% -> 39%
where the time goes in v4:
time: 99.2 us; the launch traced here: 98.9 us
  Pallas kernels  46.3 us (47%)
  starting transfers between devices  29 us (29%)
  waiting for transfers between devices  21.6 us (22%)
  local copies, waits for them, and re-layouts  1.06 us (1%)
    ppermute x25, starting transfers between devices, swap(): return lax.ppermute(value, axis, [(i, i ^ bits) for i in range(size)])  29 us
    ppermute x25, waiting for transfers between devices, swap(): return lax.ppermute(value, axis, [(i, i ^ bits) for i in range(size)])  21.6 us
    pallas_call x2, Pallas kernels, weight_grads(): pl.pallas_call(kernel, in_specs=[pl.BlockSpec(memory_space=pl.ANY)] * n_p...  18.4 us
    pallas_call x3, Pallas kernels, panel_matmul(): pl.pallas_call(kernel, in_specs=[whole_vmem()] * n_a + [pl.BlockSpec(memo...  16.6 us
    pallas_call x2, Pallas kernels, output_matmul(): pl.pallas_call(kernel, in_specs=[whole_vmem()] * 2 + [pl.BlockSpec(memory...  9.12 us
  transfers between devices with their start and end apart: 25, of which 8 were waited for; matrix products, arithmetic and copies ran while one was open for 0% of the time, Pallas kernels for 39%

profile of v4, /device:TPU:0, one launch (start us, length us, event | category | flops | bytes accessed | tf_op | source)
XLA Modules:
  0.0 98.9 jit_solution(1900164568965491856)
XLA Ops:
  0.6 3.0 %collective-permute-start = (bf16[32,2048]{1,0:T(8,128)(2,1)}, bf16[32,2048]{1,0:T(8,128)(2,1)S(1)}, u32[]{:S(2)}, u32[]{:S(2)}) collective-permute-start(bf16[32,2048]{1,0:T(8,128)(2,1)} %refs_0_.2), channel_id=1, source_target_pairs={{0,1},{1,0},{2,3},{3,2},{4,5},{5,4},{6,7},{7,6},{8,9},{9,8},{10,11... | collective-permute-start | bytes 393224 | tf_op jit(solution)/shard_map/ppermute | solution.py:355
  3.6 3.6 %collective-permute-start.1 = (bf16[32,2048]{1,0:T(8,128)(2,1)}, bf16[32,2048]{1,0:T(8,128)(2,1)S(1)}, u32[]{:S(2)}, u32[]{:S(2)}) collective-permute-start(bf16[32,2048]{1,0:T(8,128)(2,1)} %refs_0_.2), channel_id=1, source_target_pairs={{0,6},{1,7},{2,4},{3,5},{4,2},{5,3},{6,0},{7,1},{8,14},{9,15},{10,... | collective-permute-start | bytes 393224 | tf_op jit(solution)/shard_map/ppermute | solution.py:355
  7.2 0.8 collective-permute-start.2
  8.0 0.9 copy-done.1
  9.0 3.1 %collective-permute-done.1.refs_1_.refs_2_ = bf16[32,2048]{1,0:T(8,128)(2,1)S(1)} collective-permute-done((bf16[32,2048]{1,0:T(8,128)(2,1)}, bf16[32,2048]{1,0:T(8,128)(2,1)S(1)}, u32[]{:S(2)}, u32[]{:S(2)}) %collective-permute-start.1) | collective-permute-done | bytes 131104 | tf_op jit(solution)/shard_map/ppermute | solution.py:355
  12.1 2.4 %collective-permute-done.3.refs_3_.refs_0_ = bf16[32,2048]{1,0:T(8,128)(2,1)S(1)} collective-permute-done((bf16[32,2048]{1,0:T(8,128)(2,1)}, bf16[32,2048]{1,0:T(8,128)(2,1)S(1)}, u32[]{:S(2)}, u32[]{:S(2)}) %collective-permute-start.3) | collective-permute-done | bytes 131104 | tf_op jit(solution)/shard_map/ppermute | solution.py:355
  14.5 3.8 %collective-permute-done.2.refs_2_.refs_1_ = bf16[32,2048]{1,0:T(8,128)(2,1)S(1)} collective-permute-done((bf16[32,2048]{1,0:T(8,128)(2,1)}, bf16[32,2048]{1,0:T(8,128)(2,1)S(1)}, u32[]{:S(2)}, u32[]{:S(2)}) %collective-permute-start.2) | collective-permute-done | bytes 131104 | tf_op jit(solution)/shard_map/ppermute | solution.py:355
  18.3 5.9 %shard_map.112 = (bf16[128,2048]{1,0:T(8,128)(2,1)}, bf16[2,64,1792]{2,1,0:T(8,128)(2,1)S(1)}, bf16[2,64,1792]{2,1,0:T(8,128)(2,1)S(1)}, s32[8]{0:T(128)S(1)}) custom-call(bf16[64,2048]{1,0:T(8,128)(2,1)S(1)} %get-tuple-element.45.refs_0_, bf16[32,2048]{1,0:T(8,128)(2,1)S(1)} %collective-permute-done.1.refs_1_.refs_2_, ...), custom_call_target="tpu_custom_call" | custom-call | flops 1 | bytes 1 | tf_op jit(solution)/shard_map/pallas_call | solution.py:111
  24.1 0.1 collective-permute-start.4
  24.3 0.6 collective-permute-start.14
  24.9 1.2 %collective-permute-done.4.second_ref = bf16[2,64,1792]{2,1,0:T(8,128)(2,1)S(1)} collective-permute-done((bf16[2,64,1792]{2,1,0:T(8,128)(2,1)S(1)}, bf16[2,64,1792]{2,1,0:T(8,128)(2,1)S(1)}, u32[]{:S(2)}, u32[]{:S(2)}) %collective-permute-start.4) | collective-permute-done | bytes 458784 | tf_op jit(solution)/shard_map/ppermute | solution.py:355
  26.0 0.1 shard_map.113
  26.1 1.6 %collective-permute-start.5 = (bf16[2,64,1792]{2,1,0:T(8,128)(2,1)S(1)}, bf16[2,64,1792]{2,1,0:T(8,128)(2,1)S(1)}, u32[]{:S(2)}, u32[]{:S(2)}) collective-permute-start(bf16[2,64,1792]{2,1,0:T(8,128)(2,1)S(1)} %get-tuple-element.49.refs_0_), channel_id=1, source_target_pairs={{0,16},{8,24},{16,0},{24,8},{1,17},{9,25},{17,1},{25,9},{2,18},{10... | collective-permute-start | bytes 1376264 | tf_op jit(solution)/shard_map/ppermute | solution.py:355
  27.7 0.7 collective-permute-start.11
  28.4 2.3 %collective-permute-start.10 = (bf16[32,2048]{1,0:T(8,128)(2,1)S(1)}, bf16[32,2048]{1,0:T(8,128)(2,1)S(1)}, u32[]{:S(2)}, u32[]{:S(2)}) collective-permute-start(bf16[32,2048]{1,0:T(8,128)(2,1)S(1)} %copy-done), channel_id=1, source_target_pairs={{0,2},{1,3},{2,0},{3,1},{4,6},{5,7},{6,4},{7,5},{8,10},{9,11},{10,... | collective-permute-start | bytes 393224 | tf_op jit(solution)/shard_map/ppermute | solution.py:355
  30.8 1.3 %collective-permute-start.12 = (bf16[32,2048]{1,0:T(8,128)(2,1)S(1)}, bf16[32,2048]{1,0:T(8,128)(2,1)S(1)}, u32[]{:S(2)}, u32[]{:S(2)}) collective-permute-start(bf16[32,2048]{1,0:T(8,128)(2,1)S(1)} %copy-done), channel_id=1, source_target_pairs={{0,6},{1,7},{2,4},{3,5},{4,2},{5,3},{6,0},{7,1},{8,14},{9,15},{10,... | collective-permute-start | bytes 393224 | tf_op jit(solution)/shard_map/ppermute | solution.py:355
  32.1 5.4 %collective-permute-done.11.refs_2_ = bf16[32,2048]{1,0:T(8,128)(2,1)S(1)} collective-permute-done((bf16[32,2048]{1,0:T(8,128)(2,1)S(1)}, bf16[32,2048]{1,0:T(8,128)(2,1)S(1)}, u32[]{:S(2)}, u32[]{:S(2)}) %collective-permute-start.11) | collective-permute-done | bytes 131104 | tf_op jit(solution)/shard_map/ppermute | solution.py:355
  37.5 2.1 %collective-permute-done.10.refs_1_ = bf16[32,2048]{1,0:T(8,128)(2,1)S(1)} collective-permute-done((bf16[32,2048]{1,0:T(8,128)(2,1)S(1)}, bf16[32,2048]{1,0:T(8,128)(2,1)S(1)}, u32[]{:S(2)}, u32[]{:S(2)}) %collective-permute-start.10) | collective-permute-done | bytes 131104 | tf_op jit(solution)/shard_map/ppermute | solution.py:355
  39.7 0.6 collective-permute-start.13
  40.3 5.9 %shard_map.119 = (bf16[128,2048]{1,0:T(8,128)(2,1)}, bf16[2,64,1792]{2,1,0:T(8,128)(2,1)S(1)}, bf16[2,64,1792]{2,1,0:T(8,128)(2,1)S(1)}, s32[8]{0:T(128)}) custom-call(bf16[64,2048]{1,0:T(8,128)(2,1)S(1)} %get-tuple-element.45.refs_0_, bf16[96,2048]{1,0:T(8,128)(2,1)S(1)} %collective-permute-done.14.refs_1_, bf16[2048,1792]{1,0:T(8,128)(2,1)} %refs_2_.3, ...), custom_call_target="tpu_custom_call" | custom-call | flops 1 | bytes 1 | tf_op jit(solution)/shard_map/pallas_call | solution.py:111
  46.2 0.1 collective-permute-start.15
  46.2 0.2 shard_map.114
  46.4 0.5 collective-permute-start.6
  47.0 1.1 %collective-permute-done.15.second_ref = bf16[2,64,1792]{2,1,0:T(8,128)(2,1)S(1)} collective-permute-done((bf16[2,64,1792]{2,1,0:T(8,128)(2,1)S(1)}, bf16[2,64,1792]{2,1,0:T(8,128)(2,1)S(1)}, u32[]{:S(2)}, u32[]{:S(2)}) %collective-permute-start.15) | collective-permute-done | bytes 458784 | tf_op jit(solution)/shard_map/ppermute | solution.py:355
  48.0 0.1 shard_map.120
  48.1 0.6 collective-permute-start.16
  48.7 4.6 %shard_map.115 = (bf16[32,2048]{1,0:T(8,128)(2,1)S(1)}, bf16[32,2048]{1,0:T(8,128)(2,1)S(1)}, bf16[32,2048]{1,0:T(8,128)(2,1)S(1)}, bf16[32,2048]{1,0:T(8,128)(2,1)S(1)}, s32[8]{0:T(128)S(1)}) custom-call(bf16[64,1792]{1,0:T(8,128)(2,1)S(1)} %get-tuple-element.50.mine_ref.refs_1_, bf16[64,1792]{1,0:T(8,128)(2,1)S(1)} %collective-permute-done.6.theirs_ref.refs_2_, ...), custom_call_target="tpu_custom_call" | custom-call | flops 1 | bytes 1 | tf_op jit(solution)/shard_map/pallas_call | solution.py:166
  53.3 4.9 %shard_map.117 = (bf16[256,2048]{1,0:T(8,128)(2,1)}, bf16[2,64,1792]{2,1,0:T(8,128)(2,1)S(1)}, bf16[2,64,1792]{2,1,0:T(8,128)(2,1)S(1)}, s32[8]{0:T(128)}) custom-call(bf16[128,2048]{1,0:T(8,128)(2,1)S(1)} %get-tuple-element.56.refs_0_, bf16[128,2048]{1,0:T(8,128)(2,1)S(1)} %collective-permute-done.13.refs_1_, bf16[2048,1792]{1,0:T(8,128)(2,1)} %w_ref.3, ...), custom_call_target="tpu_custom_call" | custom-call | flops 1 | bytes 1 | tf_op jit(solution)/shard_map/pallas_call | solution.py:111
  58.2 0.1 collective-permute-start.22
  58.2 2.5 %collective-permute-done.16.refs_1_.refs_3_ = bf16[2,64,1792]{2,1,0:T(8,128)(2,1)S(1)} collective-permute-done((bf16[2,64,1792]{2,1,0:T(8,128)(2,1)S(1)}, bf16[2,64,1792]{2,1,0:T(8,128)(2,1)S(1)}, u32[]{:S(2)}, u32[]{:S(2)}) %collective-permute-start.16) | collective-permute-done | bytes 458784 | tf_op jit(solution)/shard_map/ppermute | solution.py:355
  60.8 0.2 shard_map.121
  61.0 0.1 shard_map.125
  61.1 0.7 collective-permute-start.23
  61.7 3.1 %collective-permute-start.7 = (bf16[32,2048]{1,0:T(8,128)(2,1)S(1)}, bf16[32,2048]{1,0:T(8,128)(2,1)S(1)}, u32[]{:S(2)}, u32[]{:S(2)}) collective-permute-start(bf16[32,2048]{1,0:T(8,128)(2,1)S(1)} %get-tuple-element.52), channel_id=1, source_target_pairs={{0,2},{1,3},{2,0},{3,1},{4,6},{5,7},{6,4},{7,5},{8,10},{9,11},{10,... | collective-permute-start | bytes 393224 | tf_op jit(solution)/shard_map/ppermute | solution.py:355
  64.9 0.3 collective-permute-start.8
  65.2 2.1 %collective-permute-start.9 = (bf16[32,2048]{1,0:T(8,128)(2,1)S(1)}, bf16[32,2048]{1,0:T(8,128)(2,1)S(1)}, u32[]{:S(2)}, u32[]{:S(2)}) collective-permute-start(bf16[32,2048]{1,0:T(8,128)(2,1)S(1)} %get-tuple-element.54), channel_id=1, source_target_pairs={{0,6},{1,7},{2,4},{3,5},{4,2},{5,3},{6,0},{7,1},{8,14},{9,15},{10,... | collective-permute-start | bytes 393224 | tf_op jit(solution)/shard_map/ppermute | solution.py:355
  67.3 4.6 %shard_map.122 = (bf16[32,2048]{1,0:T(8,128)(2,1)S(1)}, bf16[32,2048]{1,0:T(8,128)(2,1)S(1)}, bf16[32,2048]{1,0:T(8,128)(2,1)S(1)}, bf16[32,2048]{1,0:T(8,128)(2,1)S(1)}, s32[8]{0:T(128)S(1)}) custom-call(bf16[64,1792]{1,0:T(8,128)(2,1)S(1)} %get-tuple-element.66.mine_ref.refs_3_, bf16[64,1792]{1,0:T(8,128)(2,1)S(1)} %collective-permute-done.17.theirs_ref.refs_4_, ...), custom_call_target="tpu_custom_call" | custom-call | flops 1 | bytes 1 | tf_op jit(solution)/shard_map/pallas_call | solution.py:166
  71.8 7.0 %shard_map.123 = (f32[2048,1792]{1,0:T(8,128)}, s32[8]{0:T(128)S(1)}) custom-call(bf16[256,2048]{1,0:T(8,128)(2,1)} %get-tuple-element.58.refs_0_, bf16[64,1792]{1,0:T(8,128)(2,1)S(1)} %get-tuple-element.50.mine_ref.refs_1_, bf16[64,1792]{1,0:T(8,128)(2,1)S(1)} %collective-permute-done.6.theirs_ref.refs_2_, ...), custom_call_target="tpu_custom_call" | custom-call | flops 1 | bytes 1 | tf_op jit(solution)/shard_map/pallas_call | solution.py:327
  78.9 0.1 shard_map.124
  78.9 0.7 shard_map.126
  79.6 0.1 collective-permute-start.24
  79.7 1.5 %collective-permute-start.18 = (bf16[32,2048]{1,0:T(8,128)(2,1)S(1)}, bf16[32,2048]{1,0:T(8,128)(2,1)S(1)}, u32[]{:S(2)}, u32[]{:S(2)}) collective-permute-start(bf16[32,2048]{1,0:T(8,128)(2,1)S(1)} %get-tuple-element.70), channel_id=1, source_target_pairs={{0,1},{1,0},{2,3},{3,2},{4,5},{5,4},{6,7},{7,6},{8,9},{9,8},{10,11... | collective-permute-start | bytes 393224 | tf_op jit(solution)/shard_map/ppermute | solution.py:355
  81.2 1.6 %collective-permute-start.19 = (bf16[32,2048]{1,0:T(8,128)(2,1)S(1)}, bf16[32,2048]{1,0:T(8,128)(2,1)S(1)}, u32[]{:S(2)}, u32[]{:S(2)}) collective-permute-start(bf16[32,2048]{1,0:T(8,128)(2,1)S(1)} %get-tuple-element.71), channel_id=1, source_target_pairs={{0,3},{1,2},{2,1},{3,0},{4,7},{5,6},{6,5},{7,4},{8,11},{9,10},{10,... | collective-permute-start | bytes 393224 | tf_op jit(solution)/shard_map/ppermute | solution.py:355
  82.8 1.6 %collective-permute-start.20 = (bf16[32,2048]{1,0:T(8,128)(2,1)S(1)}, bf16[32,2048]{1,0:T(8,128)(2,1)S(1)}, u32[]{:S(2)}, u32[]{:S(2)}) collective-permute-start(bf16[32,2048]{1,0:T(8,128)(2,1)S(1)} %get-tuple-element.72), channel_id=1, source_target_pairs={{0,5},{1,4},{2,7},{3,6},{4,1},{5,0},{6,3},{7,2},{8,13},{9,12},{10,... | collective-permute-start | bytes 393224 | tf_op jit(solution)/shard_map/ppermute | solution.py:355
  84.4 2.1 %collective-permute-start.21 = (bf16[32,2048]{1,0:T(8,128)(2,1)S(1)}, bf16[32,2048]{1,0:T(8,128)(2,1)S(1)}, u32[]{:S(2)}, u32[]{:S(2)}) collective-permute-start(bf16[32,2048]{1,0:T(8,128)(2,1)S(1)} %get-tuple-element.73), channel_id=1, source_target_pairs={{0,7},{1,6},{2,5},{3,4},{4,3},{5,2},{6,1},{7,0},{8,15},{9,14},{10,... | collective-permute-start | bytes 393224 | tf_op jit(solution)/shard_map/ppermute | solution.py:355
  86.6 0.1 slice_bitcast_fusion
  86.6 11.4 %shard_map.127 = (f32[2048,1792]{1,0:T(8,128)}, f32[2048,1792]{1,0:T(8,128)}, s32[8]{0:T(128)S(1)}) custom-call(bf16[128,2048]{1,0:T(8,128)(2,1)} %get-tuple-element.74.refs_0_, bf16[128,2048]{1,0:T(8,128)(2,1)} %get-tuple-element.75.refs_1_, bf16[64,1792]{1,0:T(8,128)(2,1)S(1)} %get-tuple-element.93.refs_2_, ...), custom_call_target="tpu_custom_call" | custom-call | flops 3758096384 | bytes 29360128 | tf_op jit(solution)/shard_map/pallas_call | solution.py:327
  98.1 0.7 shard_map.128
  (26 shorter events, 0.2 us)
Async XLA Ops:
  0.6 27.1 %copy-start = (bf16[32,2048]{1,0:T(8,128)(2,1)S(1)}, bf16[32,2048]{1,0:T(8,128)(2,1)}, u32[]{:S(2)}) copy-start(bf16[32,2048]{1,0:T(8,128)(2,1)} %refs_0_.3) | copy-start | bytes 393220
  0.6 7.4 %collective-permute-start = (bf16[32,2048]{1,0:T(8,128)(2,1)}, bf16[32,2048]{1,0:T(8,128)(2,1)S(1)}, u32[]{:S(2)}, u32[]{:S(2)}) collective-permute-start(bf16[32,2048]{1,0:T(8,128)(2,1)} %refs_0_.2), channel_id=1, source_target_pairs={{0,1},{1,0},{2,3},{3,2},{4,5},{5,4},{6,7},{7,6},{8,9},{9,8},{10,11... | collective-permute-start | bytes 393224 | tf_op jit(solution)/shard_map/ppermute | solution.py:355
  3.6 8.4 %collective-permute-start.1 = (bf16[32,2048]{1,0:T(8,128)(2,1)}, bf16[32,2048]{1,0:T(8,128)(2,1)S(1)}, u32[]{:S(2)}, u32[]{:S(2)}) collective-permute-start(bf16[32,2048]{1,0:T(8,128)(2,1)} %refs_0_.2), channel_id=1, source_target_pairs={{0,6},{1,7},{2,4},{3,5},{4,2},{5,3},{6,0},{7,1},{8,14},{9,15},{10,... | collective-permute-start | bytes 393224 | tf_op jit(solution)/shard_map/ppermute | solution.py:355
  7.2 7.3 %collective-permute-start.3 = (bf16[32,2048]{1,0:T(8,128)(2,1)}, bf16[32,2048]{1,0:T(8,128)(2,1)S(1)}, u32[]{:S(2)}, u32[]{:S(2)}) collective-permute-start(bf16[32,2048]{1,0:T(8,128)(2,1)} %refs_0_.2), channel_id=1, source_target_pairs={{0,2},{1,3},{2,0},{3,1},{4,6},{5,7},{6,4},{7,5},{8,10},{9,11},{10,... | collective-permute-start | bytes 393224 | tf_op jit(solution)/shard_map/ppermute | solution.py:355
  7.2 11.0 %collective-permute-start.2 = (bf16[32,2048]{1,0:T(8,128)(2,1)}, bf16[32,2048]{1,0:T(8,128)(2,1)S(1)}, u32[]{:S(2)}, u32[]{:S(2)}) collective-permute-start(bf16[32,2048]{1,0:T(8,128)(2,1)} %refs_0_.2), channel_id=1, source_target_pairs={{0,4},{1,5},{2,6},{3,7},{4,0},{5,1},{6,2},{7,3},{8,12},{9,13},{10,... | collective-permute-start | bytes 393224 | tf_op jit(solution)/shard_map/ppermute | solution.py:355
  8.0 0.9 copy-start.1
  24.1 1.9 %collective-permute-start.4 = (bf16[2,64,1792]{2,1,0:T(8,128)(2,1)S(1)}, bf16[2,64,1792]{2,1,0:T(8,128)(2,1)S(1)}, u32[]{:S(2)}, u32[]{:S(2)}) collective-permute-start(bf16[2,64,1792]{2,1,0:T(8,128)(2,1)S(1)} %get-tuple-element.48), channel_id=1, source_target_pairs={{0,8},{8,0},{16,24},{24,16},{1,9},{9,1},{17,25},{25,17},{2,10},{10... | collective-permute-start | bytes 1376264 | tf_op jit(solution)/shard_map/ppermute | solution.py:355
  24.3 16.0 %collective-permute-start.14 = (bf16[96,2048]{1,0:T(8,128)(2,1)S(1)}, bf16[96,2048]{1,0:T(8,128)(2,1)S(1)}, u32[]{:S(2)}, u32[]{:S(2)}) collective-permute-start(bf16[96,2048]{1,0:T(8,128)(2,1)S(1)} %get-tuple-element.60), channel_id=1, source_target_pairs={{0,1},{1,0},{2,3},{3,2},{4,5},{5,4},{6,7},{7,6},{8,9},{9,8},{10,11... | collective-permute-start | bytes 1179656 | tf_op jit(solution)/shard_map/ppermute | solution.py:355
  26.1 20.1 %collective-permute-start.5 = (bf16[2,64,1792]{2,1,0:T(8,128)(2,1)S(1)}, bf16[2,64,1792]{2,1,0:T(8,128)(2,1)S(1)}, u32[]{:S(2)}, u32[]{:S(2)}) collective-permute-start(bf16[2,64,1792]{2,1,0:T(8,128)(2,1)S(1)} %get-tuple-element.49.refs_0_), channel_id=1, source_target_pairs={{0,16},{8,24},{16,0},{24,8},{1,17},{9,25},{17,1},{25,9},{2,18},{10... | collective-permute-start | bytes 1376264 | tf_op jit(solution)/shard_map/ppermute | solution.py:355
  27.7 9.8 %collective-permute-start.11 = (bf16[32,2048]{1,0:T(8,128)(2,1)S(1)}, bf16[32,2048]{1,0:T(8,128)(2,1)S(1)}, u32[]{:S(2)}, u32[]{:S(2)}) collective-permute-start(bf16[32,2048]{1,0:T(8,128)(2,1)S(1)} %copy-done), channel_id=1, source_target_pairs={{0,4},{1,5},{2,6},{3,7},{4,0},{5,1},{6,2},{7,3},{8,12},{9,13},{10,... | collective-permute-start | bytes 393224 | tf_op jit(solution)/shard_map/ppermute | solution.py:355
  28.4 11.2 %collective-permute-start.10 = (bf16[32,2048]{1,0:T(8,128)(2,1)S(1)}, bf16[32,2048]{1,0:T(8,128)(2,1)S(1)}, u32[]{:S(2)}, u32[]{:S(2)}) collective-permute-start(bf16[32,2048]{1,0:T(8,128)(2,1)S(1)} %copy-done), channel_id=1, source_target_pairs={{0,2},{1,3},{2,0},{3,1},{4,6},{5,7},{6,4},{7,5},{8,10},{9,11},{10,... | collective-permute-start | bytes 393224 | tf_op jit(solution)/shard_map/ppermute | solution.py:355
  30.8 8.8 %collective-permute-start.12 = (bf16[32,2048]{1,0:T(8,128)(2,1)S(1)}, bf16[32,2048]{1,0:T(8,128)(2,1)S(1)}, u32[]{:S(2)}, u32[]{:S(2)}) collective-permute-start(bf16[32,2048]{1,0:T(8,128)(2,1)S(1)} %copy-done), channel_id=1, source_target_pairs={{0,6},{1,7},{2,4},{3,5},{4,2},{5,3},{6,0},{7,1},{8,14},{9,15},{10,... | collective-permute-start | bytes 393224 | tf_op jit(solution)/shard_map/ppermute | solution.py:355
  39.7 13.6 %collective-permute-start.13 = (bf16[128,2048]{1,0:T(8,128)(2,1)S(1)}, bf16[128,2048]{1,0:T(8,128)(2,1)S(1)}, u32[]{:S(2)}, u32[]{:S(2)}) collective-permute-start(bf16[128,2048]{1,0:T(8,128)(2,1)S(1)} %get-tuple-element.56.refs_0_), channel_id=1, source_target_pairs={{0,1},{1,0},{2,3},{3,2},{4,5},{5,4},{6,7},{7,6},{8,9},{9,8},{10,11... | collective-permute-start | bytes 1572872 | tf_op jit(solution)/shard_map/ppermute | solution.py:355
  46.2 1.9 %collective-permute-start.15 = (bf16[2,64,1792]{2,1,0:T(8,128)(2,1)S(1)}, bf16[2,64,1792]{2,1,0:T(8,128)(2,1)S(1)}, u32[]{:S(2)}, u32[]{:S(2)}) collective-permute-start(bf16[2,64,1792]{2,1,0:T(8,128)(2,1)S(1)} %get-tuple-element.63), channel_id=1, source_target_pairs={{0,8},{8,0},{16,24},{24,16},{1,9},{9,1},{17,25},{25,17},{2,10},{10... | collective-permute-start | bytes 1376264 | tf_op jit(solution)/shard_map/ppermute | solution.py:355
  46.4 2.3 %collective-permute-start.6 = (bf16[64,1792]{1,0:T(8,128)(2,1)S(1)}, bf16[64,1792]{1,0:T(8,128)(2,1)S(1)}, u32[]{:S(2)}, u32[]{:S(2)}) collective-permute-start(bf16[64,1792]{1,0:T(8,128)(2,1)S(1)} %get-tuple-element.50.mine_ref.refs_1_), channel_id=1, source_target_pairs={{0,8},{8,0},{16,24},{24,16},{1,9},{9,1},{17,25},{25,17},{2,10},{10... | collective-permute-start | bytes 688136 | tf_op jit(solution)/shard_map/ppermute | solution.py:355
  48.1 12.6 %collective-permute-start.16 = (bf16[2,64,1792]{2,1,0:T(8,128)(2,1)S(1)}, bf16[2,64,1792]{2,1,0:T(8,128)(2,1)S(1)}, u32[]{:S(2)}, u32[]{:S(2)}) collective-permute-start(bf16[2,64,1792]{2,1,0:T(8,128)(2,1)S(1)} %get-tuple-element.65.refs_0_.refs_2_), channel_id=1, source_target_pairs={{0,16},{8,24},{16,0},{24,8},{1,17},{9,25},{17,1},{25,9},{2,18},{10... | collective-permute-start | bytes 1376264 | tf_op jit(solution)/shard_map/ppermute | solution.py:355
  58.2 2.8 %collective-permute-start.22 = (bf16[2,64,1792]{2,1,0:T(8,128)(2,1)S(1)}, bf16[2,64,1792]{2,1,0:T(8,128)(2,1)S(1)}, u32[]{:S(2)}, u32[]{:S(2)}) collective-permute-start(bf16[2,64,1792]{2,1,0:T(8,128)(2,1)S(1)} %get-tuple-element.77), channel_id=1, source_target_pairs={{0,8},{8,0},{16,24},{24,16},{1,9},{9,1},{17,25},{25,17},{2,10},{10... | collective-permute-start | bytes 1376264 | tf_op jit(solution)/shard_map/ppermute | solution.py:355
  61.1 17.9 %collective-permute-start.23 = (bf16[2,64,1792]{2,1,0:T(8,128)(2,1)S(1)}, bf16[2,64,1792]{2,1,0:T(8,128)(2,1)S(1)}, u32[]{:S(2)}, u32[]{:S(2)}) collective-permute-start(bf16[2,64,1792]{2,1,0:T(8,128)(2,1)S(1)} %get-tuple-element.79.refs_4_), channel_id=1, source_target_pairs={{0,16},{8,24},{16,0},{24,8},{1,17},{9,25},{17,1},{25,9},{2,18},{10... | collective-permute-start | bytes 1376264 | tf_op jit(solution)/shard_map/ppermute | solution.py:355
  61.7 5.5 %collective-permute-start.17 = (bf16[64,1792]{1,0:T(8,128)(2,1)S(1)}, bf16[64,1792]{1,0:T(8,128)(2,1)S(1)}, u32[]{:S(2)}, u32[]{:S(2)}) collective-permute-start(bf16[64,1792]{1,0:T(8,128)(2,1)S(1)} %get-tuple-element.66.mine_ref.refs_3_), channel_id=1, source_target_pairs={{0,8},{8,0},{16,24},{24,16},{1,9},{9,1},{17,25},{25,17},{2,10},{10... | collective-permute-start | bytes 688136 | tf_op jit(solution)/shard_map/ppermute | solution.py:355
  61.7 17.1 %collective-permute-start.7 = (bf16[32,2048]{1,0:T(8,128)(2,1)S(1)}, bf16[32,2048]{1,0:T(8,128)(2,1)S(1)}, u32[]{:S(2)}, u32[]{:S(2)}) collective-permute-start(bf16[32,2048]{1,0:T(8,128)(2,1)S(1)} %get-tuple-element.52), channel_id=1, source_target_pairs={{0,2},{1,3},{2,0},{3,1},{4,6},{5,7},{6,4},{7,5},{8,10},{9,11},{10,... | collective-permute-start | bytes 393224 | tf_op jit(solution)/shard_map/ppermute | solution.py:355
  64.9 14.0 %collective-permute-start.8 = (bf16[32,2048]{1,0:T(8,128)(2,1)S(1)}, bf16[32,2048]{1,0:T(8,128)(2,1)S(1)}, u32[]{:S(2)}, u32[]{:S(2)}) collective-permute-start(bf16[32,2048]{1,0:T(8,128)(2,1)S(1)} %get-tuple-element.53), channel_id=1, source_target_pairs={{0,4},{1,5},{2,6},{3,7},{4,0},{5,1},{6,2},{7,3},{8,12},{9,13},{10,... | collective-permute-start | bytes 393224 | tf_op jit(solution)/shard_map/ppermute | solution.py:355
  65.2 13.7 %collective-permute-start.9 = (bf16[32,2048]{1,0:T(8,128)(2,1)S(1)}, bf16[32,2048]{1,0:T(8,128)(2,1)S(1)}, u32[]{:S(2)}, u32[]{:S(2)}) collective-permute-start(bf16[32,2048]{1,0:T(8,128)(2,1)S(1)} %get-tuple-element.54), channel_id=1, source_target_pairs={{0,6},{1,7},{2,4},{3,5},{4,2},{5,3},{6,0},{7,1},{8,14},{9,15},{10,... | collective-permute-start | bytes 393224 | tf_op jit(solution)/shard_map/ppermute | solution.py:355
  79.6 7.0 %collective-permute-start.24 = (bf16[2,2,64,1792]{3,2,1,0:T(8,128)(2,1)S(1)}, bf16[2,2,64,1792]{3,2,1,0:T(8,128)(2,1)S(1)}, u32[]{:S(2)}, u32[]{:S(2)}) collective-permute-start(bf16[2,2,64,1792]{3,2,1,0:T(8,128)(2,1)S(1)} %shard_map.126), channel_id=1, source_target_pairs={{0,8},{8,0},{16,24},{24,16},{1,9},{9,1},{17,25},{25,17},{2,10},{10... | collective-permute-start | bytes 2752520 | tf_op jit(solution)/shard_map/ppermute | solution.py:355
  79.7 18.4 %collective-permute-start.18 = (bf16[32,2048]{1,0:T(8,128)(2,1)S(1)}, bf16[32,2048]{1,0:T(8,128)(2,1)S(1)}, u32[]{:S(2)}, u32[]{:S(2)}) collective-permute-start(bf16[32,2048]{1,0:T(8,128)(2,1)S(1)} %get-tuple-element.70), channel_id=1, source_target_pairs={{0,1},{1,0},{2,3},{3,2},{4,5},{5,4},{6,7},{7,6},{8,9},{9,8},{10,11... | collective-permute-start | bytes 393224 | tf_op jit(solution)/shard_map/ppermute | solution.py:355
  81.2 16.8 %collective-permute-start.19 = (bf16[32,2048]{1,0:T(8,128)(2,1)S(1)}, bf16[32,2048]{1,0:T(8,128)(2,1)S(1)}, u32[]{:S(2)}, u32[]{:S(2)}) collective-permute-start(bf16[32,2048]{1,0:T(8,128)(2,1)S(1)} %get-tuple-element.71), channel_id=1, source_target_pairs={{0,3},{1,2},{2,1},{3,0},{4,7},{5,6},{6,5},{7,4},{8,11},{9,10},{10,... | collective-permute-start | bytes 393224 | tf_op jit(solution)/shard_map/ppermute | solution.py:355
  82.8 15.3 %collective-permute-start.20 = (bf16[32,2048]{1,0:T(8,128)(2,1)S(1)}, bf16[32,2048]{1,0:T(8,128)(2,1)S(1)}, u32[]{:S(2)}, u32[]{:S(2)}) collective-permute-start(bf16[32,2048]{1,0:T(8,128)(2,1)S(1)} %get-tuple-element.72), channel_id=1, source_target_pairs={{0,5},{1,4},{2,7},{3,6},{4,1},{5,0},{6,3},{7,2},{8,13},{9,12},{10,... | collective-permute-start | bytes 393224 | tf_op jit(solution)/shard_map/ppermute | solution.py:355
  84.4 13.7 %collective-permute-start.21 = (bf16[32,2048]{1,0:T(8,128)(2,1)S(1)}, bf16[32,2048]{1,0:T(8,128)(2,1)S(1)}, u32[]{:S(2)}, u32[]{:S(2)}) collective-permute-start(bf16[32,2048]{1,0:T(8,128)(2,1)S(1)} %get-tuple-element.73), channel_id=1, source_target_pairs={{0,7},{1,6},{2,5},{3,4},{4,3},{5,2},{6,1},{7,0},{8,15},{9,14},{10,... | collective-permute-start | bytes 393224 | tf_op jit(solution)/shard_map/ppermute | solution.py:355
